TPU v7x, 768 devices: a whole 4x8x12 slice. The times are simulated.
768 devices in a mesh: dp: 48 (over x, z), shuffle: 16 (over y, core).
Axes of the slice: x: 4, y: 8, z: 12, core: 2. Of those that a mesh axis runs over, the one named last changes fastest.
Arguments:
- history_rows: bfloat16 [196608, 512], P(('dp', 'shuffle')), may hold values from -6 to 6
- cotangent: bfloat16 [196608, 512], P(('dp', 'shuffle')), may hold values from -6 to 6
- dest_device: int32 [768, 8], P(('dp', 'shuffle')), may hold values from 0 to 15, as said below
- source_device: int32 [768, 8], P(('dp', 'shuffle')), may hold values from 0 to 15, as said below
- source_offset: int32 [768, 8], P(('dp', 'shuffle')), may hold values from 0 to 1, as said below
- segments: int32 [768, 256], P(('dp', 'shuffle')), may hold values from 0 to 3, as said below
- row_valid: int32 [768, 256], P(('dp', 'shuffle')), may hold values from 0 to 1, as said below
- joined_weight: bfloat16 [512, 2048], replicated, may hold values from -0.25 to 0.25
- output_weight: bfloat16 [512, 512], replicated, may hold values from -0.25 to 0.25
Outputs:
- row_grad: bfloat16 [196608, 512], P(('dp', 'shuffle'))
- joined_grad: float32 [512, 2048], P('shuffle')
- output_grad: float32 [512, 512], P('shuffle')
Inputs may be any that keep to these rules, and one draw needn't show every extreme that they name: `dest_device`: each device sends its 8 blocks to devices of its own dp index, at most 2 to any one device, and in every group some device sends exactly 2 to one device; every device receives exactly 8 blocks. Consistent with dest_device: the pairs (source_device, source_offset) of one device are distinct and name exactly the blocks sent to it. `source_offset`: see source_device. `segments`: in each aligned window of 128 rows the numbers start at 0, never fall and rise by one between histories; each history fills whole blocks. `row_valid`: every block but a history's last is all ones; a history's last block has 1 to 32 leading ones, then zeros.
All inputs are finite; a program needn't handle non-finite values.
Results may differ from a plain program's by a relative error of at most 0.025.
Values may be sent and summed in bfloat16 or wider, within the bound.
No kernel may reach another device: no remote copies, remote signals or barrier semaphores. Data moves between devices by JAX's collectives and lax.ppermute only.
A program may use at most 64 MiB of HBM per device.

v0:
```python
import math

import jax
import jax.numpy as jnp
from jax import lax
from jax.sharding import PartitionSpec as P

HEADS = 8
WIN = 128


epsilon = 1e-05


def row_norm(features):
    centred = features - jnp.mean(features, axis=-1, keepdims=True)
    spread = jnp.mean(centred * centred, axis=-1, keepdims=True)
    return centred * lax.rsqrt(spread + epsilon)


def middle(projected, seg_rows, valid_rows):
    active = jax.nn.silu(projected).astype(jnp.bfloat16)
    total_rows = projected.shape[0]
    feature_count = projected.shape[1] // 4
    head_size = feature_count // HEADS
    windows = total_rows // WIN
    gate_part = active[:, :feature_count]
    value_part = active[:, feature_count : 2 * feature_count]
    query_part = active[:, 2 * feature_count : 3 * feature_count]
    key_part = active[:, 3 * feature_count :]

    def split_heads(block_part):
        return block_part.reshape(windows, WIN, HEADS, head_size)

    scores = jnp.einsum(
        "wqhe,wkhe->whqk",
        split_heads(query_part),
        split_heads(key_part),
        preferred_element_type=jnp.float32,
    ) * head_size ** (-0.5)
    seg_win = seg_rows.reshape(windows, WIN)
    valid_win = valid_rows.reshape(windows, WIN)
    places = jnp.arange(WIN, dtype=jnp.int32)
    allowed = (
        (seg_win[:, :, None] == seg_win[:, None, :])
        & (places[None, None, :] <= places[None, :, None])
        & (valid_win[:, None, :] == 1)
    )
    allowed_float = allowed.astype(jnp.float32)
    counts = jnp.sum(allowed_float, axis=-1)
    weights = allowed_float / jnp.maximum(counts, 1.0)[:, :, None]
    weighting = (jax.nn.silu(scores) * weights[:, None, :, :]).astype(jnp.bfloat16)
    mixture = jnp.einsum(
        "whqk,wkhe->wqhe", weighting, split_heads(value_part), preferred_element_type=jnp.float32
    ).reshape(total_rows, feature_count)
    return row_norm(mixture) * gate_part.astype(jnp.float32)


def forward_pass(features, seg_rows, valid_rows, joined_weight):
    normed_full, norm_back = jax.vjp(row_norm, features.astype(jnp.float32))
    normed = normed_full.astype(jnp.bfloat16)
    projected = jnp.dot(normed, joined_weight, preferred_element_type=jnp.float32)
    gated_full, middle_back = jax.vjp(
        lambda projected_in: middle(projected_in, seg_rows, valid_rows), projected
    )
    return (normed, norm_back, gated_full.astype(jnp.bfloat16), middle_back)


def backward_pass(stored, cot_rows, valid_rows, joined_weight, output_weight):
    normed, norm_back, gated_rows, middle_back = stored
    masked = cot_rows * valid_rows[:, None].astype(jnp.bfloat16)
    gated_cot = jnp.dot(masked, output_weight.T, preferred_element_type=jnp.float32)
    (proj_full,) = middle_back(gated_cot)
    proj_cot = proj_full.astype(jnp.bfloat16)
    normed_cot = jnp.dot(proj_cot, joined_weight.T, preferred_element_type=jnp.float32)
    (rows_cot,) = norm_back(normed_cot)
    work_grad = (masked.astype(jnp.float32) + rows_cot).astype(jnp.bfloat16)
    joined_part = jnp.dot(normed.T, proj_cot, preferred_element_type=jnp.float32)
    output_part = jnp.dot(gated_rows.T, masked, preferred_element_type=jnp.float32)
    return (work_grad, joined_part, output_part)


def on_device(
    history_rows,
    cotangent,
    dest_device,
    source_device,
    source_offset,
    segments,
    row_valid,
    joined_weight,
    output_weight,
):
    peer_count = lax.axis_size("shuffle")
    block_count = dest_device.shape[1]
    local_rows, feature_count = history_rows.shape
    block_rows = local_rows // block_count
    capacity = max(2, -(-block_count // peer_count))
    slot_index = jnp.arange(block_count, dtype=jnp.int32)
    buffer_index = jnp.arange(peer_count * capacity, dtype=jnp.int32)
    targets = dest_device[0]
    same_target = targets[:, None] == targets[None, :]
    rank_of_slot = jnp.sum(
        (same_target & (slot_index[None, :] < slot_index[:, None])).astype(jnp.int32),
        axis=1,
        dtype=jnp.int32,
    )
    send_table = ((targets * capacity + rank_of_slot)[None, :] == buffer_index[:, None]).astype(
        jnp.bfloat16
    )
    recv_table = (
        (source_device[0] * capacity + source_offset[0])[:, None] == buffer_index[None, :]
    ).astype(jnp.bfloat16)
    seg_rows = segments[0]
    valid_rows = row_valid[0]

    def regroup(zero_one, row_block):
        flattened = row_block.reshape(zero_one.shape[1], block_rows * feature_count)
        return jnp.dot(zero_one, flattened, preferred_element_type=jnp.float32).astype(jnp.bfloat16)

    def outgoing(row_block):
        return regroup(send_table, row_block).reshape(
            peer_count, capacity * block_rows * feature_count
        )

    def incoming(buffer):
        return regroup(recv_table, buffer).reshape(block_count * block_rows, feature_count)

    arrived_rows, arrived_cot = (
        lax.all_to_all(outgoing(history_rows), "shuffle", split_axis=0, concat_axis=0, tiled=True),
        lax.all_to_all(outgoing(cotangent), "shuffle", split_axis=0, concat_axis=0, tiled=True),
    )
    work_rows = incoming(arrived_rows)
    work_cot = incoming(arrived_cot)
    stored = forward_pass(work_rows, seg_rows, valid_rows, joined_weight)
    work_grad, joined_part, output_part = backward_pass(
        stored, work_cot, valid_rows, joined_weight, output_weight
    )
    scaling = 1.0 / math.sqrt(local_rows * peer_count * lax.axis_size("dp"))
    leaving = regroup(recv_table.T, work_grad).reshape(
        peer_count, capacity * block_rows * feature_count
    )
    arrived = lax.all_to_all(leaving, "shuffle", split_axis=0, concat_axis=0, tiled=True)
    row_grad = regroup(send_table.T, arrived).reshape(local_rows, feature_count)
    totals = lax.psum(
        (
            lax.psum_scatter(
                joined_part.astype(jnp.bfloat16), "shuffle", scatter_dimension=0, tiled=True
            ).astype(jnp.float32),
            lax.psum_scatter(
                output_part.astype(jnp.bfloat16), "shuffle", scatter_dimension=0, tiled=True
            ).astype(jnp.float32),
        ),
        "dp",
    )
    joined_grad = totals[0] * scaling
    output_grad = totals[1] * scaling
    return (row_grad, joined_grad, output_grad)


def solution(mesh):
    return jax.shard_map(
        on_device,
        mesh=mesh,
        in_specs=(
            P(("dp", "shuffle"), None),
            P(("dp", "shuffle"), None),
            P(("dp", "shuffle"), None),
            P(("dp", "shuffle"), None),
            P(("dp", "shuffle"), None),
            P(("dp", "shuffle"), None),
            P(("dp", "shuffle"), None),
            P(),
            P(),
        ),
        out_specs=(P(("dp", "shuffle"), None), P("shuffle", None), P("shuffle", None)),
        check_vma=False,
    )
```

profile of v0, /device:TPU:32, one launch (start us, length us, event | category | flops | bytes accessed | tf_op | source)
XLA Modules:
  0.0 511.8 jit_solution(11526679600064186718)
XLA Ops:
  9.9 1.4 convolution_convert_fusion.1
  11.3 4.3 all_to_all.25
  16.2 9.3 %reduce.9 = bf16[16,32768]{1,0:T(8,128)(2,1)} reduce(bf16[16,1,32768]{2,1,0:T(2,128)(2,1)} %all_to_all.25, bf16[]{:T(256)} %broadcast.193), dimensions={1}, to_apply=%all_to_all.25.reduce_sub_computation | reduce | bytes 2097154 | tf_op jit(solution)/shard_map/all_to_all | solution.py:130
  25.5 2.7 reshape.225
  28.2 13.6 %all-to-all-start.1 = ((bf16[16,2,16384]{2,1,0:T(2,128)(2,1)}), bf16[16,2,16384]{2,1,0:T(2,128)(2,1)}, u32[]{:S(2)}, u32[]{:S(2)}) async-start(bf16[16,2,16384]{2,1,0:T(2,128)(2,1)} %reshape.225), calls=%async_computation.1 | async-start | bytes 2097152 | tf_op jit(solution)/shard_map/all_to_all | solution.py:130
  41.9 1.4 convolution_convert_fusion.2
  43.3 4.3 all_to_all.24
  47.6 9.4 %reduce.10 = bf16[16,32768]{1,0:T(8,128)(2,1)} reduce(bf16[16,1,32768]{2,1,0:T(2,128)(2,1)} %all_to_all.24, bf16[]{:T(256)} %broadcast.193), dimensions={1}, to_apply=%all_to_all.24.reduce_sub_computation | reduce | bytes 2097154 | tf_op jit(solution)/shard_map/all_to_all | solution.py:131
  57.0 2.7 reshape.227
  59.7 6.2 %all-to-all-done.1 = bf16[16,2,16384]{2,1,0:T(2,128)(2,1)} async-done(((bf16[16,2,16384]{2,1,0:T(2,128)(2,1)}), bf16[16,2,16384]{2,1,0:T(2,128)(2,1)}, u32[]{:S(2)}, u32[]{:S(2)}) %all-to-all-start.1) | async-done | bytes 1048608 | tf_op jit(solution)/shard_map/all_to_all | solution.py:130
  65.9 7.3 %all-to-all-start = ((bf16[16,2,16384]{2,1,0:T(2,128)(2,1)}), bf16[16,2,16384]{2,1,0:T(2,128)(2,1)}, u32[]{:S(2)}, u32[]{:S(2)}) async-start(bf16[16,2,16384]{2,1,0:T(2,128)(2,1)} %reshape.227), calls=%async_computation | async-start | bytes 2097152 | tf_op jit(solution)/shard_map/all_to_all | solution.py:131
  74.4 5.8 %reshape.226 = bf16[16,1,32768]{2,1,0:T(2,128)(2,1)} reshape(bf16[16,2,16384]{2,1,0:T(2,128)(2,1)} %all-to-all-done.1) | data formatting | bytes 2097152
  80.2 8.7 %reduce.4 = bf16[16,32768]{1,0:T(8,128)(2,1)} reduce(bf16[16,1,32768]{2,1,0:T(2,128)(2,1)} %reshape.226, bf16[]{:T(256)} %constant.50), dimensions={1}, to_apply=%all_to_all.21.reduce_sub_computation | reduce | bytes 2097154 | tf_op jit(solution)/shard_map/all_to_all | solution.py:130
  88.9 2.3 reshape.200
  91.2 1.5 fusion
  93.2 4.3 all-to-all-done
  97.5 6.0 %reshape.228 = bf16[16,1,32768]{2,1,0:T(2,128)(2,1)} reshape(bf16[16,2,16384]{2,1,0:T(2,128)(2,1)} %all-to-all-done) | data formatting | bytes 2097152
  103.5 8.7 %reduce.2 = bf16[16,32768]{1,0:T(8,128)(2,1)} reduce(bf16[16,1,32768]{2,1,0:T(2,128)(2,1)} %reshape.228, bf16[]{:T(256)} %constant.50), dimensions={1}, to_apply=%all_to_all.19.reduce_sub_computation | reduce | bytes 2097154 | tf_op jit(solution)/shard_map/all_to_all | solution.py:131
  112.2 2.7 reshape.197
  115.0 1.5 convolution_convert_fusion.5
  116.7 2.1 multiply_convert_fusion
  120.7 1.3 reshape.219
  123.0 1.3 reshape.218
  125.3 1.3 reshape.217
  127.6 2.6 multiply_convert_fusion.1
  132.0 1.3 copy.112
  133.3 1.3 multiply_reduce_fusion.2
  134.7 1.5 reshape.213
  136.2 2.3 multiply_reduce_fusion.1
  139.6 2.2 convolution_convert_fusion.8
  141.8 2.1 fusion.36
  144.3 2.0 fusion.11
  153.1 2.1 fusion.6
  157.5 2.7 fusion.2
  161.2 2.2 convolution_convert_fusion.6
  163.4 2.1 multiply_reduce_fusion
  166.1 1.5 convolution_convert_fusion
  167.6 4.5 all_to_all.26
  172.1 9.3 %reduce.11 = bf16[16,32768]{1,0:T(8,128)(2,1)} reduce(bf16[16,1,32768]{2,1,0:T(2,128)(2,1)} %all_to_all.26, bf16[]{:T(256)} %broadcast.193), dimensions={1}, to_apply=%all_to_all.26.reduce_sub_computation | reduce | bytes 2097154 | tf_op jit(solution)/shard_map/all_to_all | solution.py:143
  181.4 2.6 reshape.229
  184.1 7.6 %all-to-all-start.2 = ((bf16[16,2,16384]{2,1,0:T(2,128)(2,1)}), bf16[16,2,16384]{2,1,0:T(2,128)(2,1)}, u32[]{:S(2)}, u32[]{:S(2)}) async-start(bf16[16,2,16384]{2,1,0:T(2,128)(2,1)} %reshape.229), calls=%async_computation.2 | async-start | bytes 2097152 | tf_op jit(solution)/shard_map/all_to_all | solution.py:143
  191.7 26.6 %reduce-scatter.5.cloned.1.call-done = bf16[32,512]{1,0:T(8,128)(2,1)} async-done(((bf16[512,512]{1,0:T(8,128)(2,1)}), bf16[32,512]{1,0:T(8,128)(2,1)}) %reduce-scatter.5.cloned.1.call-update) | async-done | bytes 32784 | tf_op jit(solution)/shard_map/reduce_scatter | solution.py:150
  218.3 5.8 %reshape.230 = bf16[16,1,32768]{2,1,0:T(2,128)(2,1)} reshape(bf16[16,2,16384]{2,1,0:T(2,128)(2,1)} %all-to-all-done.2) | data formatting | bytes 2097152
  224.1 8.7 %reduce.6 = bf16[16,32768]{1,0:T(8,128)(2,1)} reduce(bf16[16,1,32768]{2,1,0:T(2,128)(2,1)} %reshape.230, bf16[]{:T(256)} %constant.50), dimensions={1}, to_apply=%all_to_all.23.reduce_sub_computation | reduce | bytes 2097154 | tf_op jit(solution)/shard_map/all_to_all | solution.py:143
  232.8 2.3 reshape.210
  235.1 1.5 convolution_convert_fusion.3
  237.4 50.6 %reduce-scatter.3.cloned.1.call-done = bf16[32,2048]{1,0:T(8,128)(2,1)} async-done(((bf16[512,2048]{1,0:T(8,128)(2,1)}), bf16[32,2048]{1,0:T(8,128)(2,1)}) %reduce-scatter.3.cloned.1.call-update) | async-done | bytes 131088 | tf_op jit(solution)/shard_map/reduce_scatter | solution.py:147
  288.0 215.3 %all-reduce.6 = (f32[32,2048]{1,0:T(8,128)S(1)}, f32[32,512]{1,0:T(8,128)S(1)}) all-reduce(bf16[32,2048]{1,0:T(8,128)(2,1)} %reduce-scatter.3.cloned.1.call-done, bf16[32,512]{1,0:T(8,128)(2,1)S(1)} %copy-done.9), channel_id=1, replica_groups=mesh['dp'=48,'shuffle'=16] {'dp'}, use_global_device_ids=true, to_apply=%region_11.12 | all-reduce | flops 81920 | bytes 491520 | tf_op jit(solution)/shard_map/psum | solution.py:145
  (92 shorter events, 26.3 us)
Async XLA Ops:
  7.2 109.5 %copy-start = (bf16[512,2048]{1,0:T(8,128)(2,1)S(1)}, bf16[512,2048]{1,0:T(8,128)(2,1)}, u32[]{:S(2)}) copy-start(bf16[512,2048]{1,0:T(8,128)(2,1)} %param.16) | copy-start | bytes 6291460
  8.8 33.1 %copy-start.12 = (s32[8]{0:T(128)}, s32[8]{0:T(128)S(1)}, u32[]{:S(2)}) copy-start(s32[8]{0:T(128)S(1)} %fusion.32) | copy-start | bytes 100
  25.5 16.3 %copy-start.8 = (bf16[256,512]{1,0:T(8,128)(2,1)S(1)}, bf16[256,512]{1,0:T(8,128)(2,1)}, u32[]{:S(2)}) copy-start(bf16[256,512]{1,0:T(8,128)(2,1)} %param.10) | copy-start | bytes 786436
  28.2 37.7 %all-to-all-start.1 = ((bf16[16,2,16384]{2,1,0:T(2,128)(2,1)}), bf16[16,2,16384]{2,1,0:T(2,128)(2,1)}, u32[]{:S(2)}, u32[]{:S(2)}) async-start(bf16[16,2,16384]{2,1,0:T(2,128)(2,1)} %reshape.225), calls=%async_computation.1 | async-start | bytes 2097152 | tf_op jit(solution)/shard_map/all_to_all | solution.py:130
  57.0 16.4 %copy-start.18 = (s32[1,256]{1,0:T(1,128)S(1)}, s32[1,256]{1,0:T(1,128)}, u32[]{:S(2)}) copy-start(s32[1,256]{1,0:T(1,128)} %param.15) | copy-start | bytes 3076
  57.0 17.0 %copy-start.10 = (s32[1,256]{1,0:T(1,128)S(1)}, s32[1,256]{1,0:T(1,128)}, u32[]{:S(2)}) copy-start(s32[1,256]{1,0:T(1,128)} %param.14) | copy-start | bytes 3076
  57.0 17.2 %copy-start.19 = (s32[1,8]{1,0:T(1,128)S(1)}, s32[1,8]{1,0:T(1,128)}, u32[]{:S(2)}) copy-start(s32[1,8]{1,0:T(1,128)} %param.13) | copy-start | bytes 100
  57.0 17.2 %copy-start.20 = (s32[1,8]{1,0:T(1,128)S(1)}, s32[1,8]{1,0:T(1,128)}, u32[]{:S(2)}) copy-start(s32[1,8]{1,0:T(1,128)} %param.12) | copy-start | bytes 100
  65.9 31.6 %all-to-all-start = ((bf16[16,2,16384]{2,1,0:T(2,128)(2,1)}), bf16[16,2,16384]{2,1,0:T(2,128)(2,1)}, u32[]{:S(2)}, u32[]{:S(2)}) async-start(bf16[16,2,16384]{2,1,0:T(2,128)(2,1)} %reshape.227), calls=%async_computation | async-start | bytes 2097152 | tf_op jit(solution)/shard_map/all_to_all | solution.py:131
  73.2 145.1 %reduce-scatter.5.cloned.1.call-start = ((), (), s32[]{:S(2)}) async-start(), calls=%async_computation.6 | async-start | bytes 557056 | tf_op jit(solution)/shard_map/reduce_scatter | solution.py:150
  74.2 40.7 %copy-start.14 = (s32[8]{0:T(128)}, s32[8]{0:T(128)S(1)}, u32[]{:S(2)}) copy-start(s32[8]{0:T(128)S(1)} %add_bitcast_fusion) | copy-start | bytes 100
  118.8 1.0 copy-start.2
  127.6 3.4 copy-start.6
  130.2 0.8 copy-start.3
  136.2 2.3 copy-start.17
  139.1 0.5 copy-start.11
  144.2 2.1 copy-start.7
  144.2 2.1 copy-start.4
  144.2 3.3 copy-start.5
  148.5 139.5 %reduce-scatter.3.cloned.1.call-start = ((), (), s32[]{:S(2)}) async-start(), calls=%async_computation.5 | async-start | bytes 2228224 | tf_op jit(solution)/shard_map/reduce_scatter | solution.py:147
  160.2 1.0 copy-start.1
  163.4 2.4 copy-start.16
  165.5 0.6 copy-start.15
  184.1 34.2 %all-to-all-start.2 = ((bf16[16,2,16384]{2,1,0:T(2,128)(2,1)}), bf16[16,2,16384]{2,1,0:T(2,128)(2,1)}, u32[]{:S(2)}, u32[]{:S(2)}) async-start(bf16[16,2,16384]{2,1,0:T(2,128)(2,1)} %reshape.229), calls=%async_computation.2 | async-start | bytes 2097152 | tf_op jit(solution)/shard_map/all_to_all | solution.py:143
  224.1 11.0 %copy-start.13 = (s32[8]{0:T(128)S(1)}, s32[8]{0:T(128)}, u32[]{:S(2)}) copy-start(s32[8]{0:T(128)} %copy-done.12) | copy-start | bytes 100
  232.8 55.2 %copy-start.9 = (bf16[32,512]{1,0:T(8,128)(2,1)S(1)}, bf16[32,512]{1,0:T(8,128)(2,1)}, u32[]{:S(2)}) copy-start(bf16[32,512]{1,0:T(8,128)(2,1)} %reduce-scatter.5.cloned.1.call-done) | copy-start | bytes 98308
Sparse Core Ops, SparseCore 0:
  148.6 69.5 reduce-scatter.4
  221.7 66.2 reduce-scatter.2
where the time goes:
time: 520 us; the launch traced here: 512 us
  blocking collectives  215 us (41%)
  waiting for transfers between devices  87.8 us (17%)
  local copies, waits for them, and re-layouts  70 us (13%)
  other arithmetic  66.2 us (13%)
  matrix products  29.2 us (6%)
  starting transfers between devices  28.7 us (6%)
  between operations  14.7 us (3%)
    psum x1, blocking collectives, on_device(): lax.psum((lax.psum_scatter(joined_part.astype(jnp.bfloat16), 'shuffle', s...  215 us
    reduce_scatter x1, waiting for transfers between devices, on_device(): lax.psum_scatter(joined_part.astype(jnp.bfloat16), 'shuffle', scatter_dim...  50.6 us
    unnamed x48, local copies, waits for them, and re-layouts  29 us
    reduce_scatter x1, waiting for transfers between devices, on_device(): lax.psum_scatter(output_part.astype(jnp.bfloat16), 'shuffle', scatter_dim...  26.6 us
    all_to_all x2, other arithmetic, on_device(): lax.all_to_all(outgoing(cotangent), 'shuffle', split_axis=0, concat_axis=...  18.1 us
    all_to_all x2, other arithmetic, on_device(): lax.all_to_all(outgoing(history_rows), 'shuffle', split_axis=0, concat_ax...  18 us
    all_to_all x2, other arithmetic, on_device(): lax.all_to_all(leaving, 'shuffle', split_axis=0, concat_axis=0, tiled=True)  18 us
    reshape x12, local copies, waits for them, and re-layouts, split_heads(): return block_part.reshape(windows, WIN, HEADS, head_size)  13.7 us
  transfers between devices with their start and end apart: 5, of which 4 were waited for; matrix products, arithmetic and copies ran while one was open for 16% of the time, Pallas kernels for 0%

commit v1 on v0

v1 whole, which is shorter than its diff:
```python
import functools
import math

import jax
import jax.numpy as jnp
from jax import lax
from jax.experimental import pallas as pl
from jax.experimental.pallas import tpu as pltpu
from jax.sharding import Mesh, PartitionSpec as P

HEADS = 8
WIN = 128
epsilon = 1e-05
f32 = jnp.float32
bf16 = jnp.bfloat16
VMEM_LIMIT = 48 * 1024 * 1024
NT = (((1,), (1,)), ((), ()))
TN = (((0,), (0,)), ((), ()))


def dot(a, b, dims=(((1,), (0,)), ((), ()))):
    return lax.dot_general(a, b, dims, preferred_element_type=f32)


def row_norm(features):
    centred = features - jnp.mean(features, axis=-1, keepdims=True)
    spread = jnp.mean(centred * centred, axis=-1, keepdims=True)
    inverse = lax.rsqrt(spread + epsilon)
    return centred * inverse, inverse


def row_norm_back(cot, normed, inverse):
    mean_cot = jnp.mean(cot, axis=-1, keepdims=True)
    mean_both = jnp.mean(cot * normed, axis=-1, keepdims=True)
    return inverse * (cot - mean_cot - normed * mean_both)


def as_column(row, diagonal):
    return jnp.sum(jnp.where(diagonal, row, 0.0), axis=1, keepdims=True)


def forward_body(
    rows_ref,
    seg_ref,
    valid_ref,
    weight_ref,
    normed_ref,
    inverse_ref,
    active_ref,
    slope_ref,
    weighting_ref,
    score_slope_ref,
    mixed_ref,
    mix_inverse_ref,
    gated_ref,
):
    rows, width = rows_ref.shape
    head = width // HEADS
    pair = 2 * head
    normed, inverse = row_norm(rows_ref[...].astype(f32))
    normed = normed.astype(bf16)
    normed_ref[...] = normed
    inverse_ref[...] = inverse
    for quarter in range(4):
        columns = slice(quarter * width, (quarter + 1) * width)
        projected = dot(normed, weight_ref[:, columns])
        gate = jax.nn.sigmoid(projected)
        active_ref[:, columns] = (projected * gate).astype(bf16)
        slope_ref[:, columns] = (gate * (1.0 + projected * (1.0 - gate))).astype(bf16)
    left = lax.broadcasted_iota(jnp.int32, (WIN, pair), 1) < head
    place_i = lax.broadcasted_iota(jnp.int32, (WIN, WIN), 0)
    place_j = lax.broadcasted_iota(jnp.int32, (WIN, WIN), 1)
    zero = jnp.zeros((), bf16)

    def stacked(block):
        return jnp.concatenate([jnp.where(left, block, zero), jnp.where(left, zero, block)], axis=0)

    for window in range(rows // WIN):
        span = slice(window * WIN, (window + 1) * WIN)
        seg_row = seg_ref[:, span].astype(f32)
        seg_col = as_column(seg_row, place_i == place_j)
        allowed = (seg_col == seg_row) & (place_j <= place_i) & (valid_ref[:, span] == 1)
        allowed = jnp.where(allowed, 1.0, 0.0)
        weights = allowed / jnp.maximum(jnp.sum(allowed, axis=1, keepdims=True), 1.0)
        weights = jnp.concatenate([weights, weights], axis=1)
        mixture = []
        for p in range(HEADS // 2):
            at = p * pair
            value = active_ref[span, width + at : width + at + pair]
            query = active_ref[span, 2 * width + at : 2 * width + at + pair]
            key = active_ref[span, 3 * width + at : 3 * width + at + pair]
            scores = dot(query, stacked(key), NT) * head**-0.5
            gate = jax.nn.sigmoid(scores)
            weighting = (scores * gate * weights).astype(bf16)
            slot = window * (HEADS // 2) + p
            weighting_ref[slot] = weighting
            score_slope_ref[slot] = (
                gate * (1.0 + scores * (1.0 - gate)) * (weights * head**-0.5)
            ).astype(bf16)
            mixture.append(dot(weighting, stacked(value)))
        mixed, mix_inverse = row_norm(jnp.concatenate(mixture, axis=1))
        mixed_ref[span, :] = mixed
        mix_inverse_ref[span, :] = mix_inverse
        gated_ref[span, :] = (mixed * active_ref[span, :width].astype(f32)).astype(bf16)


def backward_body(
    rows_ref,
    cot_ref,
    valid_ref,
    weight_ref,
    out_weight_ref,
    normed_ref,
    inverse_ref,
    active_ref,
    slope_ref,
    weighting_ref,
    score_slope_ref,
    mixed_ref,
    mix_inverse_ref,
    gated_ref,
    proj_cot_ref,
    spread,
    keep_ref,
    send_ref,
):
    rows, width = rows_ref.shape
    head = width // HEADS
    pair = 2 * head
    place_i = lax.broadcasted_iota(jnp.int32, (rows, rows), 0)
    place_j = lax.broadcasted_iota(jnp.int32, (rows, rows), 1)
    valid_col = as_column(valid_ref[...].astype(f32), place_i == place_j)
    masked_f = cot_ref[...].astype(f32) * valid_col
    masked = masked_f.astype(bf16)
    side = width // 2

    def put_grad(factor, cot, at):
        grad = dot(factor, cot).astype(bf16)
        keep_ref[:, at : at + width] = grad[:side]
        send_ref[:, at : at + width] = grad[side:]

    put_grad(permute(spread, gated_ref[...], NT), masked, 4 * width)
    gated_cot = dot(masked, out_weight_ref[...], NT)
    mixed = mixed_ref[...]
    gate_cot = (gated_cot * mixed).astype(bf16).astype(f32)
    proj_cot_ref[:, :width] = (gate_cot * slope_ref[:, :width].astype(f32)).astype(bf16)
    mixture_cot = row_norm_back(
        gated_cot * active_ref[:, :width].astype(f32), mixed, mix_inverse_ref[...]
    ).astype(bf16)
    left = lax.broadcasted_iota(jnp.int32, (WIN, pair), 1) < head
    zero = jnp.zeros((), bf16)

    def stacked(block):
        return jnp.concatenate([jnp.where(left, block, zero), jnp.where(left, zero, block)], axis=0)

    def folded(block):
        return jnp.where(left, block[:WIN], block[WIN:])

    for window in range(rows // WIN):
        span = slice(window * WIN, (window + 1) * WIN)
        for p in range(HEADS // 2):
            at = p * pair
            slot = window * (HEADS // 2) + p

            def put(quarter, cot):
                columns = slice(quarter * width + at, quarter * width + at + pair)
                slope = slope_ref[span, columns].astype(f32)
                proj_cot_ref[span, columns] = (cot.astype(bf16).astype(f32) * slope).astype(bf16)

            value = active_ref[span, width + at : width + at + pair]
            query = active_ref[span, 2 * width + at : 2 * width + at + pair]
            key = active_ref[span, 3 * width + at : 3 * width + at + pair]
            mix_cot = mixture_cot[span, at : at + pair]
            put(1, folded(dot(weighting_ref[slot], mix_cot, TN)))
            weighting_cot = dot(mix_cot, stacked(value), NT).astype(bf16).astype(f32)
            score_cot = (weighting_cot * score_slope_ref[slot].astype(f32)).astype(bf16)
            put(2, dot(score_cot, stacked(key)))
            put(3, folded(dot(score_cot, query, TN)))
    normed_t = permute(spread, normed_ref[...], NT)
    normed_cot = jnp.zeros((rows, width), f32)
    for quarter in range(4):
        columns = slice(quarter * width, (quarter + 1) * width)
        proj_cot = proj_cot_ref[:, columns]
        put_grad(normed_t, proj_cot, quarter * width)
        normed_cot += dot(proj_cot, weight_ref[:, columns], NT)
    features = rows_ref[...].astype(f32)
    inverse = inverse_ref[...]
    normed_f = (features - jnp.mean(features, axis=-1, keepdims=True)) * inverse
    rows_cot = row_norm_back(normed_cot, normed_f, inverse)
    return (masked_f + rows_cot).astype(bf16)


def permute(order, block, dims=(((1,), (0,)), ((), ()))):
    return dot(order, block, dims).astype(bf16)


def pack_kernel(lanes, dest_ref, rows_ref, cot_ref, out_ref):
    rows, width = rows_ref.shape
    blocks = dest_ref.shape[1]
    chunk = rows // lanes
    half = chunk // blocks
    place = lax.broadcasted_iota(jnp.int32, (rows, rows), 0)
    loaded = lax.broadcasted_iota(jnp.int32, (rows, rows), 1)
    source = place % blocks * (rows // blocks) + place // blocks % half * lanes + place // chunk
    order = jnp.where(source == loaded, 1.0, 0.0).astype(bf16)
    out_ref[:, :width] = permute(order, rows_ref[...])
    out_ref[:, width : 2 * width] = permute(order, cot_ref[...])
    extra = out_ref.shape[1] - 2 * width
    block = lax.broadcasted_iota(jnp.int32, (rows, extra), 0) % blocks
    dest = jnp.zeros((rows, extra), f32)
    for j in range(blocks):
        dest = jnp.where(block == j, dest_ref[0, j].astype(f32), dest)
    out_ref[:, 2 * width :] = dest.astype(bf16)


def route_kernel(lanes, in_ref, out_ref, order_ref):
    rows, double = out_ref.shape
    chunk = rows // lanes
    blocks = chunk // 2
    extra = in_ref.shape[1] - double
    place = lax.broadcasted_iota(jnp.int32, (rows, rows), 0)
    other = lax.broadcasted_iota(jnp.int32, (rows, rows), 1)
    lane = lax.broadcasted_iota(jnp.int32, (rows, extra), 1)
    dest = in_ref[:, double:].astype(f32)
    chosen = jnp.where(dest == lane.astype(f32), 1.0, 0.0)
    same_half = place // blocks % 2 == other // blocks % 2
    earlier = jnp.where(same_half & (other < place), 1.0, 0.0).astype(bf16)
    rank = jnp.sum(dot(earlier, chosen.astype(bf16)) * chosen, axis=1, keepdims=True)
    row = lax.broadcasted_iota(jnp.int32, (rows, 1), 0)
    target = dest[:, :1] * chunk + (row // blocks % 2 * blocks).astype(f32) + rank
    order = jnp.where(target == other.astype(f32), 1.0, 0.0).astype(bf16)
    order_ref[...] = order
    out_ref[...] = permute(order, in_ref[:, :double], TN)


def gather_order(lanes, sources_ref, offsets_ref, order_ref):
    rows = order_ref.shape[0]
    blocks = sources_ref.shape[1]
    chunk = rows // lanes
    half = chunk // blocks
    span = rows // blocks
    inside = lax.broadcasted_iota(jnp.int32, (span, rows), 0)
    column = lax.broadcasted_iota(jnp.int32, (span, rows), 1)
    base = inside % lanes * chunk + inside // lanes % half * blocks
    keys = [sources_ref[0, t] * 2 + offsets_ref[0, t] for t in range(blocks)]
    for t in range(blocks):
        slot = sum(jnp.where(keys[u] < keys[t], 1, 0) for u in range(blocks) if u != t)
        order = jnp.where(column == base + slot, 1.0, 0.0)
        order_ref[t * span : (t + 1) * span, :] = order.astype(bf16)


def spread_order(parts, core, width):
    xs, ys = parts
    out = lax.broadcasted_iota(jnp.int32, (width, width), 0)
    column = lax.broadcasted_iota(jnp.int32, (width, width), 1)
    side = width // 2
    block = width // ys // 2
    piece = block // xs
    y = out // piece % ys
    x = out % side // (piece * ys)
    parity = (out // side + core) % 2
    source = y * (2 * block) + parity * block + x * piece + out % piece
    return jnp.where(source == column, 1.0, 0.0).astype(bf16)


def layer_kernel(
    lanes,
    parts,
    core_ref,
    sources_ref,
    offsets_ref,
    in_ref,
    seg_ref,
    valid_ref,
    weight_ref,
    out_weight_ref,
    leave_ref,
    keep_ref,
    send_ref,
    order_ref,
    rows_ref,
    cot_ref,
    normed_ref,
    inverse_ref,
    active_ref,
    slope_ref,
    weighting_ref,
    score_slope_ref,
    mixed_ref,
    mix_inverse_ref,
    gated_ref,
    proj_cot_ref,
):
    rows, width = rows_ref.shape
    gather_order(lanes, sources_ref, offsets_ref, order_ref)
    rows_ref[...] = permute(order_ref[...], in_ref[:, :width])
    cot_ref[...] = permute(order_ref[...], in_ref[:, width:])
    stored = (
        normed_ref,
        inverse_ref,
        active_ref,
        slope_ref,
        weighting_ref,
        score_slope_ref,
        mixed_ref,
        mix_inverse_ref,
        gated_ref,
    )
    forward_body(rows_ref, seg_ref, valid_ref, weight_ref, *stored)
    spread = spread_order(parts, core_ref[0], width)
    work_grad = backward_body(
        rows_ref,
        cot_ref,
        valid_ref,
        weight_ref,
        out_weight_ref,
        *stored,
        proj_cot_ref,
        spread,
        keep_ref,
        send_ref,
    )
    leave_ref[...] = permute(order_ref[...], work_grad, TN)


def return_kernel(order_ref, in_ref, out_ref):
    out_ref[...] = permute(order_ref[...], in_ref[...])


def unpack_kernel(lanes, blocks, in_ref, out_ref):
    rows = in_ref.shape[0]
    chunk = rows // lanes
    half = chunk // blocks
    loaded = lax.broadcasted_iota(jnp.int32, (rows, rows), 0)
    place = lax.broadcasted_iota(jnp.int32, (rows, rows), 1)
    source = place % blocks * (rows // blocks) + place // blocks % half * lanes + place // chunk
    order = jnp.where(source == loaded, 1.0, 0.0).astype(bf16)
    out_ref[...] = permute(order, in_ref[...])


def split_kernel(in_ref, out_ref):
    pieces, piece = out_ref.shape[1], out_ref.shape[3]
    for k in range(pieces):
        if (k + 1) * piece <= in_ref.shape[2]:
            out_ref[:, k] = in_ref[:, :, k * piece : (k + 1) * piece]
        else:
            out_ref[:, k] = jnp.zeros(out_ref.shape[:1] + out_ref.shape[2:], bf16)


def total_kernel(scaling, in_ref, out_ref):
    total = jnp.sum(in_ref[...].astype(f32), axis=0, keepdims=True) * scaling
    out_ref[...] = jnp.broadcast_to(total.astype(bf16), out_ref.shape)


def result_kernel(in_ref, joined_ref, output_ref):
    xs, zs, piece_rows, piece = in_ref.shape
    split = joined_ref.shape[1]
    step = math.gcd(piece, split)
    for x in range(xs):
        span = slice(x * piece_rows, (x + 1) * piece_rows)
        for at in range(0, split + output_ref.shape[1], step):
            block = in_ref[x, at // piece, :, at % piece : at % piece + step].astype(f32)
            if at < split:
                joined_ref[span, at : at + step] = block
            else:
                output_ref[span, at - split : at - split + step] = block


def call(kernel, name, out_shape, operands, flops=0, scalars=0, scratch=()):
    moved = sum(math.prod(a.shape) * a.dtype.itemsize for a in (*operands, *out_shape))
    smem = pl.BlockSpec(memory_space=pltpu.SMEM)
    vmem = pl.BlockSpec(memory_space=pltpu.VMEM)
    return pl.pallas_call(
        kernel,
        out_shape=tuple(out_shape),
        in_specs=[smem] * scalars + [vmem] * (len(operands) - scalars),
        out_specs=tuple(vmem for _ in out_shape),
        scratch_shapes=list(scratch),
        compiler_params=pltpu.CompilerParams(vmem_limit_bytes=VMEM_LIMIT),
        cost_estimate=pl.CostEstimate(flops=flops, bytes_accessed=moved, transcendentals=0),
        name=name,
    )(*operands)


def on_device(
    history_rows,
    cotangent,
    dest_device,
    source_device,
    source_offset,
    segments,
    row_valid,
    joined_weight,
    output_weight,
):
    shape = jax.ShapeDtypeStruct
    xs, zs, ys = lax.axis_size("x"), lax.axis_size("z"), lax.axis_size("y")
    lanes = ys * lax.axis_size("c")
    rows, width = history_rows.shape
    blocks = dest_device.shape[1]
    core = lax.axis_index("c").astype(jnp.int32).reshape(1)
    scaling = 1.0 / math.sqrt(rows * lanes * xs * zs)

    def exchange(block):
        chunks = block.reshape(lanes, rows // lanes, block.shape[1])
        return lax.all_to_all(chunks, ("y", "c"), 0, 0, tiled=True).reshape(block.shape)

    square = 2 * rows * rows * width
    (packed,) = call(
        functools.partial(pack_kernel, lanes),
        "pack",
        [shape((rows, 2 * width + 128), bf16)],
        (dest_device, history_rows, cotangent),
        2 * square,
        1,
    )
    routed, route = call(
        functools.partial(route_kernel, lanes),
        "route",
        [shape((rows, 2 * width), bf16), shape((rows, rows), bf16)],
        (exchange(packed),),
        2 * square,
    )
    slots = rows // WIN * HEADS // 2
    total = width * 5
    vmem = pltpu.VMEM
    leaving, keep, send = call(
        functools.partial(layer_kernel, lanes, (xs, ys)),
        "layer",
        [shape((rows, width), bf16), shape((width // 2, total), bf16), shape((width // 2, total), bf16)],
        (
            core,
            source_device,
            source_offset,
            exchange(routed),
            segments,
            row_valid,
            joined_weight,
            output_weight,
        ),
        2 * rows * width * width * 18,
        3,
        (
            vmem((rows, rows), bf16),
            vmem((rows, width), bf16),
            vmem((rows, width), bf16),
            vmem((rows, width), bf16),
            vmem((rows, 1), f32),
            vmem((rows, 4 * width), bf16),
            vmem((rows, 4 * width), bf16),
            vmem((slots, WIN, 2 * WIN), bf16),
            vmem((slots, WIN, 2 * WIN), bf16),
            vmem((rows, width), f32),
            vmem((rows, 1), f32),
            vmem((rows, width), bf16),
            vmem((rows, 4 * width), bf16),
        ),
    )
    arrived = lax.ppermute(send, "c", [(0, 1), (1, 0)])
    summed = (keep.astype(f32) + arrived.astype(f32)).astype(bf16)
    summed, leaving = lax.optimization_barrier((summed, leaving))
    partial = lax.psum_scatter(summed, "x", scatter_dimension=0, tiled=True)

    (returning,) = call(
        return_kernel, "back", [shape((rows, width), bf16)], (route, exchange(leaving)), square
    )
    (row_grad,) = call(
        functools.partial(unpack_kernel, lanes, blocks),
        "unpack",
        [shape((rows, width), bf16)],
        (exchange(returning),),
        square,
    )

    own = width // (lanes * xs)
    piece = -(-total // (zs * 128)) * 128
    (pieces,) = call(
        split_kernel, "split", [shape((ys, zs, own, piece), bf16)], (partial.reshape(ys, own, total),)
    )
    pieces = lax.all_to_all(pieces.reshape(ys * zs, own, piece), ("y", "z"), 0, 0, tiled=True)
    (spread,) = call(
        functools.partial(total_kernel, scaling), "total", [shape((xs * zs, own, piece), bf16)], (pieces,)
    )
    spread = lax.all_to_all(spread, ("x", "z"), 0, 0, tiled=True)
    joined_grad, output_grad = call(
        result_kernel,
        "result",
        [shape((width // lanes, 4 * width), f32), shape((width // lanes, width), f32)],
        (spread.reshape(xs, zs, own, piece),),
    )
    return (row_grad, joined_grad, output_grad)


def solution(mesh):
    torus = Mesh(mesh.devices.reshape(4, 12, 8, 2), ("x", "z", "y", "c"))
    everywhere = P(("x", "z", "y", "c"), None)
    return jax.shard_map(
        on_device,
        mesh=torus,
        in_specs=(everywhere,) * 7 + (P(), P()),
        out_specs=(everywhere, P(("y", "c"), None), P(("y", "c"), None)),
        check_vma=False,
    )
```

time: 520 us -> 195 us (0.38)
  the two profiles are of different devices: /device:TPU:32 before, /device:TPU:1 now
where the time goes in v1:
time: 195 us; the launch traced here: 194 us
  waiting for transfers between devices  87.9 us (45%)
  starting transfers between devices  39.8 us (20%)
  blocking collectives  32.3 us (17%)
  Pallas kernels  14.7 us (8%)
  between operations  14.2 us (7%)
  local copies, waits for them, and re-layouts  3.56 us (2%)
    all_to_all x1, blocking collectives, exchange(): lax.all_to_all(chunks, ('y', 'c'), 0, 0, tiled=True).reshape(block.shape)  32.3 us
    all_to_all x3, waiting for transfers between devices, exchange(): lax.all_to_all(chunks, ('y', 'c'), 0, 0, tiled=True).reshape(block.shape)  28.2 us
    reduce_scatter x1, waiting for transfers between devices, on_device(): partial = lax.psum_scatter(summed, 'x', scatter_dimension=0, tiled=True)  25.2 us
    all_to_all x1, waiting for transfers between devices, on_device(): lax.all_to_all(pieces.reshape(ys * zs, own, piece), ('y', 'z'), 0, 0, til...  17.3 us
    all_to_all x1, starting transfers between devices, on_device(): lax.all_to_all(pieces.reshape(ys * zs, own, piece), ('y', 'z'), 0, 0, til...  16.4 us
    all_to_all x3, starting transfers between devices, exchange(): lax.all_to_all(chunks, ('y', 'c'), 0, 0, tiled=True).reshape(block.shape)  16.2 us
    pallas_call x8, Pallas kernels, call(): pl.pallas_call(kernel, out_shape=tuple(out_shape), in_specs=[smem] * scal...  14.7 us
    all_to_all x1, waiting for transfers between devices, on_device(): spread = lax.all_to_all(spread, ('x', 'z'), 0, 0, tiled=True)  14.1 us
  transfers between devices with their start and end apart: 7, of which 6 were waited for; matrix products, arithmetic and copies ran while one was open for 0% of the time, Pallas kernels for 2%

profile of v1, /device:TPU:1, one launch (start us, length us, event | category | flops | bytes accessed | tf_op | source)
XLA Modules:
  0.0 193.8 jit_solution(18305414451566301230)
XLA Ops:
  7.2 0.0 copy-start.1
  7.2 0.9 copy-done.1
  8.1 0.0 copy-start.2
  8.1 0.9 copy-done.2
  9.1 0.0 copy-start.3
  9.1 0.7 copy-done.3
  9.7 0.9 pack.1
  10.6 0.0 copy-start.4
  10.6 0.0 copy-start.5
  10.6 0.0 copy-start.6
  10.6 0.0 copy-start.7
  10.7 0.0 copy-start.8
  10.7 0.0 copy-start.9
  10.7 32.3 %all_to_all.30 = bf16[16,16,1152]{2,1,0:T(8,128)(2,1)S(1)} all-to-all(bf16[16,16,1152]{2,1,0:T(8,128)(2,1)S(1)} %bitcast.13), channel_id=1, replica_groups=mesh['x'=4,'z'=12,'y'=8,'c'=2] {'y','c'}, dimensions={0} | all-to-all | bytes 1179648 | tf_op jit(solution)/shard_map/all_to_all | solution.py:406
  43.0 1.5 route.1
  44.4 3.5 %all-to-all-start.1 = ((bf16[16,16,1024]{2,1,0:T(8,128)(2,1)}), bf16[16,16,1024]{2,1,0:T(8,128)(2,1)S(1)}, u32[]{:S(2)}, u32[]{:S(2)}) async-start(bf16[16,16,1024]{2,1,0:T(8,128)(2,1)} %bitcast.3), calls=%async_computation.1 | async-start | bytes 1048576 | tf_op jit(solution)/shard_map/all_to_all | solution.py:406
  47.9 0.0 reduce-scatter.2.cloned.1.call-start
  48.0 17.3 %all-to-all-done.1 = bf16[16,16,1024]{2,1,0:T(8,128)(2,1)S(1)} async-done(((bf16[16,16,1024]{2,1,0:T(8,128)(2,1)}), bf16[16,16,1024]{2,1,0:T(8,128)(2,1)S(1)}, u32[]{:S(2)}, u32[]{:S(2)}) %all-to-all-start.1) | async-done | bytes 524320 | tf_op jit(solution)/shard_map/all_to_all | solution.py:406
  65.2 0.0 copy-done.4
  65.2 0.0 copy-done.5
  65.2 0.0 copy-done.6
  65.3 0.0 copy-done.7
  65.3 0.0 copy-done.8
  65.3 0.0 copy-done.9
  65.3 8.2 %layer.1 = (bf16[256,512]{1,0:T(8,128)(2,1)}, bf16[256,2560]{1,0:T(8,128)(2,1)S(1)}, bf16[256,2560]{1,0:T(8,128)(2,1)S(1)}) custom-call(s32[1]{0:T(128)} %bitcast.2.core_ref, s32[1,8]{1,0:T(1,128)S(1)} %copy-done.8, s32[1,8]{1,0:T(1,128)S(1)} %copy-done.9, bf16[256,1024]{1,0:T(8,128)(2,1)S(1)} %bitcast.17, s32[1,256]{1,0:T(1,128)S(1)} %copy-done.6, ...), custom_call_target="tpu_custom_call" | custom-call | flops 2415919104 | bytes 6031428 | tf_op jit(solution)/shard_map/layer/pallas_call | solution.py:373
  73.5 1.9 collective-permute-start
  75.4 3.0 %collective-permute-done = bf16[256,2560]{1,0:T(8,128)(2,1)S(1)} collective-permute-done((bf16[256,2560]{1,0:T(8,128)(2,1)S(1)}, bf16[256,2560]{1,0:T(8,128)(2,1)S(1)}, u32[]{:S(2)}, u32[]{:S(2)}) %collective-permute-start) | collective-permute-done | bytes 1310752 | tf_op jit(solution)/shard_map/ppermute | solution.py:459
  78.4 1.4 add_convert_fusion
  79.8 0.0 reduce-scatter.2.cloned.1.call-update
  79.8 3.5 %all-to-all-start.2 = ((bf16[16,16,512]{2,1,0:T(8,128)(2,1)}), bf16[16,16,512]{2,1,0:T(8,128)(2,1)S(1)}, u32[]{:S(2)}, u32[]{:S(2)}) async-start(bf16[16,16,512]{2,1,0:T(8,128)(2,1)} %bitcast.5), calls=%async_computation.2 | async-start | bytes 524288 | tf_op jit(solution)/shard_map/all_to_all | solution.py:406
  83.3 25.2 %reduce-scatter.2.cloned.1.call-done = bf16[64,2560]{1,0:T(8,128)(2,1)} async-done(((bf16[256,2560]{1,0:T(8,128)(2,1)}), bf16[64,2560]{1,0:T(8,128)(2,1)}) %reduce-scatter.2.cloned.1.call-update) | async-done | bytes 327696 | tf_op jit(solution)/shard_map/reduce_scatter | solution.py:462
  108.5 0.0 copy-start
  108.5 1.0 copy-done
  109.5 0.8 split.1
  110.3 0.0 all-to-all-done.2
  110.3 16.4 %all-to-all-start.4 = ((bf16[96,8,256]{2,1,0:T(8,128)(2,1)}), bf16[96,8,256]{2,1,0:T(8,128)(2,1)S(1)}, u32[]{:S(2)}, u32[]{:S(2)}) async-start(bf16[96,8,256]{2,1,0:T(8,128)(2,1)} %bitcast.10), calls=%async_computation.5 | async-start | bytes 786432 | tf_op jit(solution)/shard_map/all_to_all | solution.py:480
  126.7 0.9 back.1
  127.6 17.3 %all-to-all-done.4.in_ref = bf16[96,8,256]{2,1,0:T(8,128)(2,1)S(1)} async-done(((bf16[96,8,256]{2,1,0:T(8,128)(2,1)}), bf16[96,8,256]{2,1,0:T(8,128)(2,1)S(1)}, u32[]{:S(2)}, u32[]{:S(2)}) %all-to-all-start.4) | async-done | bytes 393248 | tf_op jit(solution)/shard_map/all_to_all | solution.py:480
  145.0 9.2 %all-to-all-start.3 = ((bf16[16,16,512]{2,1,0:T(8,128)(2,1)}), bf16[16,16,512]{2,1,0:T(8,128)(2,1)S(1)}, u32[]{:S(2)}, u32[]{:S(2)}) async-start(bf16[16,16,512]{2,1,0:T(8,128)(2,1)} %bitcast.7), calls=%async_computation.3 | async-start | bytes 524288 | tf_op jit(solution)/shard_map/all_to_all | solution.py:406
  154.2 0.8 total.1
  155.0 10.9 %all-to-all-done.3 = bf16[16,16,512]{2,1,0:T(8,128)(2,1)S(1)} async-done(((bf16[16,16,512]{2,1,0:T(8,128)(2,1)}), bf16[16,16,512]{2,1,0:T(8,128)(2,1)S(1)}, u32[]{:S(2)}, u32[]{:S(2)}) %all-to-all-start.3) | async-done | bytes 262176 | tf_op jit(solution)/shard_map/all_to_all | solution.py:406
  165.9 5.2 %all-to-all-start.5 = ((bf16[48,8,256]{2,1,0:T(8,128)(2,1)}), bf16[48,8,256]{2,1,0:T(8,128)(2,1)S(1)}, u32[]{:S(2)}, u32[]{:S(2)}) async-start(bf16[48,8,256]{2,1,0:T(8,128)(2,1)} %total.1), calls=%async_computation.6 | async-start | bytes 393216 | tf_op jit(solution)/shard_map/all_to_all | solution.py:484
  171.2 0.9 unpack.1
  172.1 14.1 %all-to-all-done.5 = bf16[48,8,256]{2,1,0:T(8,128)(2,1)S(1)} async-done(((bf16[48,8,256]{2,1,0:T(8,128)(2,1)}), bf16[48,8,256]{2,1,0:T(8,128)(2,1)S(1)}, u32[]{:S(2)}, u32[]{:S(2)}) %all-to-all-start.5) | async-done | bytes 196640 | tf_op jit(solution)/shard_map/all_to_all | solution.py:484
  186.2 0.7 result.1
Async XLA Ops:
  7.2 1.0 copy-start.1
  8.1 0.9 copy-start.2
  9.1 0.7 copy-start.3
  10.6 54.6 %copy-start.4 = (bf16[512,2048]{1,0:T(8,128)(2,1)S(1)}, bf16[512,2048]{1,0:T(8,128)(2,1)}, u32[]{:S(2)}) copy-start(bf16[512,2048]{1,0:T(8,128)(2,1)} %weight_ref.1) | copy-start | bytes 6291460
  10.6 54.6 %copy-start.5 = (bf16[512,512]{1,0:T(8,128)(2,1)S(1)}, bf16[512,512]{1,0:T(8,128)(2,1)}, u32[]{:S(2)}) copy-start(bf16[512,512]{1,0:T(8,128)(2,1)} %out_weight_ref.1) | copy-start | bytes 1572868
  10.6 54.6 %copy-start.6 = (s32[1,256]{1,0:T(1,128)S(1)}, s32[1,256]{1,0:T(1,128)}, u32[]{:S(2)}) copy-start(s32[1,256]{1,0:T(1,128)} %seg_ref.1) | copy-start | bytes 3076
  10.6 54.6 %copy-start.7 = (s32[1,256]{1,0:T(1,128)S(1)}, s32[1,256]{1,0:T(1,128)}, u32[]{:S(2)}) copy-start(s32[1,256]{1,0:T(1,128)} %valid_ref.1) | copy-start | bytes 3076
  10.7 54.6 %copy-start.8 = (s32[1,8]{1,0:T(1,128)S(1)}, s32[1,8]{1,0:T(1,128)}, u32[]{:S(2)}) copy-start(s32[1,8]{1,0:T(1,128)} %sources_ref.1) | copy-start | bytes 100
  10.7 54.6 %copy-start.9 = (s32[1,8]{1,0:T(1,128)S(1)}, s32[1,8]{1,0:T(1,128)}, u32[]{:S(2)}) copy-start(s32[1,8]{1,0:T(1,128)} %offsets_ref.1) | copy-start | bytes 100
  44.4 20.8 %all-to-all-start.1 = ((bf16[16,16,1024]{2,1,0:T(8,128)(2,1)}), bf16[16,16,1024]{2,1,0:T(8,128)(2,1)S(1)}, u32[]{:S(2)}, u32[]{:S(2)}) async-start(bf16[16,16,1024]{2,1,0:T(8,128)(2,1)} %bitcast.3), calls=%async_computation.1 | async-start | bytes 1048576 | tf_op jit(solution)/shard_map/all_to_all | solution.py:406
  47.9 60.6 %reduce-scatter.2.cloned.1.call-start = ((), (), s32[]{:S(2)}) async-start(), calls=%async_computation.7 | async-start | bytes 1638400 | tf_op jit(solution)/shard_map/reduce_scatter | solution.py:462
  73.5 4.9 %collective-permute-start = (bf16[256,2560]{1,0:T(8,128)(2,1)S(1)}, bf16[256,2560]{1,0:T(8,128)(2,1)S(1)}, u32[]{:S(2)}, u32[]{:S(2)}) collective-permute-start(bf16[256,2560]{1,0:T(8,128)(2,1)S(1)} %get-tuple-element.15), channel_id=1, source_target_pairs={{0,1},{1,0},{2,3},{3,2},{4,5},{5,4},{6,7},{7,6},{8,9},{9,8},{10,11... | collective-permute-start | bytes 3932168 | tf_op jit(solution)/shard_map/ppermute | solution.py:459
  79.8 30.5 %all-to-all-start.2 = ((bf16[16,16,512]{2,1,0:T(8,128)(2,1)}), bf16[16,16,512]{2,1,0:T(8,128)(2,1)S(1)}, u32[]{:S(2)}, u32[]{:S(2)}) async-start(bf16[16,16,512]{2,1,0:T(8,128)(2,1)} %bitcast.5), calls=%async_computation.2 | async-start | bytes 524288 | tf_op jit(solution)/shard_map/all_to_all | solution.py:406
  108.5 1.0 copy-start
  110.3 34.7 %all-to-all-start.4 = ((bf16[96,8,256]{2,1,0:T(8,128)(2,1)}), bf16[96,8,256]{2,1,0:T(8,128)(2,1)S(1)}, u32[]{:S(2)}, u32[]{:S(2)}) async-start(bf16[96,8,256]{2,1,0:T(8,128)(2,1)} %bitcast.10), calls=%async_computation.5 | async-start | bytes 786432 | tf_op jit(solution)/shard_map/all_to_all | solution.py:480
  145.0 20.9 %all-to-all-start.3 = ((bf16[16,16,512]{2,1,0:T(8,128)(2,1)}), bf16[16,16,512]{2,1,0:T(8,128)(2,1)S(1)}, u32[]{:S(2)}, u32[]{:S(2)}) async-start(bf16[16,16,512]{2,1,0:T(8,128)(2,1)} %bitcast.7), calls=%async_computation.3 | async-start | bytes 524288 | tf_op jit(solution)/shard_map/all_to_all | solution.py:406
  165.9 20.3 %all-to-all-start.5 = ((bf16[48,8,256]{2,1,0:T(8,128)(2,1)}), bf16[48,8,256]{2,1,0:T(8,128)(2,1)S(1)}, u32[]{:S(2)}, u32[]{:S(2)}) async-start(bf16[48,8,256]{2,1,0:T(8,128)(2,1)} %total.1), calls=%async_computation.6 | async-start | bytes 393216 | tf_op jit(solution)/shard_map/all_to_all | solution.py:484
Sparse Core Ops, SparseCore 0:
  79.9 28.5 reduce-scatter.1

commit v2 on v1

--- a/solution.py
+++ b/solution.py
@@ -14,6 +14,7 @@
 f32 = jnp.float32
 bf16 = jnp.bfloat16
 VMEM_LIMIT = 48 * 1024 * 1024
+VMEM_MOST = 62 * 1024 * 1024
 NT = (((1,), (1,)), ((), ()))
 TN = (((0,), (0,)), ((), ()))
 
@@ -194,7 +195,13 @@
     return dot(order, block, dims).astype(bf16)
 
 
-def pack_kernel(lanes, dest_ref, rows_ref, cot_ref, out_ref):
+def pack_kernel(lanes, dest_ref, rows_hbm, cot_hbm, out_ref, rows_ref, cot_ref, sems):
+    copies = [
+        pltpu.make_async_copy(rows_hbm, rows_ref, sems.at[0]),
+        pltpu.make_async_copy(cot_hbm, cot_ref, sems.at[1]),
+    ]
+    for copy in copies:
+        copy.start()
     rows, width = rows_ref.shape
     blocks = dest_ref.shape[1]
     chunk = rows // lanes
@@ -203,14 +210,16 @@
     loaded = lax.broadcasted_iota(jnp.int32, (rows, rows), 1)
     source = place % blocks * (rows // blocks) + place // blocks % half * lanes + place // chunk
     order = jnp.where(source == loaded, 1.0, 0.0).astype(bf16)
-    out_ref[:, :width] = permute(order, rows_ref[...])
-    out_ref[:, width : 2 * width] = permute(order, cot_ref[...])
     extra = out_ref.shape[1] - 2 * width
     block = lax.broadcasted_iota(jnp.int32, (rows, extra), 0) % blocks
     dest = jnp.zeros((rows, extra), f32)
     for j in range(blocks):
         dest = jnp.where(block == j, dest_ref[0, j].astype(f32), dest)
     out_ref[:, 2 * width :] = dest.astype(bf16)
+    copies[0].wait()
+    out_ref[:, :width] = permute(order, rows_ref[...])
+    copies[1].wait()
+    out_ref[:, width : 2 * width] = permute(order, cot_ref[...])
 
 
 def route_kernel(lanes, in_ref, out_ref, order_ref):
@@ -327,7 +336,8 @@
     out_ref[...] = permute(order_ref[...], in_ref[...])
 
 
-def unpack_kernel(lanes, blocks, in_ref, out_ref):
+def unpack_kernel(lanes, blocks, in_ref, partial_ref, out_ref, same_partial_ref):
+    del partial_ref, same_partial_ref
     rows = in_ref.shape[0]
     chunk = rows // lanes
     half = chunk // blocks
@@ -338,13 +348,17 @@
     out_ref[...] = permute(order, in_ref[...])
 
 
-def split_kernel(in_ref, out_ref):
-    pieces, piece = out_ref.shape[1], out_ref.shape[3]
+def fold_kernel(in_ref, out_ref):
+    pieces, _, piece = out_ref.shape
+    total = in_ref.shape[2]
+    folded = jnp.sum(in_ref[...].astype(f32), axis=0).astype(bf16)
     for k in range(pieces):
-        if (k + 1) * piece <= in_ref.shape[2]:
-            out_ref[:, k] = in_ref[:, :, k * piece : (k + 1) * piece]
-        else:
-            out_ref[:, k] = jnp.zeros(out_ref.shape[:1] + out_ref.shape[2:], bf16)
+        at, end = k * piece, min((k + 1) * piece, total)
+        if at < total:
+            out_ref[k, :, : end - at] = folded[:, at:end]
+        if end - at < piece:
+            rest = max(end - at, 0)
+            out_ref[k, :, rest:] = jnp.zeros((out_ref.shape[1], piece - rest), bf16)
 
 
 def total_kernel(scaling, in_ref, out_ref):
@@ -366,17 +380,21 @@
                 output_ref[span, at - split : at - split + step] = block
 
 
-def call(kernel, name, out_shape, operands, flops=0, scalars=0, scratch=()):
+def call(kernel, name, out_shape, operands, flops=0, scalars=0, scratch=(), unmoved=0, aliases=None):
     moved = sum(math.prod(a.shape) * a.dtype.itemsize for a in (*operands, *out_shape))
     smem = pl.BlockSpec(memory_space=pltpu.SMEM)
     vmem = pl.BlockSpec(memory_space=pltpu.VMEM)
+    stay = pl.BlockSpec(memory_space=pl.ANY)
+    aliases = aliases or {}
+    blocked = len(operands) - scalars - unmoved
     return pl.pallas_call(
         kernel,
         out_shape=tuple(out_shape),
-        in_specs=[smem] * scalars + [vmem] * (len(operands) - scalars),
-        out_specs=tuple(vmem for _ in out_shape),
+        in_specs=[smem] * scalars + [vmem] * blocked + [stay] * unmoved,
+        out_specs=tuple(stay if k in aliases.values() else vmem for k in range(len(out_shape))),
+        input_output_aliases=aliases,
         scratch_shapes=list(scratch),
-        compiler_params=pltpu.CompilerParams(vmem_limit_bytes=VMEM_LIMIT),
+        compiler_params=pltpu.CompilerParams(vmem_limit_bytes=VMEM_MOST if unmoved else VMEM_LIMIT),
         cost_estimate=pl.CostEstimate(flops=flops, bytes_accessed=moved, transcendentals=0),
         name=name,
     )(*operands)
@@ -413,6 +431,12 @@
         (dest_device, history_rows, cotangent),
         2 * square,
         1,
+        (
+            pltpu.VMEM((rows, width), bf16),
+            pltpu.VMEM((rows, width), bf16),
+            pltpu.SemaphoreType.DMA((2,)),
+        ),
+        2,
     )
     routed, route = call(
         functools.partial(route_kernel, lanes),
@@ -464,20 +488,21 @@
     (returning,) = call(
         return_kernel, "back", [shape((rows, width), bf16)], (route, exchange(leaving)), square
     )
-    (row_grad,) = call(
+    row_grad, partial = call(
         functools.partial(unpack_kernel, lanes, blocks),
         "unpack",
-        [shape((rows, width), bf16)],
-        (exchange(returning),),
+        [shape((rows, width), bf16), shape(partial.shape, bf16)],
+        (exchange(returning), partial),
         square,
+        unmoved=1,
+        aliases={1: 1},
     )
 
     own = width // (lanes * xs)
     piece = -(-total // (zs * 128)) * 128
-    (pieces,) = call(
-        split_kernel, "split", [shape((ys, zs, own, piece), bf16)], (partial.reshape(ys, own, total),)
-    )
-    pieces = lax.all_to_all(pieces.reshape(ys * zs, own, piece), ("y", "z"), 0, 0, tiled=True)
+    partial = lax.all_to_all(partial.reshape(ys, own, total), "y", 0, 0, tiled=True)
+    (pieces,) = call(fold_kernel, "fold", [shape((zs, own, piece), bf16)], (partial,))
+    pieces = lax.all_to_all(pieces, "z", 0, 0, tiled=True)
     (spread,) = call(
         functools.partial(total_kernel, scaling), "total", [shape((xs * zs, own, piece), bf16)], (pieces,)
     )

time: 195 us -> 175 us (0.90); the launches traced: 194 us -> 172 us
  blocking collectives: 32.3 us -> 115 us
  waiting for transfers between devices: 87.9 us -> 20.3 us
  starting transfers between devices: 39.8 us -> 5.43 us
  local copies, waits for them, and re-layouts: 3.56 us -> 0.04 us
    all_to_all x0 -> x3, blocking collectives: none -> 53.3 us  [the longest x1 19.5 us: on_device(): pieces = lax.all_to_all(pieces, 'z', 0, 0, tiled=True)]
    all_to_all x2 -> x0, waiting for transfers between devices: 31.5 us -> none  [the longest x1 17.3 us: on_device(): lax.all_to_all(pieces.reshape(ys * zs, own, piece), ('y', 'z'), 0, 0, til...]
    all_to_all x1 -> x3, blocking collectives: 32.3 us -> 62.1 us  [exchange(): lax.all_to_all(chunks, ('y', 'c'), 0, 0, tiled=True).reshape(block.shape)]
    reduce_scatter x1, waiting for transfers between devices: 25.2 us -> 0.01 us  [on_device(): partial = lax.psum_scatter(summed, 'x', scatter_dimension=0, tiled=True)]
    all_to_all x2 -> x0, starting transfers between devices: 21.6 us -> none  [the longest x1 16.4 us: on_device(): lax.all_to_all(pieces.reshape(ys * zs, own, piece), ('y', 'z'), 0, 0, til...]
    all_to_all x3 -> x1, starting transfers between devices: 16.2 us -> 3.47 us  [exchange(): lax.all_to_all(chunks, ('y', 'c'), 0, 0, tiled=True).reshape(block.shape)]
    all_to_all x3 -> x1, waiting for transfers between devices: 28.2 us -> 17.3 us  [exchange(): lax.all_to_all(chunks, ('y', 'c'), 0, 0, tiled=True).reshape(block.shape)]
    unnamed x20 -> x12, local copies, waits for them, and re-layouts: 3.56 us -> 0.04 us
  transfers between devices with their start and end apart: 7 -> 3, of which waited for: 6 -> 2; matrix products, arithmetic and copies ran while one was open for 0% -> 0% of each run, Pallas kernels for 2% -> 0%
where the time goes in v2:
time: 175 us; the launch traced here: 172 us
  blocking collectives  115 us (66%)
  waiting for transfers between devices  20.3 us (12%)
  Pallas kernels  14.8 us (8%)
  between operations  14.2 us (8%)
  starting transfers between devices  5.43 us (3%)
    all_to_all x3, blocking collectives, exchange(): lax.all_to_all(chunks, ('y', 'c'), 0, 0, tiled=True).reshape(block.shape)  62.1 us
    all_to_all x1, blocking collectives, on_device(): pieces = lax.all_to_all(pieces, 'z', 0, 0, tiled=True)  19.5 us
    all_to_all x1, blocking collectives, on_device(): spread = lax.all_to_all(spread, ('x', 'z'), 0, 0, tiled=True)  18.6 us
    all_to_all x1, waiting for transfers between devices, exchange(): lax.all_to_all(chunks, ('y', 'c'), 0, 0, tiled=True).reshape(block.shape)  17.3 us
    all_to_all x1, blocking collectives, on_device(): lax.all_to_all(partial.reshape(ys, own, total), 'y', 0, 0, tiled=True)  15.2 us
    pallas_call x8, Pallas kernels, call(): pl.pallas_call(kernel, out_shape=tuple(out_shape), in_specs=[smem] * scal...  14.8 us
  transfers between devices with their start and end apart: 3, of which 2 were waited for; matrix products, arithmetic and copies ran while one was open for 0% of the time, Pallas kernels for 0%

profile of v2, /device:TPU:1, one launch (start us, length us, event | category | flops | bytes accessed | tf_op | source)
XLA Modules:
  0.0 171.5 jit_solution(6605414465176869374)
XLA Ops:
  7.2 2.9 %pack.1 = bf16[256,1152]{1,0:T(8,128)(2,1)} custom-call(s32[1,8]{1,0:T(1,128)} %dest_ref.1, bf16[256,512]{1,0:T(8,128)(2,1)} %rows_hbm.1, bf16[256,512]{1,0:T(8,128)(2,1)} %cot_hbm.1), custom_call_target="tpu_custom_call" | custom-call | flops 134217728 | bytes 1114144 | tf_op jit(solution)/shard_map/pack/pallas_call | solution.py:390
  10.1 0.0 copy-start
  10.1 0.0 copy-start.1
  10.1 0.0 copy-start.2
  10.1 0.0 copy-start.3
  10.1 0.0 copy-start.4
  10.1 0.0 copy-start.5
  10.2 33.2 %all_to_all.35 = bf16[16,16,1152]{2,1,0:T(8,128)(2,1)S(1)} all-to-all(bf16[16,16,1152]{2,1,0:T(8,128)(2,1)} %bitcast.17), channel_id=1, replica_groups=mesh['x'=4,'z'=12,'y'=8,'c'=2] {'y','c'}, dimensions={0} | all-to-all | bytes 1179648 | tf_op jit(solution)/shard_map/all_to_all | solution.py:424
  43.4 1.5 route.1
  44.8 3.5 %all-to-all-start.1 = ((bf16[16,16,1024]{2,1,0:T(8,128)(2,1)}), bf16[16,16,1024]{2,1,0:T(8,128)(2,1)S(1)}, u32[]{:S(2)}, u32[]{:S(2)}) async-start(bf16[16,16,1024]{2,1,0:T(8,128)(2,1)} %bitcast.3), calls=%async_computation.1 | async-start | bytes 1048576 | tf_op jit(solution)/shard_map/all_to_all | solution.py:424
  48.3 0.0 reduce-scatter.2.cloned.1.call-start
  48.4 17.3 %all-to-all-done.1 = bf16[16,16,1024]{2,1,0:T(8,128)(2,1)S(1)} async-done(((bf16[16,16,1024]{2,1,0:T(8,128)(2,1)}), bf16[16,16,1024]{2,1,0:T(8,128)(2,1)S(1)}, u32[]{:S(2)}, u32[]{:S(2)}) %all-to-all-start.1) | async-done | bytes 524320 | tf_op jit(solution)/shard_map/all_to_all | solution.py:424
  65.7 0.0 copy-done
  65.7 0.0 copy-done.1
  65.7 0.0 copy-done.2
  65.7 0.0 copy-done.3
  65.7 0.0 copy-done.4
  65.7 0.0 copy-done.5
  65.7 7.5 %layer.1 = (bf16[256,512]{1,0:T(8,128)(2,1)S(1)}, bf16[256,2560]{1,0:T(8,128)(2,1)S(1)}, bf16[256,2560]{1,0:T(8,128)(2,1)S(1)}) custom-call(s32[1]{0:T(128)} %bitcast.2.core_ref, s32[1,8]{1,0:T(1,128)S(1)} %copy-done.4, s32[1,8]{1,0:T(1,128)S(1)} %copy-done.5, bf16[256,1024]{1,0:T(8,128)(2,1)S(1)} %bitcast.15, s32[1,256]{1,0:T(1,128)S(1)} %copy-done.2, ...), custom_call_target="tpu_custom_call" | custom-call | flops 2415919104 | bytes 6031428 | tf_op jit(solution)/shard_map/layer/pallas_call | solution.py:390
  73.2 1.9 %collective-permute-start = (bf16[256,2560]{1,0:T(8,128)(2,1)S(1)}, bf16[256,2560]{1,0:T(8,128)(2,1)S(1)}, u32[]{:S(2)}, u32[]{:S(2)}) collective-permute-start(bf16[256,2560]{1,0:T(8,128)(2,1)S(1)} %get-tuple-element.17), channel_id=1, source_target_pairs={{0,1},{1,0},{2,3},{3,2},{4,5},{5,4},{6,7},{7,6},{8,9},{9,8},{10,11... | collective-permute-start | bytes 3932168 | tf_op jit(solution)/shard_map/ppermute | solution.py:483
  75.1 3.0 %collective-permute-done = bf16[256,2560]{1,0:T(8,128)(2,1)S(1)} collective-permute-done((bf16[256,2560]{1,0:T(8,128)(2,1)S(1)}, bf16[256,2560]{1,0:T(8,128)(2,1)S(1)}, u32[]{:S(2)}, u32[]{:S(2)}) %collective-permute-start) | collective-permute-done | bytes 1310752 | tf_op jit(solution)/shard_map/ppermute | solution.py:483
  78.1 1.4 add_convert_fusion
  79.5 0.0 reduce-scatter.2.cloned.1.call-update
  79.5 14.4 %all_to_all.36 = bf16[16,16,512]{2,1,0:T(8,128)(2,1)S(1)} all-to-all(bf16[16,16,512]{2,1,0:T(8,128)(2,1)S(1)} %bitcast.16), channel_id=1, replica_groups=mesh['x'=4,'z'=12,'y'=8,'c'=2] {'y','c'}, dimensions={0} | all-to-all | bytes 524288 | tf_op jit(solution)/shard_map/all_to_all | solution.py:424
  94.0 0.2 back.1
  94.2 14.5 %all_to_all.37 = bf16[16,16,512]{2,1,0:T(8,128)(2,1)} all-to-all(bf16[16,16,512]{2,1,0:T(8,128)(2,1)S(1)} %bitcast.13), channel_id=1, replica_groups=mesh['x'=4,'z'=12,'y'=8,'c'=2] {'y','c'}, dimensions={0} | all-to-all | bytes 524288 | tf_op jit(solution)/shard_map/all_to_all | solution.py:424
  108.7 0.0 reduce-scatter.2.cloned.1.call-done.partial_ref
  108.7 1.9 %unpack.1 = (bf16[256,512]{1,0:T(8,128)(2,1)}, bf16[64,2560]{1,0:T(8,128)(2,1)}) custom-call(bf16[256,512]{1,0:T(8,128)(2,1)} %bitcast.19, bf16[64,2560]{1,0:T(8,128)(2,1)} %reduce-scatter.2.cloned.1.call-done.partial_ref), custom_call_target="tpu_custom_call", output_to_operand_aliasing={{1}: (1, {})} | custom-call | flops 67108864 | bytes 1179648 | tf_op jit(solution)/shard_map/unpack/pallas_call | solution.py:390
  110.5 15.2 %all_to_all.38.in_ref = bf16[8,8,2560]{2,1,0:T(8,128)(2,1)S(1)} all-to-all(bf16[8,8,2560]{2,1,0:T(8,128)(2,1)} %bitcast.18), channel_id=1, replica_groups=mesh['x'=4,'z'=12,'y'=8,'c'=2] {'y'}, dimensions={0} | all-to-all | bytes 655360 | tf_op jit(solution)/shard_map/all_to_all | solution.py:503
  125.8 19.5 %all_to_all.39.in_ref = bf16[12,8,256]{2,1,0:T(8,128)(2,1)S(1)} all-to-all(bf16[12,8,256]{2,1,0:T(8,128)(2,1)S(1)} %fold.1), channel_id=1, replica_groups=mesh['x'=4,'z'=12,'y'=8,'c'=2] {'z'}, dimensions={0} | all-to-all | bytes 98304 | tf_op jit(solution)/shard_map/all_to_all | solution.py:505
  145.3 18.6 %all_to_all.40 = bf16[48,8,256]{2,1,0:T(8,128)(2,1)S(1)} all-to-all(bf16[48,8,256]{2,1,0:T(8,128)(2,1)S(1)} %total.1), channel_id=1, replica_groups=mesh['x'=4,'z'=12,'y'=8,'c'=2] {'x','z'}, dimensions={0} | all-to-all | bytes 393216 | tf_op jit(solution)/shard_map/all_to_all | solution.py:509
  163.9 0.7 result.1
  (2 shorter events, 0.1 us)
Async XLA Ops:
  10.1 55.6 %copy-start = (bf16[512,2048]{1,0:T(8,128)(2,1)S(1)}, bf16[512,2048]{1,0:T(8,128)(2,1)}, u32[]{:S(2)}) copy-start(bf16[512,2048]{1,0:T(8,128)(2,1)} %weight_ref.1) | copy-start | bytes 6291460
  10.1 55.6 %copy-start.1 = (bf16[512,512]{1,0:T(8,128)(2,1)S(1)}, bf16[512,512]{1,0:T(8,128)(2,1)}, u32[]{:S(2)}) copy-start(bf16[512,512]{1,0:T(8,128)(2,1)} %out_weight_ref.1) | copy-start | bytes 1572868
  10.1 55.6 %copy-start.2 = (s32[1,256]{1,0:T(1,128)S(1)}, s32[1,256]{1,0:T(1,128)}, u32[]{:S(2)}) copy-start(s32[1,256]{1,0:T(1,128)} %seg_ref.1) | copy-start | bytes 3076
  10.1 55.6 %copy-start.3 = (s32[1,256]{1,0:T(1,128)S(1)}, s32[1,256]{1,0:T(1,128)}, u32[]{:S(2)}) copy-start(s32[1,256]{1,0:T(1,128)} %valid_ref.1) | copy-start | bytes 3076
  10.1 55.6 %copy-start.4 = (s32[1,8]{1,0:T(1,128)S(1)}, s32[1,8]{1,0:T(1,128)}, u32[]{:S(2)}) copy-start(s32[1,8]{1,0:T(1,128)} %sources_ref.1) | copy-start | bytes 100
  10.1 55.5 %copy-start.5 = (s32[1,8]{1,0:T(1,128)S(1)}, s32[1,8]{1,0:T(1,128)}, u32[]{:S(2)}) copy-start(s32[1,8]{1,0:T(1,128)} %offsets_ref.1) | copy-start | bytes 100
  44.8 20.8 %all-to-all-start.1 = ((bf16[16,16,1024]{2,1,0:T(8,128)(2,1)}), bf16[16,16,1024]{2,1,0:T(8,128)(2,1)S(1)}, u32[]{:S(2)}, u32[]{:S(2)}) async-start(bf16[16,16,1024]{2,1,0:T(8,128)(2,1)} %bitcast.3), calls=%async_computation.1 | async-start | bytes 1048576 | tf_op jit(solution)/shard_map/all_to_all | solution.py:424
  48.3 60.3 %reduce-scatter.2.cloned.1.call-start = ((), (), s32[]{:S(2)}) async-start(), calls=%async_computation.8 | async-start | bytes 1638400 | tf_op jit(solution)/shard_map/reduce_scatter | solution.py:486
  73.2 4.9 %collective-permute-start = (bf16[256,2560]{1,0:T(8,128)(2,1)S(1)}, bf16[256,2560]{1,0:T(8,128)(2,1)S(1)}, u32[]{:S(2)}, u32[]{:S(2)}) collective-permute-start(bf16[256,2560]{1,0:T(8,128)(2,1)S(1)} %get-tuple-element.17), channel_id=1, source_target_pairs={{0,1},{1,0},{2,3},{3,2},{4,5},{5,4},{6,7},{7,6},{8,9},{9,8},{10,11... | collective-permute-start | bytes 3932168 | tf_op jit(solution)/shard_map/ppermute | solution.py:483
Sparse Core Ops, SparseCore 0:
  79.7 27.9 reduce-scatter.1

commit v3 on v2

--- a/solution.py
+++ b/solution.py
@@ -222,7 +222,7 @@
     out_ref[:, width : 2 * width] = permute(order, cot_ref[...])
 
 
-def route_kernel(lanes, in_ref, out_ref, order_ref):
+def route_kernel(lanes, me_ref, in_ref, out_ref, places_ref, rank_ref):
     rows, double = out_ref.shape
     chunk = rows // lanes
     blocks = chunk // 2
@@ -238,8 +238,10 @@
     row = lax.broadcasted_iota(jnp.int32, (rows, 1), 0)
     target = dest[:, :1] * chunk + (row // blocks % 2 * blocks).astype(f32) + rank
     order = jnp.where(target == other.astype(f32), 1.0, 0.0).astype(bf16)
-    order_ref[...] = order
     out_ref[...] = permute(order, in_ref[:, :double], TN)
+    rank_ref[...] = jnp.broadcast_to(rank, rank_ref.shape)
+    own = pl.multiple_of(me_ref[0] * chunk, chunk)
+    places_ref[...] = rank_ref[pl.ds(own, blocks), :].astype(jnp.int32)
 
 
 def gather_order(lanes, sources_ref, offsets_ref, order_ref):
@@ -252,10 +254,13 @@
     column = lax.broadcasted_iota(jnp.int32, (span, rows), 1)
     base = inside % lanes * chunk + inside // lanes % half * blocks
     keys = [sources_ref[0, t] * 2 + offsets_ref[0, t] for t in range(blocks)]
+    slots = []
     for t in range(blocks):
         slot = sum(jnp.where(keys[u] < keys[t], 1, 0) for u in range(blocks) if u != t)
         order = jnp.where(column == base + slot, 1.0, 0.0)
         order_ref[t * span : (t + 1) * span, :] = order.astype(bf16)
+        slots.append(slot)
+    return slots
 
 
 def spread_order(parts, core, width):
@@ -275,7 +280,7 @@
 def layer_kernel(
     lanes,
     parts,
-    core_ref,
+    me_ref,
     sources_ref,
     offsets_ref,
     in_ref,
@@ -301,7 +306,7 @@
     proj_cot_ref,
 ):
     rows, width = rows_ref.shape
-    gather_order(lanes, sources_ref, offsets_ref, order_ref)
+    slots = gather_order(lanes, sources_ref, offsets_ref, order_ref)
     rows_ref[...] = permute(order_ref[...], in_ref[:, :width])
     cot_ref[...] = permute(order_ref[...], in_ref[:, width:])
     stored = (
@@ -316,7 +321,7 @@
         gated_ref,
     )
     forward_body(rows_ref, seg_ref, valid_ref, weight_ref, *stored)
-    spread = spread_order(parts, core_ref[0], width)
+    spread = spread_order(parts, me_ref[0] % 2, width)
     work_grad = backward_body(
         rows_ref,
         cot_ref,
@@ -329,23 +334,35 @@
         keep_ref,
         send_ref,
     )
-    leave_ref[...] = permute(order_ref[...], work_grad, TN)
-
-
-def return_kernel(order_ref, in_ref, out_ref):
-    out_ref[...] = permute(order_ref[...], in_ref[...])
-
-
-def unpack_kernel(lanes, blocks, in_ref, partial_ref, out_ref, same_partial_ref):
-    del partial_ref, same_partial_ref
-    rows = in_ref.shape[0]
-    chunk = rows // lanes
-    half = chunk // blocks
-    loaded = lax.broadcasted_iota(jnp.int32, (rows, rows), 0)
-    place = lax.broadcasted_iota(jnp.int32, (rows, rows), 1)
-    source = place % blocks * (rows // blocks) + place // blocks % half * lanes + place // chunk
-    order = jnp.where(source == loaded, 1.0, 0.0).astype(bf16)
-    out_ref[...] = permute(order, in_ref[...])
+    span = rows // len(slots)
+    for t, slot in enumerate(slots):
+        at = pl.multiple_of(slot * span, span)
+        leave_ref[pl.ds(at, span), :] = work_grad[t * span : (t + 1) * span]
+
+
+def collect_kernel(block_rows, dest_ref, places_ref, in_ref, out_ref, sems):
+    blocks = dest_ref.shape[1]
+    copies = []
+    for j in range(blocks):
+        at = pl.multiple_of((dest_ref[0, j] * blocks + places_ref[j, 0]) * block_rows, block_rows)
+        copies.append(
+            pltpu.make_async_copy(
+                in_ref.at[pl.ds(at, block_rows)],
+                out_ref.at[pl.ds(j * block_rows, block_rows)],
+                sems.at[j],
+            )
+        )
+    for copy in copies:
+        copy.start()
+    for copy in copies:
+        copy.wait()
+
+
+def sum_kernel(in_ref, out_ref):
+    total = in_ref[0].astype(f32)
+    for k in range(1, in_ref.shape[0]):
+        total += in_ref[k].astype(f32)
+    out_ref[...] = total.astype(bf16)
 
 
 def fold_kernel(in_ref, out_ref):
@@ -380,19 +397,17 @@
                 output_ref[span, at - split : at - split + step] = block
 
 
-def call(kernel, name, out_shape, operands, flops=0, scalars=0, scratch=(), unmoved=0, aliases=None):
+def call(kernel, name, out_shape, operands, flops=0, scalars=0, scratch=(), unmoved=0, kept=False):
     moved = sum(math.prod(a.shape) * a.dtype.itemsize for a in (*operands, *out_shape))
     smem = pl.BlockSpec(memory_space=pltpu.SMEM)
     vmem = pl.BlockSpec(memory_space=pltpu.VMEM)
     stay = pl.BlockSpec(memory_space=pl.ANY)
-    aliases = aliases or {}
     blocked = len(operands) - scalars - unmoved
     return pl.pallas_call(
         kernel,
         out_shape=tuple(out_shape),
         in_specs=[smem] * scalars + [vmem] * blocked + [stay] * unmoved,
-        out_specs=tuple(stay if k in aliases.values() else vmem for k in range(len(out_shape))),
-        input_output_aliases=aliases,
+        out_specs=tuple(stay if kept else vmem for _ in out_shape),
         scratch_shapes=list(scratch),
         compiler_params=pltpu.CompilerParams(vmem_limit_bytes=VMEM_MOST if unmoved else VMEM_LIMIT),
         cost_estimate=pl.CostEstimate(flops=flops, bytes_accessed=moved, transcendentals=0),
@@ -416,7 +431,7 @@
     lanes = ys * lax.axis_size("c")
     rows, width = history_rows.shape
     blocks = dest_device.shape[1]
-    core = lax.axis_index("c").astype(jnp.int32).reshape(1)
+    me = lax.axis_index(("y", "c")).astype(jnp.int32).reshape(1)
     scaling = 1.0 / math.sqrt(rows * lanes * xs * zs)
 
     def exchange(block):
@@ -438,12 +453,14 @@
         ),
         2,
     )
-    routed, route = call(
+    routed, places = call(
         functools.partial(route_kernel, lanes),
         "route",
-        [shape((rows, 2 * width), bf16), shape((rows, rows), bf16)],
-        (exchange(packed),),
+        [shape((rows, 2 * width), bf16), shape((blocks, 128), jnp.int32)],
+        (me, exchange(packed)),
         2 * square,
+        1,
+        (pltpu.VMEM((rows, 128), f32),),
     )
     slots = rows // WIN * HEADS // 2
     total = width * 5
@@ -453,7 +470,7 @@
         "layer",
         [shape((rows, width), bf16), shape((width // 2, total), bf16), shape((width // 2, total), bf16)],
         (
-            core,
+            me,
             source_device,
             source_offset,
             exchange(routed),
@@ -480,26 +497,13 @@
             vmem((rows, 4 * width), bf16),
         ),
     )
+    gathered = lax.all_gather(leaving, ("y", "c"), axis=0, tiled=True)
     arrived = lax.ppermute(send, "c", [(0, 1), (1, 0)])
     summed = (keep.astype(f32) + arrived.astype(f32)).astype(bf16)
-    summed, leaving = lax.optimization_barrier((summed, leaving))
-    partial = lax.psum_scatter(summed, "x", scatter_dimension=0, tiled=True)
-
-    (returning,) = call(
-        return_kernel, "back", [shape((rows, width), bf16)], (route, exchange(leaving)), square
-    )
-    row_grad, partial = call(
-        functools.partial(unpack_kernel, lanes, blocks),
-        "unpack",
-        [shape((rows, width), bf16), shape(partial.shape, bf16)],
-        (exchange(returning), partial),
-        square,
-        unmoved=1,
-        aliases={1: 1},
-    )
-
     own = width // (lanes * xs)
     piece = -(-total // (zs * 128)) * 128
+    summed = lax.all_to_all(summed.reshape(xs, ys * own, total), "x", 0, 0, tiled=True)
+    (partial,) = call(sum_kernel, "sum", [shape((ys * own, total), bf16)], (summed,))
     partial = lax.all_to_all(partial.reshape(ys, own, total), "y", 0, 0, tiled=True)
     (pieces,) = call(fold_kernel, "fold", [shape((zs, own, piece), bf16)], (partial,))
     pieces = lax.all_to_all(pieces, "z", 0, 0, tiled=True)
@@ -507,6 +511,16 @@
         functools.partial(total_kernel, scaling), "total", [shape((xs * zs, own, piece), bf16)], (pieces,)
     )
     spread = lax.all_to_all(spread, ("x", "z"), 0, 0, tiled=True)
+    (row_grad,) = call(
+        functools.partial(collect_kernel, rows // blocks),
+        "collect",
+        [shape((rows, width), bf16)],
+        (dest_device, places, gathered),
+        scalars=2,
+        scratch=(pltpu.SemaphoreType.DMA((blocks,)),),
+        unmoved=1,
+        kept=True,
+    )
     joined_grad, output_grad = call(
         result_kernel,
         "result",

time: 175 us -> 176 us (level)
  blocking collectives: 115 us -> 96.2 us
  starting transfers between devices: 5.43 us -> 16 us
  Pallas kernels: 14.8 us -> 22.4 us
  local copies, waits for them, and re-layouts: 0.04 us -> 2.16 us
    all_to_all x3 -> x1, blocking collectives: 62.1 us -> 20.1 us  [exchange(): lax.all_to_all(chunks, ('y', 'c'), 0, 0, tiled=True).reshape(block.shape)]
    all_to_all x0 -> x1, blocking collectives: none -> 20.1 us  [on_device(): lax.all_to_all(summed.reshape(xs, ys * own, total), 'x', 0, 0, tiled=True)]
    all_to_all x1, starting transfers between devices: 3.47 us -> 14 us  [exchange(): lax.all_to_all(chunks, ('y', 'c'), 0, 0, tiled=True).reshape(block.shape)]
    pallas_call x8, Pallas kernels: 14.8 us -> 22.4 us  [call(): pl.pallas_call(kernel, out_shape=tuple(out_shape), in_specs=[smem] * scal...]
    all_to_all x1, blocking collectives: 15.2 us -> 18.8 us  [on_device(): lax.all_to_all(partial.reshape(ys, own, total), 'y', 0, 0, tiled=True)]
    unnamed x12 -> x16, local copies, waits for them, and re-layouts: 0.04 us -> 2.16 us
    all_to_all x1, blocking collectives: 18.6 us -> 16.7 us  [on_device(): spread = lax.all_to_all(spread, ('x', 'z'), 0, 0, tiled=True)]
  transfers between devices with their start and end apart: 3 -> 3, of which waited for: 2 -> 2; matrix products, arithmetic and copies ran while one was open for 0% -> 0% of each run, Pallas kernels for 0% -> 1%
where the time goes in v3:
time: 176 us; the launch traced here: 173 us
  blocking collectives  96.2 us (55%)
  Pallas kernels  22.4 us (13%)
  waiting for transfers between devices  21.8 us (12%)
  starting transfers between devices  16 us (9%)
  between operations  14.2 us (8%)
  local copies, waits for them, and re-layouts  2.16 us (1%)
    pallas_call x8, Pallas kernels, call(): pl.pallas_call(kernel, out_shape=tuple(out_shape), in_specs=[smem] * scal...  22.4 us
    all_to_all x1, blocking collectives, on_device(): pieces = lax.all_to_all(pieces, 'z', 0, 0, tiled=True)  20.4 us
    all_to_all x1, blocking collectives, exchange(): lax.all_to_all(chunks, ('y', 'c'), 0, 0, tiled=True).reshape(block.shape)  20.1 us
    all_to_all x1, blocking collectives, on_device(): lax.all_to_all(summed.reshape(xs, ys * own, total), 'x', 0, 0, tiled=True)  20.1 us
    all_to_all x1, blocking collectives, on_device(): lax.all_to_all(partial.reshape(ys, own, total), 'y', 0, 0, tiled=True)  18.8 us
    all_to_all x1, waiting for transfers between devices, exchange(): lax.all_to_all(chunks, ('y', 'c'), 0, 0, tiled=True).reshape(block.shape)  18.6 us
    all_to_all x1, blocking collectives, on_device(): spread = lax.all_to_all(spread, ('x', 'z'), 0, 0, tiled=True)  16.7 us
    all_to_all x1, starting transfers between devices, exchange(): lax.all_to_all(chunks, ('y', 'c'), 0, 0, tiled=True).reshape(block.shape)  14 us
  transfers between devices with their start and end apart: 3, of which 2 were waited for; matrix products, arithmetic and copies ran while one was open for 0% of the time, Pallas kernels for 1%

profile of v3, /device:TPU:1, one launch (start us, length us, event | category | flops | bytes accessed | tf_op | source)
XLA Modules:
  0.0 173.1 jit_solution(2587282303611943763)
XLA Ops:
  7.2 2.9 %pack.1 = bf16[256,1152]{1,0:T(8,128)(2,1)} custom-call(s32[1,8]{1,0:T(1,128)} %dest_ref.3, bf16[256,512]{1,0:T(8,128)(2,1)} %rows_hbm.1, bf16[256,512]{1,0:T(8,128)(2,1)} %cot_hbm.1), custom_call_target="tpu_custom_call" | custom-call | flops 134217728 | bytes 1114144 | tf_op jit(solution)/shard_map/pack/pallas_call | solution.py:406
  10.1 0.0 copy-start.1
  10.1 0.0 copy-start.4
  10.1 0.0 copy-start.5
  10.1 0.0 copy-start.6
  10.1 0.0 copy-start.7
  10.1 14.0 %all-to-all-start = ((bf16[16,16,1152]{2,1,0:T(8,128)(2,1)}), bf16[16,16,1152]{2,1,0:T(8,128)(2,1)S(1)}, u32[]{:S(2)}, u32[]{:S(2)}) async-start(bf16[16,16,1152]{2,1,0:T(8,128)(2,1)} %bitcast.14), calls=%async_computation | async-start | bytes 1179648 | tf_op jit(solution)/shard_map/all_to_all | solution.py:439
  24.2 0.0 all-gather.2.cloned.1.call-start
  24.2 18.6 %all-to-all-done = bf16[16,16,1152]{2,1,0:T(8,128)(2,1)S(1)} async-done(((bf16[16,16,1152]{2,1,0:T(8,128)(2,1)}), bf16[16,16,1152]{2,1,0:T(8,128)(2,1)S(1)}, u32[]{:S(2)}, u32[]{:S(2)}) %all-to-all-start) | async-done | bytes 589856 | tf_op jit(solution)/shard_map/all_to_all | solution.py:439
  42.8 0.7 route.1
  43.5 0.0 copy-start
  43.5 20.1 %all_to_all.30 = bf16[16,16,1024]{2,1,0:T(8,128)(2,1)S(1)} all-to-all(bf16[16,16,1024]{2,1,0:T(8,128)(2,1)S(1)} %bitcast.12), channel_id=1, replica_groups=mesh['x'=4,'z'=12,'y'=8,'c'=2] {'y','c'}, dimensions={0} | all-to-all | bytes 1048576 | tf_op jit(solution)/shard_map/all_to_all | solution.py:439
  63.6 0.0 copy-done
  63.6 0.0 copy-done.1
  63.7 0.0 copy-done.4
  63.7 0.0 copy-done.5
  63.7 0.0 copy-done.6
  63.7 0.0 copy-done.7
  63.7 0.0 copy-start.3
  63.7 1.0 copy-done.3
  64.7 8.0 %layer.1 = (bf16[256,512]{1,0:T(8,128)(2,1)}, bf16[256,2560]{1,0:T(8,128)(2,1)S(1)}, bf16[256,2560]{1,0:T(8,128)(2,1)S(1)}) custom-call(s32[1]{0:T(128)} %bitcast.me_ref, s32[1,8]{1,0:T(1,128)S(1)} %copy-done.6, s32[1,8]{1,0:T(1,128)S(1)} %copy-done.7, bf16[256,1024]{1,0:T(8,128)(2,1)S(1)} %bitcast.11, s32[1,256]{1,0:T(1,128)S(1)} %copy-done.4, ...), custom_call_target="tpu_custom_call" | custom-call | flops 2415919104 | bytes 6031428 | tf_op jit(solution)/shard_map/layer/pallas_call | solution.py:406
  72.7 0.0 copy-start.2
  72.7 1.1 copy-done.2
  73.8 0.0 all-gather.2.cloned.1.call-update
  73.8 1.9 %collective-permute-start = (bf16[256,2560]{1,0:T(8,128)(2,1)}, bf16[256,2560]{1,0:T(8,128)(2,1)S(1)}, u32[]{:S(2)}, u32[]{:S(2)}) collective-permute-start(bf16[256,2560]{1,0:T(8,128)(2,1)} %copy-done.2), channel_id=1, source_target_pairs={{0,1},{1,0},{2,3},{3,2},{4,5},{5,4},{6,7},{7,6},{8,9},{9,8},{10,11... | collective-permute-start | bytes 3932168 | tf_op jit(solution)/shard_map/ppermute | solution.py:501
  75.8 3.2 %collective-permute-done = bf16[256,2560]{1,0:T(8,128)(2,1)S(1)} collective-permute-done((bf16[256,2560]{1,0:T(8,128)(2,1)}, bf16[256,2560]{1,0:T(8,128)(2,1)S(1)}, u32[]{:S(2)}, u32[]{:S(2)}) %collective-permute-start) | collective-permute-done | bytes 1310752 | tf_op jit(solution)/shard_map/ppermute | solution.py:501
  79.0 0.4 add_convert_fusion
  79.3 20.1 %all_to_all.31.in_ref = bf16[4,64,2560]{2,1,0:T(8,128)(2,1)S(1)} all-to-all(bf16[4,64,2560]{2,1,0:T(8,128)(2,1)S(1)} %bitcast.13), channel_id=1, replica_groups=mesh['x'=4,'z'=12,'y'=8,'c'=2] {'x'}, dimensions={0} | all-to-all | bytes 2621440 | tf_op jit(solution)/shard_map/all_to_all | solution.py:505
  99.4 0.2 sum.1
  99.6 18.8 %all_to_all.32.in_ref = bf16[8,8,2560]{2,1,0:T(8,128)(2,1)S(1)} all-to-all(bf16[8,8,2560]{2,1,0:T(8,128)(2,1)S(1)} %bitcast.9), channel_id=1, replica_groups=mesh['x'=4,'z'=12,'y'=8,'c'=2] {'y'}, dimensions={0} | all-to-all | bytes 655360 | tf_op jit(solution)/shard_map/all_to_all | solution.py:507
  118.5 20.4 %all_to_all.33.in_ref = bf16[12,8,256]{2,1,0:T(8,128)(2,1)S(1)} all-to-all(bf16[12,8,256]{2,1,0:T(8,128)(2,1)S(1)} %fold.1), channel_id=1, replica_groups=mesh['x'=4,'z'=12,'y'=8,'c'=2] {'z'}, dimensions={0} | all-to-all | bytes 98304 | tf_op jit(solution)/shard_map/all_to_all | solution.py:509
  138.9 16.7 %all_to_all.34 = bf16[48,8,256]{2,1,0:T(8,128)(2,1)S(1)} all-to-all(bf16[48,8,256]{2,1,0:T(8,128)(2,1)S(1)} %total.1), channel_id=1, replica_groups=mesh['x'=4,'z'=12,'y'=8,'c'=2] {'x','z'}, dimensions={0} | all-to-all | bytes 393216 | tf_op jit(solution)/shard_map/all_to_all | solution.py:513
  155.6 0.7 result.1
  156.4 0.0 all-gather.2.cloned.1.call-done.in_ref
  156.4 9.8 %collect.1 = bf16[256,512]{1,0:T(8,128)(2,1)} custom-call(s32[1,8]{1,0:T(1,128)} %dest_ref.3, s32[8,128]{1,0:T(8,128)} %copy-done, bf16[4096,512]{1,0:T(8,128)(2,1)} %all-gather.2.cloned.1.call-done.in_ref), custom_call_target="tpu_custom_call" | custom-call | bytes 4460576 | tf_op jit(solution)/shard_map/collect/pallas_call | solution.py:406
  (2 shorter events, 0.1 us)
Async XLA Ops:
  10.1 53.6 %copy-start.1 = (bf16[512,2048]{1,0:T(8,128)(2,1)S(1)}, bf16[512,2048]{1,0:T(8,128)(2,1)}, u32[]{:S(2)}) copy-start(bf16[512,2048]{1,0:T(8,128)(2,1)} %weight_ref.1) | copy-start | bytes 6291460
  10.1 53.6 %copy-start.4 = (s32[1,256]{1,0:T(1,128)S(1)}, s32[1,256]{1,0:T(1,128)}, u32[]{:S(2)}) copy-start(s32[1,256]{1,0:T(1,128)} %seg_ref.1) | copy-start | bytes 3076
  10.1 53.6 %copy-start.5 = (s32[1,256]{1,0:T(1,128)S(1)}, s32[1,256]{1,0:T(1,128)}, u32[]{:S(2)}) copy-start(s32[1,256]{1,0:T(1,128)} %valid_ref.1) | copy-start | bytes 3076
  10.1 53.6 %copy-start.6 = (s32[1,8]{1,0:T(1,128)S(1)}, s32[1,8]{1,0:T(1,128)}, u32[]{:S(2)}) copy-start(s32[1,8]{1,0:T(1,128)} %sources_ref.1) | copy-start | bytes 100
  10.1 53.6 %copy-start.7 = (s32[1,8]{1,0:T(1,128)S(1)}, s32[1,8]{1,0:T(1,128)}, u32[]{:S(2)}) copy-start(s32[1,8]{1,0:T(1,128)} %offsets_ref.1) | copy-start | bytes 100
  10.1 32.7 %all-to-all-start = ((bf16[16,16,1152]{2,1,0:T(8,128)(2,1)}), bf16[16,16,1152]{2,1,0:T(8,128)(2,1)S(1)}, u32[]{:S(2)}, u32[]{:S(2)}) async-start(bf16[16,16,1152]{2,1,0:T(8,128)(2,1)} %bitcast.14), calls=%async_computation | async-start | bytes 1179648 | tf_op jit(solution)/shard_map/all_to_all | solution.py:439
  24.2 132.2 %all-gather.2.cloned.1.call-start = ((), (), s32[]{:S(2)}) async-start(), calls=%async_computation.6 | async-start | bytes 4456448 | tf_op jit(solution)/shard_map/all_gather | solution.py:500
  43.5 20.2 %copy-start = (s32[8,128]{1,0:T(8,128)}, s32[8,128]{1,0:T(8,128)S(1)}, u32[]{:S(2)}) copy-start(s32[8,128]{1,0:T(8,128)S(1)} %get-tuple-element.10.places_ref) | copy-start | bytes 12292
  63.7 1.0 copy-start.3
  72.7 1.1 copy-start.2
  73.8 5.1 %collective-permute-start = (bf16[256,2560]{1,0:T(8,128)(2,1)}, bf16[256,2560]{1,0:T(8,128)(2,1)S(1)}, u32[]{:S(2)}, u32[]{:S(2)}) collective-permute-start(bf16[256,2560]{1,0:T(8,128)(2,1)} %copy-done.2), channel_id=1, source_target_pairs={{0,1},{1,0},{2,3},{3,2},{4,5},{5,4},{6,7},{7,6},{8,9},{9,8},{10,11... | collective-permute-start | bytes 3932168 | tf_op jit(solution)/shard_map/ppermute | solution.py:501
Sparse Core Ops, SparseCore 0:
  74.0 49.5 all-gather.1

commit v4 on v2

--- a/solution.py
+++ b/solution.py
@@ -13,8 +13,8 @@
 epsilon = 1e-05
 f32 = jnp.float32
 bf16 = jnp.bfloat16
-VMEM_LIMIT = 48 * 1024 * 1024
-VMEM_MOST = 62 * 1024 * 1024
+VMEM_LIMIT = 16 * 1024 * 1024
+VMEM_MOST = 60 * 1024 * 1024
 NT = (((1,), (1,)), ((), ()))
 TN = (((0,), (0,)), ((), ()))
 
@@ -106,13 +106,10 @@
 
 
 def backward_body(
-    rows_ref,
     cot_ref,
     valid_ref,
-    weight_ref,
     out_weight_ref,
     normed_ref,
-    inverse_ref,
     active_ref,
     slope_ref,
     weighting_ref,
@@ -121,26 +118,26 @@
     mix_inverse_ref,
     gated_ref,
     proj_cot_ref,
+    masked_ref,
+    normed_t_ref,
+    gated_t_ref,
     spread,
-    keep_ref,
     send_ref,
 ):
-    rows, width = rows_ref.shape
+    rows, width = cot_ref.shape
     head = width // HEADS
     pair = 2 * head
     place_i = lax.broadcasted_iota(jnp.int32, (rows, rows), 0)
     place_j = lax.broadcasted_iota(jnp.int32, (rows, rows), 1)
     valid_col = as_column(valid_ref[...].astype(f32), place_i == place_j)
-    masked_f = cot_ref[...].astype(f32) * valid_col
-    masked = masked_f.astype(bf16)
+    masked = (cot_ref[...].astype(f32) * valid_col).astype(bf16)
+    masked_ref[...] = masked
     side = width // 2
-
-    def put_grad(factor, cot, at):
-        grad = dot(factor, cot).astype(bf16)
-        keep_ref[:, at : at + width] = grad[:side]
-        send_ref[:, at : at + width] = grad[side:]
-
-    put_grad(permute(spread, gated_ref[...], NT), masked, 4 * width)
+    gated_t = permute(spread, gated_ref[...], NT)
+    gated_t_ref[...] = gated_t[:side]
+    send_ref[:, 4 * width :] = permute(gated_t[side:], masked)
+    normed_t = permute(spread, normed_ref[...], NT)
+    normed_t_ref[...] = normed_t[:side]
     gated_cot = dot(masked, out_weight_ref[...], NT)
     mixed = mixed_ref[...]
     gate_cot = (gated_cot * mixed).astype(bf16).astype(f32)
@@ -177,25 +174,17 @@
             score_cot = (weighting_cot * score_slope_ref[slot].astype(f32)).astype(bf16)
             put(2, dot(score_cot, stacked(key)))
             put(3, folded(dot(score_cot, query, TN)))
-    normed_t = permute(spread, normed_ref[...], NT)
-    normed_cot = jnp.zeros((rows, width), f32)
     for quarter in range(4):
         columns = slice(quarter * width, (quarter + 1) * width)
-        proj_cot = proj_cot_ref[:, columns]
-        put_grad(normed_t, proj_cot, quarter * width)
-        normed_cot += dot(proj_cot, weight_ref[:, columns], NT)
-    features = rows_ref[...].astype(f32)
-    inverse = inverse_ref[...]
-    normed_f = (features - jnp.mean(features, axis=-1, keepdims=True)) * inverse
-    rows_cot = row_norm_back(normed_cot, normed_f, inverse)
-    return (masked_f + rows_cot).astype(bf16)
+        send_ref[:, columns] = permute(normed_t[side:], proj_cot_ref[:, columns])
 
 
 def permute(order, block, dims=(((1,), (0,)), ((), ()))):
     return dot(order, block, dims).astype(bf16)
 
 
-def pack_kernel(lanes, dest_ref, rows_hbm, cot_hbm, out_ref, rows_ref, cot_ref, sems):
+def pack_kernel(lanes, dest_ref, me_ref, own_x_ref, rows_hbm, cot_hbm, out_ref, rows_ref, cot_ref, sems):
+    del me_ref, own_x_ref
     copies = [
         pltpu.make_async_copy(rows_hbm, rows_ref, sems.at[0]),
         pltpu.make_async_copy(cot_hbm, cot_ref, sems.at[1]),
@@ -242,6 +231,14 @@
     out_ref[...] = permute(order, in_ref[:, :double], TN)
 
 
+def slots_of(sources_ref, offsets_ref):
+    blocks = sources_ref.shape[1]
+    keys = [sources_ref[0, t] * 2 + offsets_ref[0, t] for t in range(blocks)]
+    return [
+        sum(jnp.where(keys[u] < keys[t], 1, 0) for u in range(blocks) if u != t) for t in range(blocks)
+    ]
+
+
 def gather_order(lanes, sources_ref, offsets_ref, order_ref):
     rows = order_ref.shape[0]
     blocks = sources_ref.shape[1]
@@ -251,14 +248,12 @@
     inside = lax.broadcasted_iota(jnp.int32, (span, rows), 0)
     column = lax.broadcasted_iota(jnp.int32, (span, rows), 1)
     base = inside % lanes * chunk + inside // lanes % half * blocks
-    keys = [sources_ref[0, t] * 2 + offsets_ref[0, t] for t in range(blocks)]
-    for t in range(blocks):
-        slot = sum(jnp.where(keys[u] < keys[t], 1, 0) for u in range(blocks) if u != t)
+    for t, slot in enumerate(slots_of(sources_ref, offsets_ref)):
         order = jnp.where(column == base + slot, 1.0, 0.0)
         order_ref[t * span : (t + 1) * span, :] = order.astype(bf16)
 
 
-def spread_order(parts, core, width):
+def spread_order(parts, core, own_x, width):
     xs, ys = parts
     out = lax.broadcasted_iota(jnp.int32, (width, width), 0)
     column = lax.broadcasted_iota(jnp.int32, (width, width), 1)
@@ -266,7 +261,7 @@
     block = width // ys // 2
     piece = block // xs
     y = out // piece % ys
-    x = out % side // (piece * ys)
+    x = (out % side // (piece * ys) + own_x) % xs
     parity = (out // side + core) % 2
     source = y * (2 * block) + parity * block + x * piece + out % piece
     return jnp.where(source == column, 1.0, 0.0).astype(bf16)
@@ -275,7 +270,8 @@
 def layer_kernel(
     lanes,
     parts,
-    core_ref,
+    me_ref,
+    own_x_ref,
     sources_ref,
     offsets_ref,
     in_ref,
@@ -283,14 +279,16 @@
     valid_ref,
     weight_ref,
     out_weight_ref,
-    leave_ref,
-    keep_ref,
     send_ref,
+    proj_cot_ref,
+    normed_t_ref,
+    gated_t_ref,
+    masked_ref,
+    rows_ref,
+    inverse_ref,
     order_ref,
-    rows_ref,
     cot_ref,
     normed_ref,
-    inverse_ref,
     active_ref,
     slope_ref,
     weighting_ref,
@@ -298,15 +296,12 @@
     mixed_ref,
     mix_inverse_ref,
     gated_ref,
-    proj_cot_ref,
 ):
-    rows, width = rows_ref.shape
+    width = rows_ref.shape[1]
     gather_order(lanes, sources_ref, offsets_ref, order_ref)
     rows_ref[...] = permute(order_ref[...], in_ref[:, :width])
     cot_ref[...] = permute(order_ref[...], in_ref[:, width:])
     stored = (
-        normed_ref,
-        inverse_ref,
         active_ref,
         slope_ref,
         weighting_ref,
@@ -315,50 +310,118 @@
         mix_inverse_ref,
         gated_ref,
     )
-    forward_body(rows_ref, seg_ref, valid_ref, weight_ref, *stored)
-    spread = spread_order(parts, core_ref[0], width)
-    work_grad = backward_body(
-        rows_ref,
+    forward_body(rows_ref, seg_ref, valid_ref, weight_ref, normed_ref, inverse_ref, *stored)
+    backward_body(
         cot_ref,
         valid_ref,
-        weight_ref,
         out_weight_ref,
+        normed_ref,
         *stored,
         proj_cot_ref,
-        spread,
-        keep_ref,
+        masked_ref,
+        normed_t_ref,
+        gated_t_ref,
+        spread_order(parts, me_ref[0] % 2, own_x_ref[0], width),
         send_ref,
     )
+
+
+def finish_kernel(
+    weight_ref,
+    proj_cot_ref,
+    normed_t_ref,
+    gated_t_ref,
+    masked_ref,
+    rows_ref,
+    inverse_ref,
+    order_ref,
+    leave_ref,
+    *keep_refs,
+):
+    rows, width = rows_ref.shape
+
+    def put(grad, columns):
+        size = keep_refs[0].shape[0]
+        for k, keep_ref in enumerate(keep_refs):
+            keep_ref[:, columns] = grad[k * size : (k + 1) * size]
+
+    normed_cot = jnp.zeros((rows, width), f32)
+    for quarter in range(4):
+        columns = slice(quarter * width, (quarter + 1) * width)
+        proj_cot = proj_cot_ref[:, columns]
+        normed_cot += dot(proj_cot, weight_ref[:, columns], NT)
+        put(permute(normed_t_ref[...], proj_cot), columns)
+    masked = masked_ref[...]
+    put(permute(gated_t_ref[...], masked), slice(4 * width, 5 * width))
+    features = rows_ref[...].astype(f32)
+    inverse = inverse_ref[...]
+    normed_f = (features - jnp.mean(features, axis=-1, keepdims=True)) * inverse
+    rows_cot = row_norm_back(normed_cot, normed_f, inverse)
+    work_grad = (masked.astype(f32) + rows_cot).astype(bf16)
     leave_ref[...] = permute(order_ref[...], work_grad, TN)
 
 
-def return_kernel(order_ref, in_ref, out_ref):
-    out_ref[...] = permute(order_ref[...], in_ref[...])
-
-
-def unpack_kernel(lanes, blocks, in_ref, partial_ref, out_ref, same_partial_ref):
-    del partial_ref, same_partial_ref
-    rows = in_ref.shape[0]
-    chunk = rows // lanes
-    half = chunk // blocks
-    loaded = lax.broadcasted_iota(jnp.int32, (rows, rows), 0)
-    place = lax.broadcasted_iota(jnp.int32, (rows, rows), 1)
-    source = place % blocks * (rows // blocks) + place // blocks % half * lanes + place // chunk
-    order = jnp.where(source == loaded, 1.0, 0.0).astype(bf16)
-    out_ref[...] = permute(order, in_ref[...])
-
-
-def fold_kernel(in_ref, out_ref):
-    pieces, _, piece = out_ref.shape
-    total = in_ref.shape[2]
-    folded = jnp.sum(in_ref[...].astype(f32), axis=0).astype(bf16)
+def add_kernel(arrived_ref, *refs):
+    keep_refs, out_refs = refs[: len(refs) // 2], refs[len(refs) // 2 :]
+    for k, out_ref in enumerate(out_refs):
+        span = slice(k * out_ref.shape[0], (k + 1) * out_ref.shape[0])
+        added = keep_refs[k][...].astype(f32) + arrived_ref[span, :].astype(f32)
+        out_ref[...] = added.astype(bf16)
+
+
+def merge_kernel(order_ref, back_ref, *refs):
+    *part_refs, out_ref = refs
+    ys, own, _ = out_ref.shape
+    total = part_refs[0].shape[1]
+    partial = sum(part_ref[...].astype(f32) for part_ref in part_refs)
+    out_ref[:, :, :total] = partial.reshape(ys, own, total).astype(bf16)
+    rows, width = back_ref.shape
+    groups = rows // (ys * own)
+    back = dot(order_ref[...], back_ref[...]).reshape(ys, groups, own, width)
+    for g in range(groups):
+        at = total + g * width
+        out_ref[:, :, at : at + width] = back[:, g].astype(bf16)
+
+
+def fold_kernel(me_ref, in_ref, out_ref, mine_ref, other_ref):
+    pieces, own, piece = out_ref.shape
+    ys = in_ref.shape[0]
+    width = mine_ref.shape[1]
+    halves = mine_ref.shape[0] // (ys * own)
+    total = in_ref.shape[2] - 2 * halves * width
+    folded = jnp.sum(in_ref[:, :, :total].astype(f32), axis=0).astype(bf16)
     for k in range(pieces):
         at, end = k * piece, min((k + 1) * piece, total)
         if at < total:
             out_ref[k, :, : end - at] = folded[:, at:end]
         if end - at < piece:
             rest = max(end - at, 0)
-            out_ref[k, :, rest:] = jnp.zeros((out_ref.shape[1], piece - rest), bf16)
+            out_ref[k, :, rest:] = jnp.zeros((own, piece - rest), bf16)
+    first = me_ref[0] % 2 == 0
+    for r in range(halves):
+        span = slice(r * ys * own, (r + 1) * ys * own)
+        sets = []
+        for g in (r, halves + r):
+            at = total + g * width
+            sets.append(in_ref[:, :, at : at + width].astype(f32).reshape(ys * own, width))
+        mine_ref[span, :] = jnp.where(first, sets[0], sets[1]).astype(bf16)
+        other_ref[span, :] = jnp.where(first, sets[1], sets[0]).astype(bf16)
+
+
+def unpack_kernel(lanes, blocks, me_ref, mine_ref, arrived_ref, out_ref, token_ref):
+    token_ref[...] = jnp.zeros_like(token_ref)
+    rows = out_ref.shape[0]
+    side = rows // 2
+    out = lax.broadcasted_iota(jnp.int32, (rows, rows), 0)
+    column = lax.broadcasted_iota(jnp.int32, (rows, rows), 1)
+    block = out // (rows // blocks)
+    half = out // lanes % (rows // blocks // lanes)
+    piece = out % lanes
+    place = half * (blocks * lanes // 2) + piece // 2 * blocks + block
+    place += (piece + me_ref[0]) % 2 * side
+    order = jnp.where(place == column, 1.0, 0.0).astype(bf16)
+    got = dot(order[:, :side], mine_ref[...]) + dot(order[:, side:], arrived_ref[...])
+    out_ref[...] = got.astype(bf16)
 
 
 def total_kernel(scaling, in_ref, out_ref):
@@ -366,7 +429,8 @@
     out_ref[...] = jnp.broadcast_to(total.astype(bf16), out_ref.shape)
 
 
-def result_kernel(in_ref, joined_ref, output_ref):
+def result_kernel(in_ref, after_ref, joined_ref, output_ref):
+    del after_ref
     xs, zs, piece_rows, piece = in_ref.shape
     split = joined_ref.shape[1]
     step = math.gcd(piece, split)
@@ -385,15 +449,14 @@
     smem = pl.BlockSpec(memory_space=pltpu.SMEM)
     vmem = pl.BlockSpec(memory_space=pltpu.VMEM)
     stay = pl.BlockSpec(memory_space=pl.ANY)
-    aliases = aliases or {}
     blocked = len(operands) - scalars - unmoved
     return pl.pallas_call(
         kernel,
         out_shape=tuple(out_shape),
         in_specs=[smem] * scalars + [vmem] * blocked + [stay] * unmoved,
-        out_specs=tuple(stay if k in aliases.values() else vmem for k in range(len(out_shape))),
-        input_output_aliases=aliases,
+        out_specs=tuple(vmem for _ in out_shape),
         scratch_shapes=list(scratch),
+        input_output_aliases=aliases or {},
         compiler_params=pltpu.CompilerParams(vmem_limit_bytes=VMEM_MOST if unmoved else VMEM_LIMIT),
         cost_estimate=pl.CostEstimate(flops=flops, bytes_accessed=moved, transcendentals=0),
         name=name,
@@ -416,7 +479,8 @@
     lanes = ys * lax.axis_size("c")
     rows, width = history_rows.shape
     blocks = dest_device.shape[1]
-    core = lax.axis_index("c").astype(jnp.int32).reshape(1)
+    me = lax.axis_index(("y", "c")).astype(jnp.int32).reshape(1)
+    own_x = lax.axis_index("x").astype(jnp.int32).reshape(1)
     scaling = 1.0 / math.sqrt(rows * lanes * xs * zs)
 
     def exchange(block):
@@ -428,9 +492,9 @@
         functools.partial(pack_kernel, lanes),
         "pack",
         [shape((rows, 2 * width + 128), bf16)],
-        (dest_device, history_rows, cotangent),
+        (dest_device, me, own_x, history_rows, cotangent),
         2 * square,
-        1,
+        3,
         (
             pltpu.VMEM((rows, width), bf16),
             pltpu.VMEM((rows, width), bf16),
@@ -448,12 +512,23 @@
     slots = rows // WIN * HEADS // 2
     total = width * 5
     vmem = pltpu.VMEM
-    leaving, keep, send = call(
+    side = width // 2
+    send, *stored = call(
         functools.partial(layer_kernel, lanes, (xs, ys)),
         "layer",
-        [shape((rows, width), bf16), shape((width // 2, total), bf16), shape((width // 2, total), bf16)],
+        [
+            shape((side, total), bf16),
+            shape((rows, 4 * width), bf16),
+            shape((side, rows), bf16),
+            shape((side, rows), bf16),
+            shape((rows, width), bf16),
+            shape((rows, width), bf16),
+            shape((rows, 1), f32),
+            shape((rows, rows), bf16),
+        ],
         (
-            core,
+            me,
+            own_x,
             source_device,
             source_offset,
             exchange(routed),
@@ -462,14 +537,11 @@
             joined_weight,
             output_weight,
         ),
-        2 * rows * width * width * 18,
-        3,
+        2 * rows * width * width * 10,
+        4,
         (
-            vmem((rows, rows), bf16),
             vmem((rows, width), bf16),
             vmem((rows, width), bf16),
-            vmem((rows, width), bf16),
-            vmem((rows, 1), f32),
             vmem((rows, 4 * width), bf16),
             vmem((rows, 4 * width), bf16),
             vmem((slots, WIN, 2 * WIN), bf16),
@@ -477,31 +549,51 @@
             vmem((rows, width), f32),
             vmem((rows, 1), f32),
             vmem((rows, width), bf16),
-            vmem((rows, 4 * width), bf16),
         ),
     )
-    arrived = lax.ppermute(send, "c", [(0, 1), (1, 0)])
-    summed = (keep.astype(f32) + arrived.astype(f32)).astype(bf16)
-    summed, leaving = lax.optimization_barrier((summed, leaving))
-    partial = lax.psum_scatter(summed, "x", scatter_dimension=0, tiled=True)
-
-    (returning,) = call(
-        return_kernel, "back", [shape((rows, width), bf16)], (route, exchange(leaving)), square
-    )
-    row_grad, partial = call(
+    own = width // (lanes * xs)
+    quarters = [shape((ys * own, total), bf16)] * xs
+    leaving, *keep = call(
+        finish_kernel,
+        "finish",
+        [shape((rows, width), bf16)] + quarters,
+        (joined_weight, *stored),
+        2 * rows * width * width * 8,
+    )
+    swap = [(0, 1), (1, 0)]
+    arrived = lax.ppermute(send, "c", swap)
+    parts = call(
+        add_kernel, "add", quarters, (arrived, *keep), aliases={k + 1: k for k in range(xs)}
+    )
+    parts = [
+        parts[k] if k == 0 else lax.ppermute(parts[k], "x", [(i, (i + k) % xs) for i in range(xs)])
+        for k in range(xs)
+    ]
+    (merged,) = call(
+        merge_kernel,
+        "merge",
+        [shape((ys, own, total + rows // (ys * own) * width), bf16)],
+        (route, exchange(leaving), *parts),
+        square,
+    )
+    merged = lax.all_to_all(merged, "y", 0, 0, tiled=True)
+    piece = -(-total // (zs * 128)) * 128
+    pieces, mine, other = call(
+        fold_kernel,
+        "fold",
+        [shape((zs, own, piece), bf16)] + [shape((rows // 2, width), bf16)] * 2,
+        (me, merged),
+        0,
+        1,
+    )
+    row_grad, token = call(
         functools.partial(unpack_kernel, lanes, blocks),
         "unpack",
-        [shape((rows, width), bf16), shape(partial.shape, bf16)],
-        (exchange(returning), partial),
+        [shape((rows, width), bf16), shape((8, 128), f32)],
+        (me, mine, lax.ppermute(other, "c", swap)),
         square,
-        unmoved=1,
-        aliases={1: 1},
-    )
-
-    own = width // (lanes * xs)
-    piece = -(-total // (zs * 128)) * 128
-    partial = lax.all_to_all(partial.reshape(ys, own, total), "y", 0, 0, tiled=True)
-    (pieces,) = call(fold_kernel, "fold", [shape((zs, own, piece), bf16)], (partial,))
+        1,
+    )
     pieces = lax.all_to_all(pieces, "z", 0, 0, tiled=True)
     (spread,) = call(
         functools.partial(total_kernel, scaling), "total", [shape((xs * zs, own, piece), bf16)], (pieces,)
@@ -511,7 +603,7 @@
         result_kernel,
         "result",
         [shape((width // lanes, 4 * width), f32), shape((width // lanes, width), f32)],
-        (spread.reshape(xs, zs, own, piece),),
+        (spread.reshape(xs, zs, own, piece), token),
     )
     return (row_grad, joined_grad, output_grad)
 

time: 175 us -> 163 us (0.931)
  starting transfers between devices: 5.43 us -> 27.2 us
  blocking collectives: 115 us -> 94.8 us
  between operations: 14.2 us -> 0.8 us
  Pallas kernels: 14.8 us -> 17.1 us
    all_to_all x1, waiting for transfers between devices: 17.3 us -> 2.43 us  [exchange(): lax.all_to_all(chunks, ('y', 'c'), 0, 0, tiled=True).reshape(block.shape)]
    ppermute x1 -> x5, starting transfers between devices: 1.92 us -> 15.3 us  [the longest x3 8.41 us: on_device(): lax.ppermute(parts[k], 'x', [(i, (i + k) % xs) for i in range(xs)])]
    all_to_all x2 -> x1, blocking collectives: 33.9 us -> 22.6 us  [on_device(): merged = lax.all_to_all(merged, 'y', 0, 0, tiled=True)]
    all_to_all x3 -> x2, blocking collectives: 62.1 us -> 53.1 us  [exchange(): lax.all_to_all(chunks, ('y', 'c'), 0, 0, tiled=True).reshape(block.shape)]
    ppermute x1 -> x5, waiting for transfers between devices: 3 us -> 11.5 us  [the longest x3 10.6 us: on_device(): lax.ppermute(parts[k], 'x', [(i, (i + k) % xs) for i in range(xs)])]
    all_to_all x0 -> x1, starting transfers between devices: none -> 8.08 us  [on_device(): spread = lax.all_to_all(spread, ('x', 'z'), 0, 0, tiled=True)]
    all_to_all x0 -> x1, waiting for transfers between devices: none -> 5.91 us  [on_device(): spread = lax.all_to_all(spread, ('x', 'z'), 0, 0, tiled=True)]
    pallas_call x8 -> x10, Pallas kernels: 14.8 us -> 17.1 us  [call(): pl.pallas_call(kernel, out_shape=tuple(out_shape), in_specs=[smem] * scal...]
  transfers between devices with their start and end apart: 3 -> 7, of which waited for: 2 -> 5; matrix products, arithmetic and copies ran while one was open for 0% -> 0% of each run, Pallas kernels for 0% -> 3%
where the time goes in v4:
time: 163 us; the launch traced here: 160 us
  blocking collectives  94.8 us (58%)
  starting transfers between devices  27.2 us (17%)
  waiting for transfers between devices  19.9 us (12%)
  Pallas kernels  17.1 us (10%)
    all_to_all x2, blocking collectives, exchange(): lax.all_to_all(chunks, ('y', 'c'), 0, 0, tiled=True).reshape(block.shape)  53.1 us
    all_to_all x1, blocking collectives, on_device(): merged = lax.all_to_all(merged, 'y', 0, 0, tiled=True)  22.6 us
    all_to_all x1, blocking collectives, on_device(): pieces = lax.all_to_all(pieces, 'z', 0, 0, tiled=True)  19 us
    pallas_call x10, Pallas kernels, call(): pl.pallas_call(kernel, out_shape=tuple(out_shape), in_specs=[smem] * scal...  17.1 us
    ppermute x3, waiting for transfers between devices, on_device(): lax.ppermute(parts[k], 'x', [(i, (i + k) % xs) for i in range(xs)])  10.6 us
    ppermute x3, starting transfers between devices, on_device(): lax.ppermute(parts[k], 'x', [(i, (i + k) % xs) for i in range(xs)])  8.41 us
    all_to_all x1, starting transfers between devices, on_device(): spread = lax.all_to_all(spread, ('x', 'z'), 0, 0, tiled=True)  8.08 us
    all_to_all x1, waiting for transfers between devices, on_device(): spread = lax.all_to_all(spread, ('x', 'z'), 0, 0, tiled=True)  5.91 us
  transfers between devices with their start and end apart: 7, of which 5 were waited for; matrix products, arithmetic and copies ran while one was open for 0% of the time, Pallas kernels for 3%

profile of v4, /device:TPU:1, one launch (start us, length us, event | category | flops | bytes accessed | tf_op | source)
XLA Modules:
  0.0 159.8 jit_solution(1420767862742614105)
XLA Ops:
  0.6 2.9 %pack.1 = bf16[256,1152]{1,0:T(8,128)(2,1)} custom-call(s32[1,8]{1,0:T(1,128)} %dest_ref.1, s32[1]{0:T(128)} %bitcast.me_ref, s32[1]{0:T(128)} %bitcast.1.own_x_ref, bf16[256,512]{1,0:T(8,128)(2,1)} %rows_hbm.1, bf16[256,512]{1,0:T(8,128)(2,1)} %cot_hbm.1), custom_call_target="tpu_custom_call" | custom-call | flops 134217728 | bytes 1114152 | tf_op jit(solution)/shard_map/pack/pallas_call | solution.py:453
  3.6 0.0 copy-start
  3.6 0.0 copy-start.1
  3.6 0.0 copy-start.2
  3.6 0.0 copy-start.3
  3.6 0.0 copy-start.4
  3.6 0.0 copy-start.5
  3.6 33.2 %all_to_all.30 = bf16[16,16,1152]{2,1,0:T(8,128)(2,1)S(1)} all-to-all(bf16[16,16,1152]{2,1,0:T(8,128)(2,1)} %bitcast.14), channel_id=1, replica_groups=mesh['x'=4,'z'=12,'y'=8,'c'=2] {'y','c'}, dimensions={0} | all-to-all | bytes 1179648 | tf_op jit(solution)/shard_map/all_to_all | solution.py:488
  36.9 0.7 route.1
  37.5 19.9 %all_to_all.31 = bf16[16,16,1024]{2,1,0:T(8,128)(2,1)S(1)} all-to-all(bf16[16,16,1024]{2,1,0:T(8,128)(2,1)S(1)} %bitcast.13), channel_id=1, replica_groups=mesh['x'=4,'z'=12,'y'=8,'c'=2] {'y','c'}, dimensions={0} | all-to-all | bytes 1048576 | tf_op jit(solution)/shard_map/all_to_all | solution.py:488
  57.4 0.0 copy-done
  57.4 0.0 copy-done.1
  57.4 0.0 copy-done.2
  57.4 0.0 copy-done.3
  57.5 0.0 copy-done.4
  57.5 0.0 copy-done.5
  57.5 7.5 %layer.1 = (bf16[256,2560]{1,0:T(8,128)(2,1)}, bf16[256,2048]{1,0:T(8,128)(2,1)S(1)}, bf16[256,256]{1,0:T(8,128)(2,1)S(1)}, bf16[256,256]{1,0:T(8,128)(2,1)S(1)}...) custom-call(s32[1]{0:T(128)} %bitcast.me_ref, ...), custom_call_target="tpu_custom_call" | custom-call | flops 1342177280 | bytes 6425672 | tf_op jit(solution)/shard_map/layer/pallas_call | solution.py:453
  65.0 1.9 %collective-permute-start = (bf16[256,2560]{1,0:T(8,128)(2,1)}, bf16[256,2560]{1,0:T(8,128)(2,1)S(1)}, u32[]{:S(2)}, u32[]{:S(2)}) collective-permute-start(bf16[256,2560]{1,0:T(8,128)(2,1)} %get-tuple-element.39), channel_id=1, source_target_pairs={{0,1},{1,0},{2,3},{3,2},{4,5},{5,4},{6,7},{7,6},{8,9},{9,8},{10,11... | collective-permute-start | bytes 3932168 | tf_op jit(solution)/shard_map/ppermute | solution.py:564
  66.9 2.1 %finish.1 = (bf16[256,512]{1,0:T(8,128)(2,1)}, bf16[64,2560]{1,0:T(8,128)(2,1)S(1)}, bf16[64,2560]{1,0:T(8,128)(2,1)S(1)}, bf16[64,2560]{1,0:T(8,128)(2,1)S(1)}, bf16[64,2560]{1,0:T(8,128)(2,1)S(1)}) custom-call(bf16[512,2048]{1,0:T(8,128)(2,1)S(1)} %copy-done, bf16[256,2048]{1,0:T(8,128)(2,1)S(1)} %get-tuple-element.31.proj_cot_ref, ...), custom_call_target="tpu_custom_call" | custom-call | flops 1073741824 | bytes 5637120 | tf_op jit(solution)/shard_map/finish/pallas_call | solution.py:453
  69.0 3.8 %all-to-all-start.2 = ((bf16[16,16,512]{2,1,0:T(8,128)(2,1)}), bf16[16,16,512]{2,1,0:T(8,128)(2,1)S(1)}, u32[]{:S(2)}, u32[]{:S(2)}) async-start(bf16[16,16,512]{2,1,0:T(8,128)(2,1)} %bitcast.6), calls=%async_computation.2 | async-start | bytes 524288 | tf_op jit(solution)/shard_map/all_to_all | solution.py:488
  72.8 0.0 collective-permute-done.arrived_ref
  72.8 1.0 add.5
  73.8 1.9 %collective-permute-start.1 = (bf16[64,2560]{1,0:T(8,128)(2,1)S(1)}, bf16[64,2560]{1,0:T(8,128)(2,1)S(1)}, u32[]{:S(2)}, u32[]{:S(2)}) collective-permute-start(bf16[64,2560]{1,0:T(8,128)(2,1)S(1)} %get-tuple-element.45), channel_id=1, source_target_pairs={{0,192},{192,384},{384,576},{576,0},{1,193},{193,385},{385,577},{5... | collective-permute-start | bytes 983048 | tf_op jit(solution)/shard_map/ppermute | solution.py:569
  75.7 1.9 %collective-permute-start.2 = (bf16[64,2560]{1,0:T(8,128)(2,1)S(1)}, bf16[64,2560]{1,0:T(8,128)(2,1)S(1)}, u32[]{:S(2)}, u32[]{:S(2)}) collective-permute-start(bf16[64,2560]{1,0:T(8,128)(2,1)S(1)} %get-tuple-element.46), channel_id=1, source_target_pairs={{0,384},{192,576},{384,0},{576,192},{1,385},{193,577},{385,1},{577... | collective-permute-start | bytes 983048 | tf_op jit(solution)/shard_map/ppermute | solution.py:569
  77.6 4.6 %collective-permute-start.3 = (bf16[64,2560]{1,0:T(8,128)(2,1)S(1)}, bf16[64,2560]{1,0:T(8,128)(2,1)S(1)}, u32[]{:S(2)}, u32[]{:S(2)}) collective-permute-start(bf16[64,2560]{1,0:T(8,128)(2,1)S(1)} %get-tuple-element.47), channel_id=1, source_target_pairs={{0,576},{192,0},{384,192},{576,384},{1,577},{193,1},{385,193},{577... | collective-permute-start | bytes 983048 | tf_op jit(solution)/shard_map/ppermute | solution.py:569
  82.2 2.4 %all-to-all-done.2 = bf16[16,16,512]{2,1,0:T(8,128)(2,1)S(1)} async-done(((bf16[16,16,512]{2,1,0:T(8,128)(2,1)}), bf16[16,16,512]{2,1,0:T(8,128)(2,1)S(1)}, u32[]{:S(2)}, u32[]{:S(2)}) %all-to-all-start.2) | async-done | bytes 262176 | tf_op jit(solution)/shard_map/all_to_all | solution.py:488
  84.6 8.3 %collective-permute-done.1.refs_1_ = bf16[64,2560]{1,0:T(8,128)(2,1)S(1)} collective-permute-done((bf16[64,2560]{1,0:T(8,128)(2,1)S(1)}, bf16[64,2560]{1,0:T(8,128)(2,1)S(1)}, u32[]{:S(2)}, u32[]{:S(2)}) %collective-permute-start.1) | collective-permute-done | bytes 327712 | tf_op jit(solution)/shard_map/ppermute | solution.py:569
  93.0 0.0 collective-permute-done.2.refs_2_
  93.0 2.2 %collective-permute-done.3.refs_3_ = bf16[64,2560]{1,0:T(8,128)(2,1)S(1)} collective-permute-done((bf16[64,2560]{1,0:T(8,128)(2,1)S(1)}, bf16[64,2560]{1,0:T(8,128)(2,1)S(1)}, u32[]{:S(2)}, u32[]{:S(2)}) %collective-permute-start.3) | collective-permute-done | bytes 327712 | tf_op jit(solution)/shard_map/ppermute | solution.py:569
  95.2 0.4 merge.1
  95.6 22.6 %all_to_all.32.in_ref = bf16[8,8,4608]{2,1,0:T(8,128)(2,1)S(1)} all-to-all(bf16[8,8,4608]{2,1,0:T(8,128)(2,1)S(1)} %merge.1), channel_id=1, replica_groups=mesh['x'=4,'z'=12,'y'=8,'c'=2] {'y'}, dimensions={0} | all-to-all | bytes 1179648 | tf_op jit(solution)/shard_map/all_to_all | solution.py:579
  118.2 0.1 fold.1
  118.3 19.0 %all_to_all.33.in_ref = bf16[12,8,256]{2,1,0:T(8,128)(2,1)S(1)} all-to-all(bf16[12,8,256]{2,1,0:T(8,128)(2,1)S(1)} %get-tuple-element.51), channel_id=1, replica_groups=mesh['x'=4,'z'=12,'y'=8,'c'=2] {'z'}, dimensions={0} | all-to-all | bytes 98304 | tf_op jit(solution)/shard_map/all_to_all | solution.py:597
  137.3 0.7 total.1
  138.1 8.1 %all-to-all-start.5 = ((bf16[48,8,256]{2,1,0:T(8,128)(2,1)}), bf16[48,8,256]{2,1,0:T(8,128)(2,1)S(1)}, u32[]{:S(2)}, u32[]{:S(2)}) async-start(bf16[48,8,256]{2,1,0:T(8,128)(2,1)} %total.1), calls=%async_computation.5 | async-start | bytes 393216 | tf_op jit(solution)/shard_map/all_to_all | solution.py:601
  146.1 5.0 %collective-permute-start.4 = (bf16[128,512]{1,0:T(8,128)(2,1)S(1)}, bf16[128,512]{1,0:T(8,128)(2,1)S(1)}, u32[]{:S(2)}, u32[]{:S(2)}) collective-permute-start(bf16[128,512]{1,0:T(8,128)(2,1)S(1)} %get-tuple-element.49), channel_id=1, source_target_pairs={{0,1},{1,0},{2,3},{3,2},{4,5},{5,4},{6,7},{7,6},{8,9},{9,8},{10,11... | collective-permute-start | bytes 393224 | tf_op jit(solution)/shard_map/ppermute | solution.py:593
  151.1 1.0 collective-permute-done.4.arrived_ref
  152.1 1.0 unpack.1
  153.1 5.9 %all-to-all-done.5 = bf16[48,8,256]{2,1,0:T(8,128)(2,1)S(1)} async-done(((bf16[48,8,256]{2,1,0:T(8,128)(2,1)}), bf16[48,8,256]{2,1,0:T(8,128)(2,1)S(1)}, u32[]{:S(2)}, u32[]{:S(2)}) %all-to-all-start.5) | async-done | bytes 196640 | tf_op jit(solution)/shard_map/all_to_all | solution.py:601
  159.0 0.7 result.1
Async XLA Ops:
  3.6 53.9 %copy-start = (bf16[512,2048]{1,0:T(8,128)(2,1)S(1)}, bf16[512,2048]{1,0:T(8,128)(2,1)}, u32[]{:S(2)}) copy-start(bf16[512,2048]{1,0:T(8,128)(2,1)} %weight_ref.3) | copy-start | bytes 6291460
  3.6 53.9 %copy-start.1 = (bf16[512,512]{1,0:T(8,128)(2,1)S(1)}, bf16[512,512]{1,0:T(8,128)(2,1)}, u32[]{:S(2)}) copy-start(bf16[512,512]{1,0:T(8,128)(2,1)} %out_weight_ref.1) | copy-start | bytes 1572868
  3.6 53.9 %copy-start.2 = (s32[1,256]{1,0:T(1,128)S(1)}, s32[1,256]{1,0:T(1,128)}, u32[]{:S(2)}) copy-start(s32[1,256]{1,0:T(1,128)} %seg_ref.1) | copy-start | bytes 3076
  3.6 53.8 %copy-start.3 = (s32[1,256]{1,0:T(1,128)S(1)}, s32[1,256]{1,0:T(1,128)}, u32[]{:S(2)}) copy-start(s32[1,256]{1,0:T(1,128)} %valid_ref.1) | copy-start | bytes 3076
  3.6 53.8 %copy-start.4 = (s32[1,8]{1,0:T(1,128)S(1)}, s32[1,8]{1,0:T(1,128)}, u32[]{:S(2)}) copy-start(s32[1,8]{1,0:T(1,128)} %sources_ref.1) | copy-start | bytes 100
  3.6 53.8 %copy-start.5 = (s32[1,8]{1,0:T(1,128)S(1)}, s32[1,8]{1,0:T(1,128)}, u32[]{:S(2)}) copy-start(s32[1,8]{1,0:T(1,128)} %offsets_ref.1) | copy-start | bytes 100
  65.0 7.8 %collective-permute-start = (bf16[256,2560]{1,0:T(8,128)(2,1)}, bf16[256,2560]{1,0:T(8,128)(2,1)S(1)}, u32[]{:S(2)}, u32[]{:S(2)}) collective-permute-start(bf16[256,2560]{1,0:T(8,128)(2,1)} %get-tuple-element.39), channel_id=1, source_target_pairs={{0,1},{1,0},{2,3},{3,2},{4,5},{5,4},{6,7},{7,6},{8,9},{9,8},{10,11... | collective-permute-start | bytes 3932168 | tf_op jit(solution)/shard_map/ppermute | solution.py:564
  69.0 15.7 %all-to-all-start.2 = ((bf16[16,16,512]{2,1,0:T(8,128)(2,1)}), bf16[16,16,512]{2,1,0:T(8,128)(2,1)S(1)}, u32[]{:S(2)}, u32[]{:S(2)}) async-start(bf16[16,16,512]{2,1,0:T(8,128)(2,1)} %bitcast.6), calls=%async_computation.2 | async-start | bytes 524288 | tf_op jit(solution)/shard_map/all_to_all | solution.py:488
  73.8 19.2 %collective-permute-start.1 = (bf16[64,2560]{1,0:T(8,128)(2,1)S(1)}, bf16[64,2560]{1,0:T(8,128)(2,1)S(1)}, u32[]{:S(2)}, u32[]{:S(2)}) collective-permute-start(bf16[64,2560]{1,0:T(8,128)(2,1)S(1)} %get-tuple-element.45), channel_id=1, source_target_pairs={{0,192},{192,384},{384,576},{576,0},{1,193},{193,385},{385,577},{5... | collective-permute-start | bytes 983048 | tf_op jit(solution)/shard_map/ppermute | solution.py:569
  75.7 17.3 %collective-permute-start.2 = (bf16[64,2560]{1,0:T(8,128)(2,1)S(1)}, bf16[64,2560]{1,0:T(8,128)(2,1)S(1)}, u32[]{:S(2)}, u32[]{:S(2)}) collective-permute-start(bf16[64,2560]{1,0:T(8,128)(2,1)S(1)} %get-tuple-element.46), channel_id=1, source_target_pairs={{0,384},{192,576},{384,0},{576,192},{1,385},{193,577},{385,1},{577... | collective-permute-start | bytes 983048 | tf_op jit(solution)/shard_map/ppermute | solution.py:569
  77.6 17.6 %collective-permute-start.3 = (bf16[64,2560]{1,0:T(8,128)(2,1)S(1)}, bf16[64,2560]{1,0:T(8,128)(2,1)S(1)}, u32[]{:S(2)}, u32[]{:S(2)}) collective-permute-start(bf16[64,2560]{1,0:T(8,128)(2,1)S(1)} %get-tuple-element.47), channel_id=1, source_target_pairs={{0,576},{192,0},{384,192},{576,384},{1,577},{193,1},{385,193},{577... | collective-permute-start | bytes 983048 | tf_op jit(solution)/shard_map/ppermute | solution.py:569
  138.1 21.0 %all-to-all-start.5 = ((bf16[48,8,256]{2,1,0:T(8,128)(2,1)}), bf16[48,8,256]{2,1,0:T(8,128)(2,1)S(1)}, u32[]{:S(2)}, u32[]{:S(2)}) async-start(bf16[48,8,256]{2,1,0:T(8,128)(2,1)} %total.1), calls=%async_computation.5 | async-start | bytes 393216 | tf_op jit(solution)/shard_map/all_to_all | solution.py:601
  146.1 5.9 %collective-permute-start.4 = (bf16[128,512]{1,0:T(8,128)(2,1)S(1)}, bf16[128,512]{1,0:T(8,128)(2,1)S(1)}, u32[]{:S(2)}, u32[]{:S(2)}) collective-permute-start(bf16[128,512]{1,0:T(8,128)(2,1)S(1)} %get-tuple-element.49), channel_id=1, source_target_pairs={{0,1},{1,0},{2,3},{3,2},{4,5},{5,4},{6,7},{7,6},{8,9},{9,8},{10,11... | collective-permute-start | bytes 393224 | tf_op jit(solution)/shard_map/ppermute | solution.py:593

commit v5 on v4

--- a/solution.py
+++ b/solution.py
@@ -193,42 +193,42 @@
         copy.start()
     rows, width = rows_ref.shape
     blocks = dest_ref.shape[1]
-    chunk = rows // lanes
-    half = chunk // blocks
-    place = lax.broadcasted_iota(jnp.int32, (rows, rows), 0)
-    loaded = lax.broadcasted_iota(jnp.int32, (rows, rows), 1)
-    source = place % blocks * (rows // blocks) + place // blocks % half * lanes + place // chunk
-    order = jnp.where(source == loaded, 1.0, 0.0).astype(bf16)
-    extra = out_ref.shape[1] - 2 * width
-    block = lax.broadcasted_iota(jnp.int32, (rows, extra), 0) % blocks
-    dest = jnp.zeros((rows, extra), f32)
+    units = lanes * blocks
+    halves = rows // units
+    place = lax.broadcasted_iota(jnp.int32, (units, rows), 0)
+    loaded = lax.broadcasted_iota(jnp.int32, (units, rows), 1)
+    orders = []
+    for r in range(halves):
+        source = place % blocks * (rows // blocks) + r * lanes + place // blocks
+        orders.append(jnp.where(source == loaded, 1.0, 0.0).astype(bf16))
+    extra = out_ref.shape[1] - 2 * halves * width
+    block = lax.broadcasted_iota(jnp.int32, (units, extra), 0) % blocks
+    dest = jnp.zeros((units, extra), f32)
     for j in range(blocks):
         dest = jnp.where(block == j, dest_ref[0, j].astype(f32), dest)
-    out_ref[:, 2 * width :] = dest.astype(bf16)
-    copies[0].wait()
-    out_ref[:, :width] = permute(order, rows_ref[...])
-    copies[1].wait()
-    out_ref[:, width : 2 * width] = permute(order, cot_ref[...])
+    out_ref[:, 2 * halves * width :] = dest.astype(bf16)
+    for k, block_ref in enumerate((rows_ref, cot_ref)):
+        copies[k].wait()
+        for r in range(halves):
+            at = (2 * r + k) * width
+            out_ref[:, at : at + width] = permute(orders[r], block_ref[...])
 
 
 def route_kernel(lanes, in_ref, out_ref, order_ref):
-    rows, double = out_ref.shape
-    chunk = rows // lanes
-    blocks = chunk // 2
-    extra = in_ref.shape[1] - double
-    place = lax.broadcasted_iota(jnp.int32, (rows, rows), 0)
-    other = lax.broadcasted_iota(jnp.int32, (rows, rows), 1)
-    lane = lax.broadcasted_iota(jnp.int32, (rows, extra), 1)
-    dest = in_ref[:, double:].astype(f32)
+    units, payload = out_ref.shape
+    blocks = units // lanes
+    extra = in_ref.shape[1] - payload
+    place = lax.broadcasted_iota(jnp.int32, (units, units), 0)
+    other = lax.broadcasted_iota(jnp.int32, (units, units), 1)
+    lane = lax.broadcasted_iota(jnp.int32, (units, extra), 1)
+    dest = in_ref[:, payload:].astype(f32)
     chosen = jnp.where(dest == lane.astype(f32), 1.0, 0.0)
-    same_half = place // blocks % 2 == other // blocks % 2
-    earlier = jnp.where(same_half & (other < place), 1.0, 0.0).astype(bf16)
+    earlier = jnp.where(other < place, 1.0, 0.0).astype(bf16)
     rank = jnp.sum(dot(earlier, chosen.astype(bf16)) * chosen, axis=1, keepdims=True)
-    row = lax.broadcasted_iota(jnp.int32, (rows, 1), 0)
-    target = dest[:, :1] * chunk + (row // blocks % 2 * blocks).astype(f32) + rank
+    target = dest[:, :1] * blocks + rank
     order = jnp.where(target == other.astype(f32), 1.0, 0.0).astype(bf16)
     order_ref[...] = order
-    out_ref[...] = permute(order, in_ref[:, :double], TN)
+    out_ref[...] = permute(order, in_ref[:, :payload], TN)
 
 
 def slots_of(sources_ref, offsets_ref):
@@ -240,17 +240,13 @@
 
 
 def gather_order(lanes, sources_ref, offsets_ref, order_ref):
-    rows = order_ref.shape[0]
+    units = order_ref.shape[0]
     blocks = sources_ref.shape[1]
-    chunk = rows // lanes
-    half = chunk // blocks
-    span = rows // blocks
-    inside = lax.broadcasted_iota(jnp.int32, (span, rows), 0)
-    column = lax.broadcasted_iota(jnp.int32, (span, rows), 1)
-    base = inside % lanes * chunk + inside // lanes % half * blocks
+    inside = lax.broadcasted_iota(jnp.int32, (lanes, units), 0)
+    column = lax.broadcasted_iota(jnp.int32, (lanes, units), 1)
     for t, slot in enumerate(slots_of(sources_ref, offsets_ref)):
-        order = jnp.where(column == base + slot, 1.0, 0.0)
-        order_ref[t * span : (t + 1) * span, :] = order.astype(bf16)
+        order = jnp.where(column == inside * blocks + slot, 1.0, 0.0)
+        order_ref[t * lanes : (t + 1) * lanes, :] = order.astype(bf16)
 
 
 def spread_order(parts, core, own_x, width):
@@ -261,7 +257,7 @@
     block = width // ys // 2
     piece = block // xs
     y = out // piece % ys
-    x = (out % side // (piece * ys) + own_x) % xs
+    x = out % side // (piece * ys) ^ own_x
     parity = (out // side + core) % 2
     source = y * (2 * block) + parity * block + x * piece + out % piece
     return jnp.where(source == column, 1.0, 0.0).astype(bf16)
@@ -299,8 +295,14 @@
 ):
     width = rows_ref.shape[1]
     gather_order(lanes, sources_ref, offsets_ref, order_ref)
-    rows_ref[...] = permute(order_ref[...], in_ref[:, :width])
-    cot_ref[...] = permute(order_ref[...], in_ref[:, width:])
+    halves = in_ref.shape[1] // (2 * width)
+    for k, block_ref in enumerate((rows_ref, cot_ref)):
+        for r in range(halves):
+            at = (2 * r + k) * width
+            block = permute(order_ref[...], in_ref[:, at : at + width])
+            for t in range(order_ref.shape[0] // lanes):
+                to = (t * halves + r) * lanes
+                block_ref[to : to + lanes, :] = block[t * lanes : (t + 1) * lanes]
     stored = (
         active_ref,
         slope_ref,
@@ -327,6 +329,7 @@
 
 
 def finish_kernel(
+    lanes,
     weight_ref,
     proj_cot_ref,
     normed_t_ref,
@@ -358,7 +361,15 @@
     normed_f = (features - jnp.mean(features, axis=-1, keepdims=True)) * inverse
     rows_cot = row_norm_back(normed_cot, normed_f, inverse)
     work_grad = (masked.astype(f32) + rows_cot).astype(bf16)
-    leave_ref[...] = permute(order_ref[...], work_grad, TN)
+    units = order_ref.shape[0]
+    halves = rows // units
+    for r in range(halves):
+        parts = [
+            work_grad[(t * halves + r) * lanes : (t * halves + r + 1) * lanes]
+            for t in range(units // lanes)
+        ]
+        grad = permute(order_ref[...], jnp.concatenate(parts, axis=0), TN)
+        leave_ref[:, r * width : (r + 1) * width] = grad
 
 
 def add_kernel(arrived_ref, *refs):
@@ -375,8 +386,8 @@
     total = part_refs[0].shape[1]
     partial = sum(part_ref[...].astype(f32) for part_ref in part_refs)
     out_ref[:, :, :total] = partial.reshape(ys, own, total).astype(bf16)
-    rows, width = back_ref.shape
-    groups = rows // (ys * own)
+    units, width = back_ref.shape
+    groups = units // (ys * own)
     back = dot(order_ref[...], back_ref[...]).reshape(ys, groups, own, width)
     for g in range(groups):
         at = total + g * width
@@ -484,14 +495,16 @@
     scaling = 1.0 / math.sqrt(rows * lanes * xs * zs)
 
     def exchange(block):
-        chunks = block.reshape(lanes, rows // lanes, block.shape[1])
+        chunks = block.reshape(lanes, blocks, block.shape[1])
         return lax.all_to_all(chunks, ("y", "c"), 0, 0, tiled=True).reshape(block.shape)
 
-    square = 2 * rows * rows * width
+    units = lanes * blocks
+    halves = rows // units
+    square = 2 * rows * units * width
     (packed,) = call(
         functools.partial(pack_kernel, lanes),
         "pack",
-        [shape((rows, 2 * width + 128), bf16)],
+        [shape((units, 2 * halves * width + 128), bf16)],
         (dest_device, me, own_x, history_rows, cotangent),
         2 * square,
         3,
@@ -505,7 +518,7 @@
     routed, route = call(
         functools.partial(route_kernel, lanes),
         "route",
-        [shape((rows, 2 * width), bf16), shape((rows, rows), bf16)],
+        [shape((units, 2 * halves * width), bf16), shape((units, units), bf16)],
         (exchange(packed),),
         2 * square,
     )
@@ -524,7 +537,7 @@
             shape((rows, width), bf16),
             shape((rows, width), bf16),
             shape((rows, 1), f32),
-            shape((rows, rows), bf16),
+            shape((units, units), bf16),
         ],
         (
             me,
@@ -554,9 +567,9 @@
     own = width // (lanes * xs)
     quarters = [shape((ys * own, total), bf16)] * xs
     leaving, *keep = call(
-        finish_kernel,
+        functools.partial(finish_kernel, lanes),
         "finish",
-        [shape((rows, width), bf16)] + quarters,
+        [shape((units, halves * width), bf16)] + quarters,
         (joined_weight, *stored),
         2 * rows * width * width * 8,
     )
@@ -565,10 +578,10 @@
     parts = call(
         add_kernel, "add", quarters, (arrived, *keep), aliases={k + 1: k for k in range(xs)}
     )
-    parts = [
-        parts[k] if k == 0 else lax.ppermute(parts[k], "x", [(i, (i + k) % xs) for i in range(xs)])
-        for k in range(xs)
-    ]
+    arriving = {
+        k: lax.ppermute(parts[k], "x", [(i, i ^ k) for i in range(xs)]) for k in sorted(range(1, xs), key=lambda k: (-(k & 2), k & 1))
+    }
+    parts = [parts[0], *arriving.values()]
     (merged,) = call(
         merge_kernel,
         "merge",

time: 163 us -> 161 us (0.988)
  starting transfers between devices: 27.2 us -> 25.1 us
    all_to_all x1, blocking collectives: 22.6 us -> 24.7 us  [on_device(): merged = lax.all_to_all(merged, 'y', 0, 0, tiled=True)]
    all_to_all x1, starting transfers between devices: 8.08 us -> 6.1 us  [on_device(): spread = lax.all_to_all(spread, ('x', 'z'), 0, 0, tiled=True)]
where the time goes in v5:
time: 161 us; the launch traced here: 158 us
  blocking collectives  96 us (60%)
  starting transfers between devices  25.1 us (16%)
  waiting for transfers between devices  18.6 us (12%)
  Pallas kernels  17.1 us (11%)
    all_to_all x2, blocking collectives, exchange(): lax.all_to_all(chunks, ('y', 'c'), 0, 0, tiled=True).reshape(block.shape)  52.8 us
    all_to_all x1, blocking collectives, on_device(): merged = lax.all_to_all(merged, 'y', 0, 0, tiled=True)  24.7 us
    all_to_all x1, blocking collectives, on_device(): pieces = lax.all_to_all(pieces, 'z', 0, 0, tiled=True)  18.6 us
    pallas_call x10, Pallas kernels, call(): pl.pallas_call(kernel, out_shape=tuple(out_shape), in_specs=[smem] * scal...  17.1 us
    ppermute x3, waiting for transfers between devices, on_device(): lax.ppermute(parts[k], 'x', [(i, i ^ k) for i in range(xs)])  9.22 us
    ppermute x3, starting transfers between devices, on_device(): lax.ppermute(parts[k], 'x', [(i, i ^ k) for i in range(xs)])  8.37 us
    all_to_all x1, starting transfers between devices, on_device(): spread = lax.all_to_all(spread, ('x', 'z'), 0, 0, tiled=True)  6.1 us
    all_to_all x1, waiting for transfers between devices, on_device(): spread = lax.all_to_all(spread, ('x', 'z'), 0, 0, tiled=True)  5.97 us
  transfers between devices with their start and end apart: 7, of which 5 were waited for; matrix products, arithmetic and copies ran while one was open for 0% of the time, Pallas kernels for 3%

profile of v5, /device:TPU:1, one launch (start us, length us, event | category | flops | bytes accessed | tf_op | source)
XLA Modules:
  0.0 157.6 jit_solution(7404643212589983384)
XLA Ops:
  0.6 2.9 %pack.1 = bf16[128,2176]{1,0:T(8,128)(2,1)} custom-call(s32[1,8]{1,0:T(1,128)} %dest_ref.1, s32[1]{0:T(128)} %bitcast.me_ref, s32[1]{0:T(128)} %bitcast.1.own_x_ref, bf16[256,512]{1,0:T(8,128)(2,1)} %rows_hbm.1, bf16[256,512]{1,0:T(8,128)(2,1)} %cot_hbm.1), custom_call_target="tpu_custom_call" | custom-call | flops 67108864 | bytes 1081384 | tf_op jit(solution)/shard_map/pack/pallas_call | solution.py:464
  3.6 0.0 copy-start
  3.6 0.0 copy-start.1
  3.6 0.0 copy-start.2
  3.6 0.0 copy-start.3
  3.6 0.0 copy-start.4
  3.6 0.0 copy-start.5
  3.6 32.6 %all_to_all.30 = bf16[16,8,2176]{2,1,0:T(8,128)(2,1)S(1)} all-to-all(bf16[16,8,2176]{2,1,0:T(8,128)(2,1)} %bitcast.14), channel_id=1, replica_groups=mesh['x'=4,'z'=12,'y'=8,'c'=2] {'y','c'}, dimensions={0} | all-to-all | bytes 1114112 | tf_op jit(solution)/shard_map/all_to_all | solution.py:499
  36.2 0.6 route.1
  36.9 20.2 %all_to_all.31 = bf16[16,8,2048]{2,1,0:T(8,128)(2,1)S(1)} all-to-all(bf16[16,8,2048]{2,1,0:T(8,128)(2,1)S(1)} %bitcast.13), channel_id=1, replica_groups=mesh['x'=4,'z'=12,'y'=8,'c'=2] {'y','c'}, dimensions={0} | all-to-all | bytes 1048576 | tf_op jit(solution)/shard_map/all_to_all | solution.py:499
  57.0 0.0 copy-done
  57.0 0.0 copy-done.1
  57.0 0.0 copy-done.2
  57.1 0.0 copy-done.3
  57.1 0.0 copy-done.4
  57.1 0.0 copy-done.5
  57.1 7.5 %layer.1 = (bf16[256,2560]{1,0:T(8,128)(2,1)}, bf16[256,2048]{1,0:T(8,128)(2,1)S(1)}, bf16[256,256]{1,0:T(8,128)(2,1)S(1)}, bf16[256,256]{1,0:T(8,128)(2,1)S(1)}...) custom-call(s32[1]{0:T(128)} %bitcast.me_ref, ...), custom_call_target="tpu_custom_call" | custom-call | flops 1342177280 | bytes 6327368 | tf_op jit(solution)/shard_map/layer/pallas_call | solution.py:464
  64.5 1.9 %collective-permute-start = (bf16[256,2560]{1,0:T(8,128)(2,1)}, bf16[256,2560]{1,0:T(8,128)(2,1)S(1)}, u32[]{:S(2)}, u32[]{:S(2)}) collective-permute-start(bf16[256,2560]{1,0:T(8,128)(2,1)} %get-tuple-element.39), channel_id=1, source_target_pairs={{0,1},{1,0},{2,3},{3,2},{4,5},{5,4},{6,7},{7,6},{8,9},{9,8},{10,11... | collective-permute-start | bytes 3932168 | tf_op jit(solution)/shard_map/ppermute | solution.py:577
  66.5 2.0 %finish.1 = (bf16[128,1024]{1,0:T(8,128)(2,1)}, bf16[64,2560]{1,0:T(8,128)(2,1)S(1)}, bf16[64,2560]{1,0:T(8,128)(2,1)S(1)}, bf16[64,2560]{1,0:T(8,128)(2,1)S(1)}, bf16[64,2560]{1,0:T(8,128)(2,1)S(1)}) custom-call(bf16[512,2048]{1,0:T(8,128)(2,1)S(1)} %copy-done, bf16[256,2048]{1,0:T(8,128)(2,1)S(1)} %get-tuple-element.31.proj_cot_ref, ...), custom_call_target="tpu_custom_call" | custom-call | flops 1073741824 | bytes 5538816 | tf_op jit(solution)/shard_map/finish/pallas_call | solution.py:464
  68.5 3.8 %all-to-all-start.2 = ((bf16[16,8,1024]{2,1,0:T(8,128)(2,1)}), bf16[16,8,1024]{2,1,0:T(8,128)(2,1)S(1)}, u32[]{:S(2)}, u32[]{:S(2)}) async-start(bf16[16,8,1024]{2,1,0:T(8,128)(2,1)} %bitcast.6), calls=%async_computation.2 | async-start | bytes 524288 | tf_op jit(solution)/shard_map/all_to_all | solution.py:499
  72.3 0.0 collective-permute-done.arrived_ref
  72.3 1.0 add.5
  73.3 1.9 %collective-permute-start.1 = (bf16[64,2560]{1,0:T(8,128)(2,1)S(1)}, bf16[64,2560]{1,0:T(8,128)(2,1)S(1)}, u32[]{:S(2)}, u32[]{:S(2)}) collective-permute-start(bf16[64,2560]{1,0:T(8,128)(2,1)S(1)} %get-tuple-element.45), channel_id=1, source_target_pairs={{0,384},{192,576},{384,0},{576,192},{1,385},{193,577},{385,1},{577... | collective-permute-start | bytes 983048 | tf_op jit(solution)/shard_map/ppermute | solution.py:582
  75.2 1.9 %collective-permute-start.2 = (bf16[64,2560]{1,0:T(8,128)(2,1)S(1)}, bf16[64,2560]{1,0:T(8,128)(2,1)S(1)}, u32[]{:S(2)}, u32[]{:S(2)}) collective-permute-start(bf16[64,2560]{1,0:T(8,128)(2,1)S(1)} %get-tuple-element.46), channel_id=1, source_target_pairs={{0,576},{192,384},{384,192},{576,0},{1,577},{193,385},{385,193},{5... | collective-permute-start | bytes 983048 | tf_op jit(solution)/shard_map/ppermute | solution.py:582
  77.2 4.5 %collective-permute-start.3 = (bf16[64,2560]{1,0:T(8,128)(2,1)S(1)}, bf16[64,2560]{1,0:T(8,128)(2,1)S(1)}, u32[]{:S(2)}, u32[]{:S(2)}) collective-permute-start(bf16[64,2560]{1,0:T(8,128)(2,1)S(1)} %get-tuple-element.47), channel_id=1, source_target_pairs={{0,192},{192,0},{384,576},{576,384},{1,193},{193,1},{385,577},{577... | collective-permute-start | bytes 983048 | tf_op jit(solution)/shard_map/ppermute | solution.py:582
  81.7 2.5 %all-to-all-done.2 = bf16[16,8,1024]{2,1,0:T(8,128)(2,1)S(1)} async-done(((bf16[16,8,1024]{2,1,0:T(8,128)(2,1)}), bf16[16,8,1024]{2,1,0:T(8,128)(2,1)S(1)}, u32[]{:S(2)}, u32[]{:S(2)}) %all-to-all-start.2) | async-done | bytes 262176 | tf_op jit(solution)/shard_map/all_to_all | solution.py:499
  84.2 1.7 %collective-permute-done.1.refs_1_ = bf16[64,2560]{1,0:T(8,128)(2,1)S(1)} collective-permute-done((bf16[64,2560]{1,0:T(8,128)(2,1)S(1)}, bf16[64,2560]{1,0:T(8,128)(2,1)S(1)}, u32[]{:S(2)}, u32[]{:S(2)}) %collective-permute-start.1) | collective-permute-done | bytes 327712 | tf_op jit(solution)/shard_map/ppermute | solution.py:582
  85.8 7.6 %collective-permute-done.2.refs_2_ = bf16[64,2560]{1,0:T(8,128)(2,1)S(1)} collective-permute-done((bf16[64,2560]{1,0:T(8,128)(2,1)S(1)}, bf16[64,2560]{1,0:T(8,128)(2,1)S(1)}, u32[]{:S(2)}, u32[]{:S(2)}) %collective-permute-start.2) | collective-permute-done | bytes 327712 | tf_op jit(solution)/shard_map/ppermute | solution.py:582
  93.4 0.0 collective-permute-done.3.refs_3_
  93.4 0.5 merge.1
  93.9 24.7 %all_to_all.32.in_ref = bf16[8,8,4608]{2,1,0:T(8,128)(2,1)S(1)} all-to-all(bf16[8,8,4608]{2,1,0:T(8,128)(2,1)S(1)} %merge.1), channel_id=1, replica_groups=mesh['x'=4,'z'=12,'y'=8,'c'=2] {'y'}, dimensions={0} | all-to-all | bytes 1179648 | tf_op jit(solution)/shard_map/all_to_all | solution.py:592
  118.5 0.1 fold.1
  118.6 18.6 %all_to_all.33.in_ref = bf16[12,8,256]{2,1,0:T(8,128)(2,1)S(1)} all-to-all(bf16[12,8,256]{2,1,0:T(8,128)(2,1)S(1)} %get-tuple-element.51), channel_id=1, replica_groups=mesh['x'=4,'z'=12,'y'=8,'c'=2] {'z'}, dimensions={0} | all-to-all | bytes 98304 | tf_op jit(solution)/shard_map/all_to_all | solution.py:610
  137.2 0.7 total.1
  137.9 6.1 %all-to-all-start.5 = ((bf16[48,8,256]{2,1,0:T(8,128)(2,1)}), bf16[48,8,256]{2,1,0:T(8,128)(2,1)S(1)}, u32[]{:S(2)}, u32[]{:S(2)}) async-start(bf16[48,8,256]{2,1,0:T(8,128)(2,1)} %total.1), calls=%async_computation.5 | async-start | bytes 393216 | tf_op jit(solution)/shard_map/all_to_all | solution.py:614
  144.0 4.9 %collective-permute-start.4 = (bf16[128,512]{1,0:T(8,128)(2,1)S(1)}, bf16[128,512]{1,0:T(8,128)(2,1)S(1)}, u32[]{:S(2)}, u32[]{:S(2)}) collective-permute-start(bf16[128,512]{1,0:T(8,128)(2,1)S(1)} %get-tuple-element.49), channel_id=1, source_target_pairs={{0,1},{1,0},{2,3},{3,2},{4,5},{5,4},{6,7},{7,6},{8,9},{9,8},{10,11... | collective-permute-start | bytes 393224 | tf_op jit(solution)/shard_map/ppermute | solution.py:606
  148.9 1.0 collective-permute-done.4.arrived_ref
  149.9 1.0 unpack.1
  150.9 6.0 %all-to-all-done.5 = bf16[48,8,256]{2,1,0:T(8,128)(2,1)S(1)} async-done(((bf16[48,8,256]{2,1,0:T(8,128)(2,1)}), bf16[48,8,256]{2,1,0:T(8,128)(2,1)S(1)}, u32[]{:S(2)}, u32[]{:S(2)}) %all-to-all-start.5) | async-done | bytes 196640 | tf_op jit(solution)/shard_map/all_to_all | solution.py:614
  156.9 0.7 result.1
Async XLA Ops:
  3.6 53.5 %copy-start = (bf16[512,2048]{1,0:T(8,128)(2,1)S(1)}, bf16[512,2048]{1,0:T(8,128)(2,1)}, u32[]{:S(2)}) copy-start(bf16[512,2048]{1,0:T(8,128)(2,1)} %weight_ref.3) | copy-start | bytes 6291460
  3.6 53.5 %copy-start.1 = (bf16[512,512]{1,0:T(8,128)(2,1)S(1)}, bf16[512,512]{1,0:T(8,128)(2,1)}, u32[]{:S(2)}) copy-start(bf16[512,512]{1,0:T(8,128)(2,1)} %out_weight_ref.1) | copy-start | bytes 1572868
  3.6 53.5 %copy-start.2 = (s32[1,256]{1,0:T(1,128)S(1)}, s32[1,256]{1,0:T(1,128)}, u32[]{:S(2)}) copy-start(s32[1,256]{1,0:T(1,128)} %seg_ref.1) | copy-start | bytes 3076
  3.6 53.5 %copy-start.3 = (s32[1,256]{1,0:T(1,128)S(1)}, s32[1,256]{1,0:T(1,128)}, u32[]{:S(2)}) copy-start(s32[1,256]{1,0:T(1,128)} %valid_ref.1) | copy-start | bytes 3076
  3.6 53.5 %copy-start.4 = (s32[1,8]{1,0:T(1,128)S(1)}, s32[1,8]{1,0:T(1,128)}, u32[]{:S(2)}) copy-start(s32[1,8]{1,0:T(1,128)} %sources_ref.1) | copy-start | bytes 100
  3.6 53.5 %copy-start.5 = (s32[1,8]{1,0:T(1,128)S(1)}, s32[1,8]{1,0:T(1,128)}, u32[]{:S(2)}) copy-start(s32[1,8]{1,0:T(1,128)} %offsets_ref.1) | copy-start | bytes 100
  64.5 7.8 %collective-permute-start = (bf16[256,2560]{1,0:T(8,128)(2,1)}, bf16[256,2560]{1,0:T(8,128)(2,1)S(1)}, u32[]{:S(2)}, u32[]{:S(2)}) collective-permute-start(bf16[256,2560]{1,0:T(8,128)(2,1)} %get-tuple-element.39), channel_id=1, source_target_pairs={{0,1},{1,0},{2,3},{3,2},{4,5},{5,4},{6,7},{7,6},{8,9},{9,8},{10,11... | collective-permute-start | bytes 3932168 | tf_op jit(solution)/shard_map/ppermute | solution.py:577
  68.5 15.7 %all-to-all-start.2 = ((bf16[16,8,1024]{2,1,0:T(8,128)(2,1)}), bf16[16,8,1024]{2,1,0:T(8,128)(2,1)S(1)}, u32[]{:S(2)}, u32[]{:S(2)}) async-start(bf16[16,8,1024]{2,1,0:T(8,128)(2,1)} %bitcast.6), calls=%async_computation.2 | async-start | bytes 524288 | tf_op jit(solution)/shard_map/all_to_all | solution.py:499
  73.3 12.5 %collective-permute-start.1 = (bf16[64,2560]{1,0:T(8,128)(2,1)S(1)}, bf16[64,2560]{1,0:T(8,128)(2,1)S(1)}, u32[]{:S(2)}, u32[]{:S(2)}) collective-permute-start(bf16[64,2560]{1,0:T(8,128)(2,1)S(1)} %get-tuple-element.45), channel_id=1, source_target_pairs={{0,384},{192,576},{384,0},{576,192},{1,385},{193,577},{385,1},{577... | collective-permute-start | bytes 983048 | tf_op jit(solution)/shard_map/ppermute | solution.py:582
  75.2 18.2 %collective-permute-start.2 = (bf16[64,2560]{1,0:T(8,128)(2,1)S(1)}, bf16[64,2560]{1,0:T(8,128)(2,1)S(1)}, u32[]{:S(2)}, u32[]{:S(2)}) collective-permute-start(bf16[64,2560]{1,0:T(8,128)(2,1)S(1)} %get-tuple-element.46), channel_id=1, source_target_pairs={{0,576},{192,384},{384,192},{576,0},{1,577},{193,385},{385,193},{5... | collective-permute-start | bytes 983048 | tf_op jit(solution)/shard_map/ppermute | solution.py:582
  77.2 16.2 %collective-permute-start.3 = (bf16[64,2560]{1,0:T(8,128)(2,1)S(1)}, bf16[64,2560]{1,0:T(8,128)(2,1)S(1)}, u32[]{:S(2)}, u32[]{:S(2)}) collective-permute-start(bf16[64,2560]{1,0:T(8,128)(2,1)S(1)} %get-tuple-element.47), channel_id=1, source_target_pairs={{0,192},{192,0},{384,576},{576,384},{1,193},{193,1},{385,577},{577... | collective-permute-start | bytes 983048 | tf_op jit(solution)/shard_map/ppermute | solution.py:582
  137.9 19.0 %all-to-all-start.5 = ((bf16[48,8,256]{2,1,0:T(8,128)(2,1)}), bf16[48,8,256]{2,1,0:T(8,128)(2,1)S(1)}, u32[]{:S(2)}, u32[]{:S(2)}) async-start(bf16[48,8,256]{2,1,0:T(8,128)(2,1)} %total.1), calls=%async_computation.5 | async-start | bytes 393216 | tf_op jit(solution)/shard_map/all_to_all | solution.py:614
  144.0 5.9 %collective-permute-start.4 = (bf16[128,512]{1,0:T(8,128)(2,1)S(1)}, bf16[128,512]{1,0:T(8,128)(2,1)S(1)}, u32[]{:S(2)}, u32[]{:S(2)}) collective-permute-start(bf16[128,512]{1,0:T(8,128)(2,1)S(1)} %get-tuple-element.49), channel_id=1, source_target_pairs={{0,1},{1,0},{2,3},{3,2},{4,5},{5,4},{6,7},{7,6},{8,9},{9,8},{10,11... | collective-permute-start | bytes 393224 | tf_op jit(solution)/shard_map/ppermute | solution.py:606

commit v6 on v5

--- a/solution.py
+++ b/solution.py
@@ -84,7 +84,7 @@
         allowed = jnp.where(allowed, 1.0, 0.0)
         weights = allowed / jnp.maximum(jnp.sum(allowed, axis=1, keepdims=True), 1.0)
         weights = jnp.concatenate([weights, weights], axis=1)
-        mixture = []
+        mixture, kept = [], []
         for p in range(HEADS // 2):
             at = p * pair
             value = active_ref[span, width + at : width + at + pair]
@@ -93,12 +93,13 @@
             scores = dot(query, stacked(key), NT) * head**-0.5
             gate = jax.nn.sigmoid(scores)
             weighting = (scores * gate * weights).astype(bf16)
+            slope = gate * (1.0 + scores * (1.0 - gate)) * (weights * head**-0.5)
+            kept.append((weighting, slope.astype(bf16)))
+            mixture.append(dot(weighting, stacked(value)))
+        for p, (weighting, slope) in enumerate(kept):
             slot = window * (HEADS // 2) + p
             weighting_ref[slot] = weighting
-            score_slope_ref[slot] = (
-                gate * (1.0 + scores * (1.0 - gate)) * (weights * head**-0.5)
-            ).astype(bf16)
-            mixture.append(dot(weighting, stacked(value)))
+            score_slope_ref[slot] = slope
         mixed, mix_inverse = row_norm(jnp.concatenate(mixture, axis=1))
         mixed_ref[span, :] = mixed
         mix_inverse_ref[span, :] = mix_inverse
@@ -122,7 +123,7 @@
     normed_t_ref,
     gated_t_ref,
     spread,
-    send_ref,
+    send,
 ):
     rows, width = cot_ref.shape
     head = width // HEADS
@@ -135,13 +136,14 @@
     side = width // 2
     gated_t = permute(spread, gated_ref[...], NT)
     gated_t_ref[...] = gated_t[:side]
-    send_ref[:, 4 * width :] = permute(gated_t[side:], masked)
+    send(4, permute(gated_t[side:], masked))
     normed_t = permute(spread, normed_ref[...], NT)
     normed_t_ref[...] = normed_t[:side]
     gated_cot = dot(masked, out_weight_ref[...], NT)
     mixed = mixed_ref[...]
     gate_cot = (gated_cot * mixed).astype(bf16).astype(f32)
     proj_cot_ref[:, :width] = (gate_cot * slope_ref[:, :width].astype(f32)).astype(bf16)
+    send(0, permute(normed_t[side:], proj_cot_ref[:, :width]))
     mixture_cot = row_norm_back(
         gated_cot * active_ref[:, :width].astype(f32), mixed, mix_inverse_ref[...]
     ).astype(bf16)
@@ -156,27 +158,28 @@
 
     for window in range(rows // WIN):
         span = slice(window * WIN, (window + 1) * WIN)
+        cots = []
         for p in range(HEADS // 2):
             at = p * pair
             slot = window * (HEADS // 2) + p
-
-            def put(quarter, cot):
-                columns = slice(quarter * width + at, quarter * width + at + pair)
-                slope = slope_ref[span, columns].astype(f32)
-                proj_cot_ref[span, columns] = (cot.astype(bf16).astype(f32) * slope).astype(bf16)
-
             value = active_ref[span, width + at : width + at + pair]
             query = active_ref[span, 2 * width + at : 2 * width + at + pair]
             key = active_ref[span, 3 * width + at : 3 * width + at + pair]
             mix_cot = mixture_cot[span, at : at + pair]
-            put(1, folded(dot(weighting_ref[slot], mix_cot, TN)))
             weighting_cot = dot(mix_cot, stacked(value), NT).astype(bf16).astype(f32)
             score_cot = (weighting_cot * score_slope_ref[slot].astype(f32)).astype(bf16)
-            put(2, dot(score_cot, stacked(key)))
-            put(3, folded(dot(score_cot, query, TN)))
-    for quarter in range(4):
+            value_cot = folded(dot(weighting_ref[slot], mix_cot, TN))
+            query_cot = dot(score_cot, stacked(key))
+            key_cot = folded(dot(score_cot, query, TN))
+            for quarter, cot in ((1, value_cot), (2, query_cot), (3, key_cot)):
+                columns = slice(quarter * width + at, quarter * width + at + pair)
+                slope = slope_ref[span, columns].astype(f32)
+                cots.append((columns, (cot.astype(bf16).astype(f32) * slope).astype(bf16)))
+        for columns, cot in cots:
+            proj_cot_ref[span, columns] = cot
+    for quarter in range(1, 4):
         columns = slice(quarter * width, (quarter + 1) * width)
-        send_ref[:, columns] = permute(normed_t[side:], proj_cot_ref[:, columns])
+        send(quarter, permute(normed_t[side:], proj_cot_ref[:, columns]))
 
 
 def permute(order, block, dims=(((1,), (0,)), ((), ()))):
@@ -195,7 +198,7 @@
     blocks = dest_ref.shape[1]
     units = lanes * blocks
     halves = rows // units
-    place = lax.broadcasted_iota(jnp.int32, (units, rows), 0)
+    place = lax.broadcasted_iota(jnp.int32, (units, 1), 0)
     loaded = lax.broadcasted_iota(jnp.int32, (units, rows), 1)
     orders = []
     for r in range(halves):
@@ -242,7 +245,7 @@
 def gather_order(lanes, sources_ref, offsets_ref, order_ref):
     units = order_ref.shape[0]
     blocks = sources_ref.shape[1]
-    inside = lax.broadcasted_iota(jnp.int32, (lanes, units), 0)
+    inside = lax.broadcasted_iota(jnp.int32, (lanes, 1), 0)
     column = lax.broadcasted_iota(jnp.int32, (lanes, units), 1)
     for t, slot in enumerate(slots_of(sources_ref, offsets_ref)):
         order = jnp.where(column == inside * blocks + slot, 1.0, 0.0)
@@ -251,7 +254,7 @@
 
 def spread_order(parts, core, own_x, width):
     xs, ys = parts
-    out = lax.broadcasted_iota(jnp.int32, (width, width), 0)
+    out = lax.broadcasted_iota(jnp.int32, (width, 1), 0)
     column = lax.broadcasted_iota(jnp.int32, (width, width), 1)
     side = width // 2
     block = width // ys // 2
@@ -292,8 +295,20 @@
     mixed_ref,
     mix_inverse_ref,
     gated_ref,
+    held_ref,
+    sems,
 ):
     width = rows_ref.shape[1]
+    copies = []
+
+    def send(quarter, grad):
+        columns = slice(quarter * width, (quarter + 1) * width)
+        held_ref[:, columns] = grad
+        copies.append(
+            pltpu.make_async_copy(held_ref.at[:, columns], send_ref.at[:, columns], sems.at[quarter])
+        )
+        copies[-1].start()
+
     gather_order(lanes, sources_ref, offsets_ref, order_ref)
     halves = in_ref.shape[1] // (2 * width)
     for k, block_ref in enumerate((rows_ref, cot_ref)):
@@ -324,8 +339,10 @@
         normed_t_ref,
         gated_t_ref,
         spread_order(parts, me_ref[0] % 2, own_x_ref[0], width),
-        send_ref,
-    )
+        send,
+    )
+    for copy in copies:
+        copy.wait()
 
 
 def finish_kernel(
@@ -376,8 +393,7 @@
     keep_refs, out_refs = refs[: len(refs) // 2], refs[len(refs) // 2 :]
     for k, out_ref in enumerate(out_refs):
         span = slice(k * out_ref.shape[0], (k + 1) * out_ref.shape[0])
-        added = keep_refs[k][...].astype(f32) + arrived_ref[span, :].astype(f32)
-        out_ref[...] = added.astype(bf16)
+        out_ref[...] = keep_refs[k][...] + arrived_ref[span, :]
 
 
 def merge_kernel(order_ref, back_ref, *refs):
@@ -423,7 +439,7 @@
     token_ref[...] = jnp.zeros_like(token_ref)
     rows = out_ref.shape[0]
     side = rows // 2
-    out = lax.broadcasted_iota(jnp.int32, (rows, rows), 0)
+    out = lax.broadcasted_iota(jnp.int32, (rows, 1), 0)
     column = lax.broadcasted_iota(jnp.int32, (rows, rows), 1)
     block = out // (rows // blocks)
     half = out // lanes % (rows // blocks // lanes)
@@ -455,7 +471,7 @@
                 output_ref[span, at - split : at - split + step] = block
 
 
-def call(kernel, name, out_shape, operands, flops=0, scalars=0, scratch=(), unmoved=0, aliases=None):
+def call(kernel, name, out_shape, operands, flops=0, scalars=0, scratch=(), unmoved=0, aliases=None, loose=0):
     moved = sum(math.prod(a.shape) * a.dtype.itemsize for a in (*operands, *out_shape))
     smem = pl.BlockSpec(memory_space=pltpu.SMEM)
     vmem = pl.BlockSpec(memory_space=pltpu.VMEM)
@@ -465,7 +481,7 @@
         kernel,
         out_shape=tuple(out_shape),
         in_specs=[smem] * scalars + [vmem] * blocked + [stay] * unmoved,
-        out_specs=tuple(vmem for _ in out_shape),
+        out_specs=tuple(stay if k < loose else vmem for k in range(len(out_shape))),
         scratch_shapes=list(scratch),
         input_output_aliases=aliases or {},
         compiler_params=pltpu.CompilerParams(vmem_limit_bytes=VMEM_MOST if unmoved else VMEM_LIMIT),
@@ -562,7 +578,10 @@
             vmem((rows, width), f32),
             vmem((rows, 1), f32),
             vmem((rows, width), bf16),
+            vmem((side, total), bf16),
+            pltpu.SemaphoreType.DMA((5,)),
         ),
+        loose=1,
     )
     own = width // (lanes * xs)
     quarters = [shape((ys * own, total), bf16)] * xs

time: 161 us -> 159 us (0.988)
  transfers between devices with their start and end apart: 7 -> 7, of which waited for: 5 -> 5; matrix products, arithmetic and copies ran while one was open for 0% -> 0% of each run, Pallas kernels for 3% -> 2%
where the time goes in v6:
time: 159 us; the launch traced here: 156 us
  blocking collectives  96 us (60%)
  starting transfers between devices  25.1 us (16%)
  waiting for transfers between devices  18.6 us (12%)
  Pallas kernels  15.5 us (10%)
    all_to_all x2, blocking collectives, exchange(): lax.all_to_all(chunks, ('y', 'c'), 0, 0, tiled=True).reshape(block.shape)  52.8 us
    all_to_all x1, blocking collectives, on_device(): merged = lax.all_to_all(merged, 'y', 0, 0, tiled=True)  24.7 us
    all_to_all x1, blocking collectives, on_device(): pieces = lax.all_to_all(pieces, 'z', 0, 0, tiled=True)  18.6 us
    pallas_call x10, Pallas kernels, call(): pl.pallas_call(kernel, out_shape=tuple(out_shape), in_specs=[smem] * scal...  15.5 us
    ppermute x3, waiting for transfers between devices, on_device(): lax.ppermute(parts[k], 'x', [(i, i ^ k) for i in range(xs)])  8.46 us
    ppermute x3, starting transfers between devices, on_device(): lax.ppermute(parts[k], 'x', [(i, i ^ k) for i in range(xs)])  8.37 us
    all_to_all x1, starting transfers between devices, on_device(): spread = lax.all_to_all(spread, ('x', 'z'), 0, 0, tiled=True)  6.1 us
    all_to_all x1, waiting for transfers between devices, on_device(): spread = lax.all_to_all(spread, ('x', 'z'), 0, 0, tiled=True)  5.97 us
  transfers between devices with their start and end apart: 7, of which 5 were waited for; matrix products, arithmetic and copies ran while one was open for 0% of the time, Pallas kernels for 2%

profile of v6, /device:TPU:1, one launch (start us, length us, event | category | flops | bytes accessed | tf_op | source)
XLA Modules:
  0.0 156.0 jit_solution(15510984685952073609)
XLA Ops:
  0.6 2.9 %pack.1 = bf16[128,2176]{1,0:T(8,128)(2,1)} custom-call(s32[1,8]{1,0:T(1,128)} %dest_ref.1, s32[1]{0:T(128)} %bitcast.me_ref, s32[1]{0:T(128)} %bitcast.1.own_x_ref, bf16[256,512]{1,0:T(8,128)(2,1)} %rows_hbm.1, bf16[256,512]{1,0:T(8,128)(2,1)} %cot_hbm.1), custom_call_target="tpu_custom_call" | custom-call | flops 67108864 | bytes 1081384 | tf_op jit(solution)/shard_map/pack/pallas_call | solution.py:480
  3.6 0.0 copy-start
  3.6 0.0 copy-start.1
  3.6 0.0 copy-start.2
  3.6 0.0 copy-start.3
  3.6 0.0 copy-start.4
  3.6 0.0 copy-start.5
  3.6 32.6 %all_to_all.30 = bf16[16,8,2176]{2,1,0:T(8,128)(2,1)S(1)} all-to-all(bf16[16,8,2176]{2,1,0:T(8,128)(2,1)} %bitcast.14), channel_id=1, replica_groups=mesh['x'=4,'z'=12,'y'=8,'c'=2] {'y','c'}, dimensions={0} | all-to-all | bytes 1114112 | tf_op jit(solution)/shard_map/all_to_all | solution.py:515
  36.2 0.6 route.1
  36.9 20.2 %all_to_all.31 = bf16[16,8,2048]{2,1,0:T(8,128)(2,1)S(1)} all-to-all(bf16[16,8,2048]{2,1,0:T(8,128)(2,1)S(1)} %bitcast.13), channel_id=1, replica_groups=mesh['x'=4,'z'=12,'y'=8,'c'=2] {'y','c'}, dimensions={0} | all-to-all | bytes 1048576 | tf_op jit(solution)/shard_map/all_to_all | solution.py:515
  57.0 0.0 copy-done
  57.0 0.0 copy-done.1
  57.0 0.0 copy-done.2
  57.1 0.0 copy-done.3
  57.1 0.0 copy-done.4
  57.1 0.0 copy-done.5
  57.1 6.6 %layer.1 = (bf16[256,2560]{1,0:T(8,128)(2,1)}, bf16[256,2048]{1,0:T(8,128)(2,1)S(1)}, bf16[256,256]{1,0:T(8,128)(2,1)S(1)}, bf16[256,256]{1,0:T(8,128)(2,1)S(1)}...) custom-call(s32[1]{0:T(128)} %bitcast.me_ref, ...), custom_call_target="tpu_custom_call" | custom-call | flops 1342177280 | bytes 6327368 | tf_op jit(solution)/shard_map/layer/pallas_call | solution.py:480
  63.7 1.9 %collective-permute-start = (bf16[256,2560]{1,0:T(8,128)(2,1)}, bf16[256,2560]{1,0:T(8,128)(2,1)S(1)}, u32[]{:S(2)}, u32[]{:S(2)}) collective-permute-start(bf16[256,2560]{1,0:T(8,128)(2,1)} %get-tuple-element.39), channel_id=1, source_target_pairs={{0,1},{1,0},{2,3},{3,2},{4,5},{5,4},{6,7},{7,6},{8,9},{9,8},{10,11... | collective-permute-start | bytes 3932168 | tf_op jit(solution)/shard_map/ppermute | solution.py:596
  65.6 2.0 %finish.1 = (bf16[128,1024]{1,0:T(8,128)(2,1)}, bf16[64,2560]{1,0:T(8,128)(2,1)S(1)}, bf16[64,2560]{1,0:T(8,128)(2,1)S(1)}, bf16[64,2560]{1,0:T(8,128)(2,1)S(1)}, bf16[64,2560]{1,0:T(8,128)(2,1)S(1)}) custom-call(bf16[512,2048]{1,0:T(8,128)(2,1)S(1)} %copy-done, bf16[256,2048]{1,0:T(8,128)(2,1)S(1)} %get-tuple-element.31.proj_cot_ref, ...), custom_call_target="tpu_custom_call" | custom-call | flops 1073741824 | bytes 5538816 | tf_op jit(solution)/shard_map/finish/pallas_call | solution.py:480
  67.7 3.8 %all-to-all-start.2 = ((bf16[16,8,1024]{2,1,0:T(8,128)(2,1)}), bf16[16,8,1024]{2,1,0:T(8,128)(2,1)S(1)}, u32[]{:S(2)}, u32[]{:S(2)}) async-start(bf16[16,8,1024]{2,1,0:T(8,128)(2,1)} %bitcast.6), calls=%async_computation.2 | async-start | bytes 524288 | tf_op jit(solution)/shard_map/all_to_all | solution.py:515
  71.5 0.0 collective-permute-done.arrived_ref
  71.5 0.2 add.5
  71.7 1.9 %collective-permute-start.1 = (bf16[64,2560]{1,0:T(8,128)(2,1)S(1)}, bf16[64,2560]{1,0:T(8,128)(2,1)S(1)}, u32[]{:S(2)}, u32[]{:S(2)}) collective-permute-start(bf16[64,2560]{1,0:T(8,128)(2,1)S(1)} %get-tuple-element.45), channel_id=1, source_target_pairs={{0,384},{192,576},{384,0},{576,192},{1,385},{193,577},{385,1},{577... | collective-permute-start | bytes 983048 | tf_op jit(solution)/shard_map/ppermute | solution.py:601
  73.7 1.9 %collective-permute-start.2 = (bf16[64,2560]{1,0:T(8,128)(2,1)S(1)}, bf16[64,2560]{1,0:T(8,128)(2,1)S(1)}, u32[]{:S(2)}, u32[]{:S(2)}) collective-permute-start(bf16[64,2560]{1,0:T(8,128)(2,1)S(1)} %get-tuple-element.46), channel_id=1, source_target_pairs={{0,576},{192,384},{384,192},{576,0},{1,577},{193,385},{385,193},{5... | collective-permute-start | bytes 983048 | tf_op jit(solution)/shard_map/ppermute | solution.py:601
  75.6 4.5 %collective-permute-start.3 = (bf16[64,2560]{1,0:T(8,128)(2,1)S(1)}, bf16[64,2560]{1,0:T(8,128)(2,1)S(1)}, u32[]{:S(2)}, u32[]{:S(2)}) collective-permute-start(bf16[64,2560]{1,0:T(8,128)(2,1)S(1)} %get-tuple-element.47), channel_id=1, source_target_pairs={{0,192},{192,0},{384,576},{576,384},{1,193},{193,1},{385,577},{577... | collective-permute-start | bytes 983048 | tf_op jit(solution)/shard_map/ppermute | solution.py:601
  80.1 3.2 %all-to-all-done.2 = bf16[16,8,1024]{2,1,0:T(8,128)(2,1)S(1)} async-done(((bf16[16,8,1024]{2,1,0:T(8,128)(2,1)}), bf16[16,8,1024]{2,1,0:T(8,128)(2,1)S(1)}, u32[]{:S(2)}, u32[]{:S(2)}) %all-to-all-start.2) | async-done | bytes 262176 | tf_op jit(solution)/shard_map/all_to_all | solution.py:515
  83.4 0.9 collective-permute-done.1.refs_1_
  84.3 7.6 %collective-permute-done.2.refs_2_ = bf16[64,2560]{1,0:T(8,128)(2,1)S(1)} collective-permute-done((bf16[64,2560]{1,0:T(8,128)(2,1)S(1)}, bf16[64,2560]{1,0:T(8,128)(2,1)S(1)}, u32[]{:S(2)}, u32[]{:S(2)}) %collective-permute-start.2) | collective-permute-done | bytes 327712 | tf_op jit(solution)/shard_map/ppermute | solution.py:601
  91.8 0.0 collective-permute-done.3.refs_3_
  91.8 0.5 merge.1
  92.3 24.7 %all_to_all.32.in_ref = bf16[8,8,4608]{2,1,0:T(8,128)(2,1)S(1)} all-to-all(bf16[8,8,4608]{2,1,0:T(8,128)(2,1)S(1)} %merge.1), channel_id=1, replica_groups=mesh['x'=4,'z'=12,'y'=8,'c'=2] {'y'}, dimensions={0} | all-to-all | bytes 1179648 | tf_op jit(solution)/shard_map/all_to_all | solution.py:611
  117.0 0.1 fold.1
  117.1 18.6 %all_to_all.33.in_ref = bf16[12,8,256]{2,1,0:T(8,128)(2,1)S(1)} all-to-all(bf16[12,8,256]{2,1,0:T(8,128)(2,1)S(1)} %get-tuple-element.51), channel_id=1, replica_groups=mesh['x'=4,'z'=12,'y'=8,'c'=2] {'z'}, dimensions={0} | all-to-all | bytes 98304 | tf_op jit(solution)/shard_map/all_to_all | solution.py:629
  135.6 0.7 total.1
  136.3 6.1 %all-to-all-start.5 = ((bf16[48,8,256]{2,1,0:T(8,128)(2,1)}), bf16[48,8,256]{2,1,0:T(8,128)(2,1)S(1)}, u32[]{:S(2)}, u32[]{:S(2)}) async-start(bf16[48,8,256]{2,1,0:T(8,128)(2,1)} %total.1), calls=%async_computation.5 | async-start | bytes 393216 | tf_op jit(solution)/shard_map/all_to_all | solution.py:633
  142.4 4.9 %collective-permute-start.4 = (bf16[128,512]{1,0:T(8,128)(2,1)S(1)}, bf16[128,512]{1,0:T(8,128)(2,1)S(1)}, u32[]{:S(2)}, u32[]{:S(2)}) collective-permute-start(bf16[128,512]{1,0:T(8,128)(2,1)S(1)} %get-tuple-element.49), channel_id=1, source_target_pairs={{0,1},{1,0},{2,3},{3,2},{4,5},{5,4},{6,7},{7,6},{8,9},{9,8},{10,11... | collective-permute-start | bytes 393224 | tf_op jit(solution)/shard_map/ppermute | solution.py:625
  147.3 1.0 collective-permute-done.4.arrived_ref
  148.3 1.0 unpack.1
  149.3 6.0 %all-to-all-done.5 = bf16[48,8,256]{2,1,0:T(8,128)(2,1)S(1)} async-done(((bf16[48,8,256]{2,1,0:T(8,128)(2,1)}), bf16[48,8,256]{2,1,0:T(8,128)(2,1)S(1)}, u32[]{:S(2)}, u32[]{:S(2)}) %all-to-all-start.5) | async-done | bytes 196640 | tf_op jit(solution)/shard_map/all_to_all | solution.py:633
  155.3 0.7 result.1
Async XLA Ops:
  3.6 53.5 %copy-start = (bf16[512,2048]{1,0:T(8,128)(2,1)S(1)}, bf16[512,2048]{1,0:T(8,128)(2,1)}, u32[]{:S(2)}) copy-start(bf16[512,2048]{1,0:T(8,128)(2,1)} %weight_ref.3) | copy-start | bytes 6291460
  3.6 53.5 %copy-start.1 = (bf16[512,512]{1,0:T(8,128)(2,1)S(1)}, bf16[512,512]{1,0:T(8,128)(2,1)}, u32[]{:S(2)}) copy-start(bf16[512,512]{1,0:T(8,128)(2,1)} %out_weight_ref.1) | copy-start | bytes 1572868
  3.6 53.5 %copy-start.2 = (s32[1,256]{1,0:T(1,128)S(1)}, s32[1,256]{1,0:T(1,128)}, u32[]{:S(2)}) copy-start(s32[1,256]{1,0:T(1,128)} %seg_ref.1) | copy-start | bytes 3076
  3.6 53.5 %copy-start.3 = (s32[1,256]{1,0:T(1,128)S(1)}, s32[1,256]{1,0:T(1,128)}, u32[]{:S(2)}) copy-start(s32[1,256]{1,0:T(1,128)} %valid_ref.1) | copy-start | bytes 3076
  3.6 53.5 %copy-start.4 = (s32[1,8]{1,0:T(1,128)S(1)}, s32[1,8]{1,0:T(1,128)}, u32[]{:S(2)}) copy-start(s32[1,8]{1,0:T(1,128)} %sources_ref.1) | copy-start | bytes 100
  3.6 53.5 %copy-start.5 = (s32[1,8]{1,0:T(1,128)S(1)}, s32[1,8]{1,0:T(1,128)}, u32[]{:S(2)}) copy-start(s32[1,8]{1,0:T(1,128)} %offsets_ref.1) | copy-start | bytes 100
  63.7 7.8 %collective-permute-start = (bf16[256,2560]{1,0:T(8,128)(2,1)}, bf16[256,2560]{1,0:T(8,128)(2,1)S(1)}, u32[]{:S(2)}, u32[]{:S(2)}) collective-permute-start(bf16[256,2560]{1,0:T(8,128)(2,1)} %get-tuple-element.39), channel_id=1, source_target_pairs={{0,1},{1,0},{2,3},{3,2},{4,5},{5,4},{6,7},{7,6},{8,9},{9,8},{10,11... | collective-permute-start | bytes 3932168 | tf_op jit(solution)/shard_map/ppermute | solution.py:596
  67.7 15.7 %all-to-all-start.2 = ((bf16[16,8,1024]{2,1,0:T(8,128)(2,1)}), bf16[16,8,1024]{2,1,0:T(8,128)(2,1)S(1)}, u32[]{:S(2)}, u32[]{:S(2)}) async-start(bf16[16,8,1024]{2,1,0:T(8,128)(2,1)} %bitcast.6), calls=%async_computation.2 | async-start | bytes 524288 | tf_op jit(solution)/shard_map/all_to_all | solution.py:515
  71.7 12.5 %collective-permute-start.1 = (bf16[64,2560]{1,0:T(8,128)(2,1)S(1)}, bf16[64,2560]{1,0:T(8,128)(2,1)S(1)}, u32[]{:S(2)}, u32[]{:S(2)}) collective-permute-start(bf16[64,2560]{1,0:T(8,128)(2,1)S(1)} %get-tuple-element.45), channel_id=1, source_target_pairs={{0,384},{192,576},{384,0},{576,192},{1,385},{193,577},{385,1},{577... | collective-permute-start | bytes 983048 | tf_op jit(solution)/shard_map/ppermute | solution.py:601
  73.7 18.2 %collective-permute-start.2 = (bf16[64,2560]{1,0:T(8,128)(2,1)S(1)}, bf16[64,2560]{1,0:T(8,128)(2,1)S(1)}, u32[]{:S(2)}, u32[]{:S(2)}) collective-permute-start(bf16[64,2560]{1,0:T(8,128)(2,1)S(1)} %get-tuple-element.46), channel_id=1, source_target_pairs={{0,576},{192,384},{384,192},{576,0},{1,577},{193,385},{385,193},{5... | collective-permute-start | bytes 983048 | tf_op jit(solution)/shard_map/ppermute | solution.py:601
  75.6 16.2 %collective-permute-start.3 = (bf16[64,2560]{1,0:T(8,128)(2,1)S(1)}, bf16[64,2560]{1,0:T(8,128)(2,1)S(1)}, u32[]{:S(2)}, u32[]{:S(2)}) collective-permute-start(bf16[64,2560]{1,0:T(8,128)(2,1)S(1)} %get-tuple-element.47), channel_id=1, source_target_pairs={{0,192},{192,0},{384,576},{576,384},{1,193},{193,1},{385,577},{577... | collective-permute-start | bytes 983048 | tf_op jit(solution)/shard_map/ppermute | solution.py:601
  136.3 19.0 %all-to-all-start.5 = ((bf16[48,8,256]{2,1,0:T(8,128)(2,1)}), bf16[48,8,256]{2,1,0:T(8,128)(2,1)S(1)}, u32[]{:S(2)}, u32[]{:S(2)}) async-start(bf16[48,8,256]{2,1,0:T(8,128)(2,1)} %total.1), calls=%async_computation.5 | async-start | bytes 393216 | tf_op jit(solution)/shard_map/all_to_all | solution.py:633
  142.4 5.9 %collective-permute-start.4 = (bf16[128,512]{1,0:T(8,128)(2,1)S(1)}, bf16[128,512]{1,0:T(8,128)(2,1)S(1)}, u32[]{:S(2)}, u32[]{:S(2)}) collective-permute-start(bf16[128,512]{1,0:T(8,128)(2,1)S(1)} %get-tuple-element.49), channel_id=1, source_target_pairs={{0,1},{1,0},{2,3},{3,2},{4,5},{5,4},{6,7},{7,6},{8,9},{9,8},{10,11... | collective-permute-start | bytes 393224 | tf_op jit(solution)/shard_map/ppermute | solution.py:625

commit v7 on v6

--- a/solution.py
+++ b/solution.py
@@ -84,22 +84,24 @@
         allowed = jnp.where(allowed, 1.0, 0.0)
         weights = allowed / jnp.maximum(jnp.sum(allowed, axis=1, keepdims=True), 1.0)
         weights = jnp.concatenate([weights, weights], axis=1)
-        mixture, kept = [], []
-        for p in range(HEADS // 2):
-            at = p * pair
-            value = active_ref[span, width + at : width + at + pair]
-            query = active_ref[span, 2 * width + at : 2 * width + at + pair]
-            key = active_ref[span, 3 * width + at : 3 * width + at + pair]
-            scores = dot(query, stacked(key), NT) * head**-0.5
-            gate = jax.nn.sigmoid(scores)
-            weighting = (scores * gate * weights).astype(bf16)
-            slope = gate * (1.0 + scores * (1.0 - gate)) * (weights * head**-0.5)
-            kept.append((weighting, slope.astype(bf16)))
-            mixture.append(dot(weighting, stacked(value)))
-        for p, (weighting, slope) in enumerate(kept):
+        pairs = [slice(p * pair, (p + 1) * pair) for p in range(HEADS // 2)]
+        values, queries, keys = (
+            [active_ref[span, k * width + at.start : k * width + at.stop] for at in pairs]
+            for k in (1, 2, 3)
+        )
+        scores = [dot(query, stacked(key), NT) * head**-0.5 for query, key in zip(queries, keys)]
+        gates = [jax.nn.sigmoid(score) for score in scores]
+        weightings = [
+            (score * gate * weights).astype(bf16) for score, gate in zip(scores, gates)
+        ]
+        mixture = [
+            dot(weighting, stacked(value)) for weighting, value in zip(weightings, values)
+        ]
+        for p, (score, gate) in enumerate(zip(scores, gates)):
             slot = window * (HEADS // 2) + p
-            weighting_ref[slot] = weighting
-            score_slope_ref[slot] = slope
+            weighting_ref[slot] = weightings[p]
+            slope = gate * (1.0 + score * (1.0 - gate)) * (weights * head**-0.5)
+            score_slope_ref[slot] = slope.astype(bf16)
         mixed, mix_inverse = row_norm(jnp.concatenate(mixture, axis=1))
         mixed_ref[span, :] = mixed
         mix_inverse_ref[span, :] = mix_inverse
@@ -159,20 +161,25 @@
     for window in range(rows // WIN):
         span = slice(window * WIN, (window + 1) * WIN)
         cots = []
+        pairs = [slice(p * pair, (p + 1) * pair) for p in range(HEADS // 2)]
+        values, queries, keys = (
+            [active_ref[span, k * width + at.start : k * width + at.stop] for at in pairs]
+            for k in (1, 2, 3)
+        )
+        mix_cots = [mixture_cot[span, at] for at in pairs]
+        first = window * (HEADS // 2)
+        score_cots = []
         for p in range(HEADS // 2):
-            at = p * pair
-            slot = window * (HEADS // 2) + p
-            value = active_ref[span, width + at : width + at + pair]
-            query = active_ref[span, 2 * width + at : 2 * width + at + pair]
-            key = active_ref[span, 3 * width + at : 3 * width + at + pair]
-            mix_cot = mixture_cot[span, at : at + pair]
-            weighting_cot = dot(mix_cot, stacked(value), NT).astype(bf16).astype(f32)
-            score_cot = (weighting_cot * score_slope_ref[slot].astype(f32)).astype(bf16)
-            value_cot = folded(dot(weighting_ref[slot], mix_cot, TN))
-            query_cot = dot(score_cot, stacked(key))
-            key_cot = folded(dot(score_cot, query, TN))
-            for quarter, cot in ((1, value_cot), (2, query_cot), (3, key_cot)):
-                columns = slice(quarter * width + at, quarter * width + at + pair)
+            weighting_cot = dot(mix_cots[p], stacked(values[p]), NT).astype(bf16).astype(f32)
+            score_cots.append((weighting_cot * score_slope_ref[first + p].astype(f32)).astype(bf16))
+        value_cots = [
+            folded(dot(weighting_ref[first + p], mix_cots[p], TN)) for p in range(HEADS // 2)
+        ]
+        query_cots = [dot(score_cots[p], stacked(keys[p])) for p in range(HEADS // 2)]
+        key_cots = [folded(dot(score_cots[p], queries[p], TN)) for p in range(HEADS // 2)]
+        for quarter, parts in ((1, value_cots), (2, query_cots), (3, key_cots)):
+            for at, cot in zip(pairs, parts):
+                columns = slice(quarter * width + at.start, quarter * width + at.stop)
                 slope = slope_ref[span, columns].astype(f32)
                 cots.append((columns, (cot.astype(bf16).astype(f32) * slope).astype(bf16)))
         for columns, cot in cots:
@@ -355,9 +362,10 @@
     rows_ref,
     inverse_ref,
     order_ref,
-    leave_ref,
-    *keep_refs,
+    leave_hbm,
+    *refs,
 ):
+    *keep_refs, leave_ref, sem = refs
     rows, width = rows_ref.shape
 
     def put(grad, columns):
@@ -370,9 +378,7 @@
         columns = slice(quarter * width, (quarter + 1) * width)
         proj_cot = proj_cot_ref[:, columns]
         normed_cot += dot(proj_cot, weight_ref[:, columns], NT)
-        put(permute(normed_t_ref[...], proj_cot), columns)
     masked = masked_ref[...]
-    put(permute(gated_t_ref[...], masked), slice(4 * width, 5 * width))
     features = rows_ref[...].astype(f32)
     inverse = inverse_ref[...]
     normed_f = (features - jnp.mean(features, axis=-1, keepdims=True)) * inverse
@@ -387,6 +393,13 @@
         ]
         grad = permute(order_ref[...], jnp.concatenate(parts, axis=0), TN)
         leave_ref[:, r * width : (r + 1) * width] = grad
+    copy = pltpu.make_async_copy(leave_ref, leave_hbm, sem)
+    copy.start()
+    put(permute(gated_t_ref[...], masked), slice(4 * width, 5 * width))
+    for quarter in range(4):
+        columns = slice(quarter * width, (quarter + 1) * width)
+        put(permute(normed_t_ref[...], proj_cot_ref[:, columns]), columns)
+    copy.wait()
 
 
 def add_kernel(arrived_ref, *refs):
@@ -591,6 +604,8 @@
         [shape((units, halves * width), bf16)] + quarters,
         (joined_weight, *stored),
         2 * rows * width * width * 8,
+        scratch=(vmem((units, halves * width), bf16), pltpu.SemaphoreType.DMA(())),
+        loose=1,
     )
     swap = [(0, 1), (1, 0)]
     arrived = lax.ppermute(send, "c", swap)

time: 159 us -> 158 us (level)
  no operation moved by 1% of the time
where the time goes in v7:
time: 158 us; the launch traced here: 155 us
  blocking collectives  96.3 us (61%)
  starting transfers between devices  24.9 us (16%)
  waiting for transfers between devices  18.6 us (12%)
  Pallas kernels  14.7 us (9%)
    all_to_all x2, blocking collectives, exchange(): lax.all_to_all(chunks, ('y', 'c'), 0, 0, tiled=True).reshape(block.shape)  52.8 us
    all_to_all x1, blocking collectives, on_device(): merged = lax.all_to_all(merged, 'y', 0, 0, tiled=True)  24.7 us
    all_to_all x1, blocking collectives, on_device(): pieces = lax.all_to_all(pieces, 'z', 0, 0, tiled=True)  18.8 us
    pallas_call x10, Pallas kernels, call(): pl.pallas_call(kernel, out_shape=tuple(out_shape), in_specs=[smem] * scal...  14.7 us
    ppermute x3, waiting for transfers between devices, on_device(): lax.ppermute(parts[k], 'x', [(i, i ^ k) for i in range(xs)])  8.46 us
    ppermute x3, starting transfers between devices, on_device(): lax.ppermute(parts[k], 'x', [(i, i ^ k) for i in range(xs)])  8.37 us
    all_to_all x1, waiting for transfers between devices, on_device(): spread = lax.all_to_all(spread, ('x', 'z'), 0, 0, tiled=True)  5.97 us
    all_to_all x1, starting transfers between devices, on_device(): spread = lax.all_to_all(spread, ('x', 'z'), 0, 0, tiled=True)  5.81 us
  transfers between devices with their start and end apart: 7, of which 5 were waited for; matrix products, arithmetic and copies ran while one was open for 0% of the time, Pallas kernels for 2%

profile of v7, /device:TPU:1, one launch (start us, length us, event | category | flops | bytes accessed | tf_op | source)
XLA Modules:
  0.0 155.3 jit_solution(16456661972173803465)
XLA Ops:
  0.6 2.9 %pack.1 = bf16[128,2176]{1,0:T(8,128)(2,1)} custom-call(s32[1,8]{1,0:T(1,128)} %dest_ref.1, s32[1]{0:T(128)} %bitcast.me_ref, s32[1]{0:T(128)} %bitcast.1.own_x_ref, bf16[256,512]{1,0:T(8,128)(2,1)} %rows_hbm.1, bf16[256,512]{1,0:T(8,128)(2,1)} %cot_hbm.1), custom_call_target="tpu_custom_call" | custom-call | flops 67108864 | bytes 1081384 | tf_op jit(solution)/shard_map/pack/pallas_call | solution.py:493
  3.6 0.0 copy-start
  3.6 0.0 copy-start.1
  3.6 0.0 copy-start.2
  3.6 0.0 copy-start.3
  3.6 0.0 copy-start.4
  3.6 0.0 copy-start.5
  3.6 32.6 %all_to_all.30 = bf16[16,8,2176]{2,1,0:T(8,128)(2,1)S(1)} all-to-all(bf16[16,8,2176]{2,1,0:T(8,128)(2,1)} %bitcast.14), channel_id=1, replica_groups=mesh['x'=4,'z'=12,'y'=8,'c'=2] {'y','c'}, dimensions={0} | all-to-all | bytes 1114112 | tf_op jit(solution)/shard_map/all_to_all | solution.py:528
  36.2 0.6 route.1
  36.9 20.2 %all_to_all.31 = bf16[16,8,2048]{2,1,0:T(8,128)(2,1)S(1)} all-to-all(bf16[16,8,2048]{2,1,0:T(8,128)(2,1)S(1)} %bitcast.13), channel_id=1, replica_groups=mesh['x'=4,'z'=12,'y'=8,'c'=2] {'y','c'}, dimensions={0} | all-to-all | bytes 1048576 | tf_op jit(solution)/shard_map/all_to_all | solution.py:528
  57.0 0.0 copy-done
  57.0 0.0 copy-done.1
  57.0 0.0 copy-done.2
  57.1 0.0 copy-done.3
  57.1 0.0 copy-done.4
  57.1 0.0 copy-done.5
  57.1 6.0 %layer.1 = (bf16[256,2560]{1,0:T(8,128)(2,1)}, bf16[256,2048]{1,0:T(8,128)(2,1)S(1)}, bf16[256,256]{1,0:T(8,128)(2,1)S(1)}, bf16[256,256]{1,0:T(8,128)(2,1)S(1)}...) custom-call(s32[1]{0:T(128)} %bitcast.me_ref, ...), custom_call_target="tpu_custom_call" | custom-call | flops 1342177280 | bytes 6327368 | tf_op jit(solution)/shard_map/layer/pallas_call | solution.py:493
  63.1 1.9 %collective-permute-start = (bf16[256,2560]{1,0:T(8,128)(2,1)}, bf16[256,2560]{1,0:T(8,128)(2,1)S(1)}, u32[]{:S(2)}, u32[]{:S(2)}) collective-permute-start(bf16[256,2560]{1,0:T(8,128)(2,1)} %get-tuple-element.39), channel_id=1, source_target_pairs={{0,1},{1,0},{2,3},{3,2},{4,5},{5,4},{6,7},{7,6},{8,9},{9,8},{10,11... | collective-permute-start | bytes 3932168 | tf_op jit(solution)/shard_map/ppermute | solution.py:611
  65.1 1.8 %finish.1 = (bf16[128,1024]{1,0:T(8,128)(2,1)}, bf16[64,2560]{1,0:T(8,128)(2,1)S(1)}, bf16[64,2560]{1,0:T(8,128)(2,1)S(1)}, bf16[64,2560]{1,0:T(8,128)(2,1)S(1)}, bf16[64,2560]{1,0:T(8,128)(2,1)S(1)}) custom-call(bf16[512,2048]{1,0:T(8,128)(2,1)S(1)} %copy-done, bf16[256,2048]{1,0:T(8,128)(2,1)S(1)} %get-tuple-element.31.proj_cot_ref, ...), custom_call_target="tpu_custom_call" | custom-call | flops 1073741824 | bytes 5538816 | tf_op jit(solution)/shard_map/finish/pallas_call | solution.py:493
  66.9 3.8 %all-to-all-start.2 = ((bf16[16,8,1024]{2,1,0:T(8,128)(2,1)}), bf16[16,8,1024]{2,1,0:T(8,128)(2,1)S(1)}, u32[]{:S(2)}, u32[]{:S(2)}) async-start(bf16[16,8,1024]{2,1,0:T(8,128)(2,1)} %bitcast.6), calls=%async_computation.2 | async-start | bytes 524288 | tf_op jit(solution)/shard_map/all_to_all | solution.py:528
  70.7 0.0 collective-permute-done.arrived_ref
  70.8 0.2 add.5
  71.0 1.9 %collective-permute-start.1 = (bf16[64,2560]{1,0:T(8,128)(2,1)S(1)}, bf16[64,2560]{1,0:T(8,128)(2,1)S(1)}, u32[]{:S(2)}, u32[]{:S(2)}) collective-permute-start(bf16[64,2560]{1,0:T(8,128)(2,1)S(1)} %get-tuple-element.45), channel_id=1, source_target_pairs={{0,384},{192,576},{384,0},{576,192},{1,385},{193,577},{385,1},{577... | collective-permute-start | bytes 983048 | tf_op jit(solution)/shard_map/ppermute | solution.py:616
  72.9 1.9 %collective-permute-start.2 = (bf16[64,2560]{1,0:T(8,128)(2,1)S(1)}, bf16[64,2560]{1,0:T(8,128)(2,1)S(1)}, u32[]{:S(2)}, u32[]{:S(2)}) collective-permute-start(bf16[64,2560]{1,0:T(8,128)(2,1)S(1)} %get-tuple-element.46), channel_id=1, source_target_pairs={{0,576},{192,384},{384,192},{576,0},{1,577},{193,385},{385,193},{5... | collective-permute-start | bytes 983048 | tf_op jit(solution)/shard_map/ppermute | solution.py:616
  74.8 4.5 %collective-permute-start.3 = (bf16[64,2560]{1,0:T(8,128)(2,1)S(1)}, bf16[64,2560]{1,0:T(8,128)(2,1)S(1)}, u32[]{:S(2)}, u32[]{:S(2)}) collective-permute-start(bf16[64,2560]{1,0:T(8,128)(2,1)S(1)} %get-tuple-element.47), channel_id=1, source_target_pairs={{0,192},{192,0},{384,576},{576,384},{1,193},{193,1},{385,577},{577... | collective-permute-start | bytes 983048 | tf_op jit(solution)/shard_map/ppermute | solution.py:616
  79.4 3.2 %all-to-all-done.2 = bf16[16,8,1024]{2,1,0:T(8,128)(2,1)S(1)} async-done(((bf16[16,8,1024]{2,1,0:T(8,128)(2,1)}), bf16[16,8,1024]{2,1,0:T(8,128)(2,1)S(1)}, u32[]{:S(2)}, u32[]{:S(2)}) %all-to-all-start.2) | async-done | bytes 262176 | tf_op jit(solution)/shard_map/all_to_all | solution.py:528
  82.6 0.9 collective-permute-done.1.refs_1_
  83.5 7.6 %collective-permute-done.2.refs_2_ = bf16[64,2560]{1,0:T(8,128)(2,1)S(1)} collective-permute-done((bf16[64,2560]{1,0:T(8,128)(2,1)S(1)}, bf16[64,2560]{1,0:T(8,128)(2,1)S(1)}, u32[]{:S(2)}, u32[]{:S(2)}) %collective-permute-start.2) | collective-permute-done | bytes 327712 | tf_op jit(solution)/shard_map/ppermute | solution.py:616
  91.1 0.0 collective-permute-done.3.refs_3_
  91.1 0.5 merge.1
  91.5 24.7 %all_to_all.32.in_ref = bf16[8,8,4608]{2,1,0:T(8,128)(2,1)S(1)} all-to-all(bf16[8,8,4608]{2,1,0:T(8,128)(2,1)S(1)} %merge.1), channel_id=1, replica_groups=mesh['x'=4,'z'=12,'y'=8,'c'=2] {'y'}, dimensions={0} | all-to-all | bytes 1179648 | tf_op jit(solution)/shard_map/all_to_all | solution.py:626
  116.2 0.1 fold.1
  116.3 18.8 %all_to_all.33.in_ref = bf16[12,8,256]{2,1,0:T(8,128)(2,1)S(1)} all-to-all(bf16[12,8,256]{2,1,0:T(8,128)(2,1)S(1)} %get-tuple-element.51), channel_id=1, replica_groups=mesh['x'=4,'z'=12,'y'=8,'c'=2] {'z'}, dimensions={0} | all-to-all | bytes 98304 | tf_op jit(solution)/shard_map/all_to_all | solution.py:644
  135.1 0.7 total.1
  135.8 5.8 %all-to-all-start.5 = ((bf16[48,8,256]{2,1,0:T(8,128)(2,1)}), bf16[48,8,256]{2,1,0:T(8,128)(2,1)S(1)}, u32[]{:S(2)}, u32[]{:S(2)}) async-start(bf16[48,8,256]{2,1,0:T(8,128)(2,1)} %total.1), calls=%async_computation.5 | async-start | bytes 393216 | tf_op jit(solution)/shard_map/all_to_all | solution.py:648
  141.7 4.9 %collective-permute-start.4 = (bf16[128,512]{1,0:T(8,128)(2,1)S(1)}, bf16[128,512]{1,0:T(8,128)(2,1)S(1)}, u32[]{:S(2)}, u32[]{:S(2)}) collective-permute-start(bf16[128,512]{1,0:T(8,128)(2,1)S(1)} %get-tuple-element.49), channel_id=1, source_target_pairs={{0,1},{1,0},{2,3},{3,2},{4,5},{5,4},{6,7},{7,6},{8,9},{9,8},{10,11... | collective-permute-start | bytes 393224 | tf_op jit(solution)/shard_map/ppermute | solution.py:640
  146.6 1.0 collective-permute-done.4.arrived_ref
  147.5 1.0 unpack.1
  148.6 6.0 %all-to-all-done.5 = bf16[48,8,256]{2,1,0:T(8,128)(2,1)S(1)} async-done(((bf16[48,8,256]{2,1,0:T(8,128)(2,1)}), bf16[48,8,256]{2,1,0:T(8,128)(2,1)S(1)}, u32[]{:S(2)}, u32[]{:S(2)}) %all-to-all-start.5) | async-done | bytes 196640 | tf_op jit(solution)/shard_map/all_to_all | solution.py:648
  154.5 0.7 result.1
Async XLA Ops:
  3.6 53.5 %copy-start = (bf16[512,2048]{1,0:T(8,128)(2,1)S(1)}, bf16[512,2048]{1,0:T(8,128)(2,1)}, u32[]{:S(2)}) copy-start(bf16[512,2048]{1,0:T(8,128)(2,1)} %weight_ref.3) | copy-start | bytes 6291460
  3.6 53.5 %copy-start.1 = (bf16[512,512]{1,0:T(8,128)(2,1)S(1)}, bf16[512,512]{1,0:T(8,128)(2,1)}, u32[]{:S(2)}) copy-start(bf16[512,512]{1,0:T(8,128)(2,1)} %out_weight_ref.1) | copy-start | bytes 1572868
  3.6 53.5 %copy-start.2 = (s32[1,256]{1,0:T(1,128)S(1)}, s32[1,256]{1,0:T(1,128)}, u32[]{:S(2)}) copy-start(s32[1,256]{1,0:T(1,128)} %seg_ref.1) | copy-start | bytes 3076
  3.6 53.5 %copy-start.3 = (s32[1,256]{1,0:T(1,128)S(1)}, s32[1,256]{1,0:T(1,128)}, u32[]{:S(2)}) copy-start(s32[1,256]{1,0:T(1,128)} %valid_ref.1) | copy-start | bytes 3076
  3.6 53.5 %copy-start.4 = (s32[1,8]{1,0:T(1,128)S(1)}, s32[1,8]{1,0:T(1,128)}, u32[]{:S(2)}) copy-start(s32[1,8]{1,0:T(1,128)} %sources_ref.1) | copy-start | bytes 100
  3.6 53.5 %copy-start.5 = (s32[1,8]{1,0:T(1,128)S(1)}, s32[1,8]{1,0:T(1,128)}, u32[]{:S(2)}) copy-start(s32[1,8]{1,0:T(1,128)} %offsets_ref.1) | copy-start | bytes 100
  63.1 7.6 %collective-permute-start = (bf16[256,2560]{1,0:T(8,128)(2,1)}, bf16[256,2560]{1,0:T(8,128)(2,1)S(1)}, u32[]{:S(2)}, u32[]{:S(2)}) collective-permute-start(bf16[256,2560]{1,0:T(8,128)(2,1)} %get-tuple-element.39), channel_id=1, source_target_pairs={{0,1},{1,0},{2,3},{3,2},{4,5},{5,4},{6,7},{7,6},{8,9},{9,8},{10,11... | collective-permute-start | bytes 3932168 | tf_op jit(solution)/shard_map/ppermute | solution.py:611
  66.9 15.7 %all-to-all-start.2 = ((bf16[16,8,1024]{2,1,0:T(8,128)(2,1)}), bf16[16,8,1024]{2,1,0:T(8,128)(2,1)S(1)}, u32[]{:S(2)}, u32[]{:S(2)}) async-start(bf16[16,8,1024]{2,1,0:T(8,128)(2,1)} %bitcast.6), calls=%async_computation.2 | async-start | bytes 524288 | tf_op jit(solution)/shard_map/all_to_all | solution.py:528
  71.0 12.5 %collective-permute-start.1 = (bf16[64,2560]{1,0:T(8,128)(2,1)S(1)}, bf16[64,2560]{1,0:T(8,128)(2,1)S(1)}, u32[]{:S(2)}, u32[]{:S(2)}) collective-permute-start(bf16[64,2560]{1,0:T(8,128)(2,1)S(1)} %get-tuple-element.45), channel_id=1, source_target_pairs={{0,384},{192,576},{384,0},{576,192},{1,385},{193,577},{385,1},{577... | collective-permute-start | bytes 983048 | tf_op jit(solution)/shard_map/ppermute | solution.py:616
  72.9 18.2 %collective-permute-start.2 = (bf16[64,2560]{1,0:T(8,128)(2,1)S(1)}, bf16[64,2560]{1,0:T(8,128)(2,1)S(1)}, u32[]{:S(2)}, u32[]{:S(2)}) collective-permute-start(bf16[64,2560]{1,0:T(8,128)(2,1)S(1)} %get-tuple-element.46), channel_id=1, source_target_pairs={{0,576},{192,384},{384,192},{576,0},{1,577},{193,385},{385,193},{5... | collective-permute-start | bytes 983048 | tf_op jit(solution)/shard_map/ppermute | solution.py:616
  74.8 16.2 %collective-permute-start.3 = (bf16[64,2560]{1,0:T(8,128)(2,1)S(1)}, bf16[64,2560]{1,0:T(8,128)(2,1)S(1)}, u32[]{:S(2)}, u32[]{:S(2)}) collective-permute-start(bf16[64,2560]{1,0:T(8,128)(2,1)S(1)} %get-tuple-element.47), channel_id=1, source_target_pairs={{0,192},{192,0},{384,576},{576,384},{1,193},{193,1},{385,577},{577... | collective-permute-start | bytes 983048 | tf_op jit(solution)/shard_map/ppermute | solution.py:616
  135.8 18.7 %all-to-all-start.5 = ((bf16[48,8,256]{2,1,0:T(8,128)(2,1)}), bf16[48,8,256]{2,1,0:T(8,128)(2,1)S(1)}, u32[]{:S(2)}, u32[]{:S(2)}) async-start(bf16[48,8,256]{2,1,0:T(8,128)(2,1)} %total.1), calls=%async_computation.5 | async-start | bytes 393216 | tf_op jit(solution)/shard_map/all_to_all | solution.py:648
  141.7 5.9 %collective-permute-start.4 = (bf16[128,512]{1,0:T(8,128)(2,1)S(1)}, bf16[128,512]{1,0:T(8,128)(2,1)S(1)}, u32[]{:S(2)}, u32[]{:S(2)}) collective-permute-start(bf16[128,512]{1,0:T(8,128)(2,1)S(1)} %get-tuple-element.49), channel_id=1, source_target_pairs={{0,1},{1,0},{2,3},{3,2},{4,5},{5,4},{6,7},{7,6},{8,9},{9,8},{10,11... | collective-permute-start | bytes 393224 | tf_op jit(solution)/shard_map/ppermute | solution.py:640

commit v8 on v7

--- a/solution.py
+++ b/solution.py
@@ -125,6 +125,7 @@
     normed_t_ref,
     gated_t_ref,
     spread,
+    normed_t_early,
     send,
 ):
     rows, width = cot_ref.shape
@@ -139,7 +140,7 @@
     gated_t = permute(spread, gated_ref[...], NT)
     gated_t_ref[...] = gated_t[:side]
     send(4, permute(gated_t[side:], masked))
-    normed_t = permute(spread, normed_ref[...], NT)
+    normed_t = normed_t_early
     normed_t_ref[...] = normed_t[:side]
     gated_cot = dot(masked, out_weight_ref[...], NT)
     mixed = mixed_ref[...]
@@ -334,7 +335,9 @@
         mix_inverse_ref,
         gated_ref,
     )
+    spread = spread_order(parts, me_ref[0] % 2, own_x_ref[0], width)
     forward_body(rows_ref, seg_ref, valid_ref, weight_ref, normed_ref, inverse_ref, *stored)
+    normed_t_early = permute(spread, normed_ref[...], NT)
     backward_body(
         cot_ref,
         valid_ref,
@@ -345,7 +348,8 @@
         masked_ref,
         normed_t_ref,
         gated_t_ref,
-        spread_order(parts, me_ref[0] % 2, own_x_ref[0], width),
+        spread,
+        normed_t_early,
         send,
     )
     for copy in copies:

time: 158 us -> 158 us (level)
  no operation moved by 1% of the time
where the time goes in v8:
time: 158 us; the launch traced here: 155 us
  blocking collectives  95.9 us (61%)
  starting transfers between devices  25.2 us (16%)
  waiting for transfers between devices  18.6 us (12%)
  Pallas kernels  14.6 us (9%)
    all_to_all x2, blocking collectives, exchange(): lax.all_to_all(chunks, ('y', 'c'), 0, 0, tiled=True).reshape(block.shape)  52.8 us
    all_to_all x1, blocking collectives, on_device(): merged = lax.all_to_all(merged, 'y', 0, 0, tiled=True)  24.7 us
    all_to_all x1, blocking collectives, on_device(): pieces = lax.all_to_all(pieces, 'z', 0, 0, tiled=True)  18.5 us
    pallas_call x10, Pallas kernels, call(): pl.pallas_call(kernel, out_shape=tuple(out_shape), in_specs=[smem] * scal...  14.6 us
    ppermute x3, waiting for transfers between devices, on_device(): lax.ppermute(parts[k], 'x', [(i, i ^ k) for i in range(xs)])  8.46 us
    ppermute x3, starting transfers between devices, on_device(): lax.ppermute(parts[k], 'x', [(i, i ^ k) for i in range(xs)])  8.37 us
    all_to_all x1, starting transfers between devices, on_device(): spread = lax.all_to_all(spread, ('x', 'z'), 0, 0, tiled=True)  6.2 us
    all_to_all x1, waiting for transfers between devices, on_device(): spread = lax.all_to_all(spread, ('x', 'z'), 0, 0, tiled=True)  5.97 us
  transfers between devices with their start and end apart: 7, of which 5 were waited for; matrix products, arithmetic and copies ran while one was open for 0% of the time, Pallas kernels for 2%

profile of v8, /device:TPU:1, one launch (start us, length us, event | category | flops | bytes accessed | tf_op | source)
XLA Modules:
  0.0 155.2 jit_solution(18366329627651001136)
XLA Ops:
  0.6 2.9 %pack.1 = bf16[128,2176]{1,0:T(8,128)(2,1)} custom-call(s32[1,8]{1,0:T(1,128)} %dest_ref.1, s32[1]{0:T(128)} %bitcast.me_ref, s32[1]{0:T(128)} %bitcast.1.own_x_ref, bf16[256,512]{1,0:T(8,128)(2,1)} %rows_hbm.1, bf16[256,512]{1,0:T(8,128)(2,1)} %cot_hbm.1), custom_call_target="tpu_custom_call" | custom-call | flops 67108864 | bytes 1081384 | tf_op jit(solution)/shard_map/pack/pallas_call | solution.py:497
  3.6 0.0 copy-start
  3.6 0.0 copy-start.1
  3.6 0.0 copy-start.2
  3.6 0.0 copy-start.3
  3.6 0.0 copy-start.4
  3.6 0.0 copy-start.5
  3.6 32.6 %all_to_all.30 = bf16[16,8,2176]{2,1,0:T(8,128)(2,1)S(1)} all-to-all(bf16[16,8,2176]{2,1,0:T(8,128)(2,1)} %bitcast.14), channel_id=1, replica_groups=mesh['x'=4,'z'=12,'y'=8,'c'=2] {'y','c'}, dimensions={0} | all-to-all | bytes 1114112 | tf_op jit(solution)/shard_map/all_to_all | solution.py:532
  36.2 0.6 route.1
  36.9 20.2 %all_to_all.31 = bf16[16,8,2048]{2,1,0:T(8,128)(2,1)S(1)} all-to-all(bf16[16,8,2048]{2,1,0:T(8,128)(2,1)S(1)} %bitcast.13), channel_id=1, replica_groups=mesh['x'=4,'z'=12,'y'=8,'c'=2] {'y','c'}, dimensions={0} | all-to-all | bytes 1048576 | tf_op jit(solution)/shard_map/all_to_all | solution.py:532
  57.0 0.0 copy-done
  57.0 0.0 copy-done.1
  57.0 0.0 copy-done.2
  57.1 0.0 copy-done.3
  57.1 0.0 copy-done.4
  57.1 0.0 copy-done.5
  57.1 5.9 %layer.1 = (bf16[256,2560]{1,0:T(8,128)(2,1)}, bf16[256,2048]{1,0:T(8,128)(2,1)S(1)}, bf16[256,256]{1,0:T(8,128)(2,1)S(1)}, bf16[256,256]{1,0:T(8,128)(2,1)S(1)}...) custom-call(s32[1]{0:T(128)} %bitcast.me_ref, ...), custom_call_target="tpu_custom_call" | custom-call | flops 1342177280 | bytes 6327368 | tf_op jit(solution)/shard_map/layer/pallas_call | solution.py:497
  63.0 1.9 %collective-permute-start = (bf16[256,2560]{1,0:T(8,128)(2,1)}, bf16[256,2560]{1,0:T(8,128)(2,1)S(1)}, u32[]{:S(2)}, u32[]{:S(2)}) collective-permute-start(bf16[256,2560]{1,0:T(8,128)(2,1)} %get-tuple-element.39), channel_id=1, source_target_pairs={{0,1},{1,0},{2,3},{3,2},{4,5},{5,4},{6,7},{7,6},{8,9},{9,8},{10,11... | collective-permute-start | bytes 3932168 | tf_op jit(solution)/shard_map/ppermute | solution.py:615
  65.0 1.8 %finish.1 = (bf16[128,1024]{1,0:T(8,128)(2,1)}, bf16[64,2560]{1,0:T(8,128)(2,1)S(1)}, bf16[64,2560]{1,0:T(8,128)(2,1)S(1)}, bf16[64,2560]{1,0:T(8,128)(2,1)S(1)}, bf16[64,2560]{1,0:T(8,128)(2,1)S(1)}) custom-call(bf16[512,2048]{1,0:T(8,128)(2,1)S(1)} %copy-done, bf16[256,2048]{1,0:T(8,128)(2,1)S(1)} %get-tuple-element.31.proj_cot_ref, ...), custom_call_target="tpu_custom_call" | custom-call | flops 1073741824 | bytes 5538816 | tf_op jit(solution)/shard_map/finish/pallas_call | solution.py:497
  66.8 3.8 %all-to-all-start.2 = ((bf16[16,8,1024]{2,1,0:T(8,128)(2,1)}), bf16[16,8,1024]{2,1,0:T(8,128)(2,1)S(1)}, u32[]{:S(2)}, u32[]{:S(2)}) async-start(bf16[16,8,1024]{2,1,0:T(8,128)(2,1)} %bitcast.6), calls=%async_computation.2 | async-start | bytes 524288 | tf_op jit(solution)/shard_map/all_to_all | solution.py:532
  70.6 0.0 collective-permute-done.arrived_ref
  70.6 0.2 add.5
  70.9 1.9 %collective-permute-start.1 = (bf16[64,2560]{1,0:T(8,128)(2,1)S(1)}, bf16[64,2560]{1,0:T(8,128)(2,1)S(1)}, u32[]{:S(2)}, u32[]{:S(2)}) collective-permute-start(bf16[64,2560]{1,0:T(8,128)(2,1)S(1)} %get-tuple-element.45), channel_id=1, source_target_pairs={{0,384},{192,576},{384,0},{576,192},{1,385},{193,577},{385,1},{577... | collective-permute-start | bytes 983048 | tf_op jit(solution)/shard_map/ppermute | solution.py:620
  72.8 1.9 %collective-permute-start.2 = (bf16[64,2560]{1,0:T(8,128)(2,1)S(1)}, bf16[64,2560]{1,0:T(8,128)(2,1)S(1)}, u32[]{:S(2)}, u32[]{:S(2)}) collective-permute-start(bf16[64,2560]{1,0:T(8,128)(2,1)S(1)} %get-tuple-element.46), channel_id=1, source_target_pairs={{0,576},{192,384},{384,192},{576,0},{1,577},{193,385},{385,193},{5... | collective-permute-start | bytes 983048 | tf_op jit(solution)/shard_map/ppermute | solution.py:620
  74.7 4.5 %collective-permute-start.3 = (bf16[64,2560]{1,0:T(8,128)(2,1)S(1)}, bf16[64,2560]{1,0:T(8,128)(2,1)S(1)}, u32[]{:S(2)}, u32[]{:S(2)}) collective-permute-start(bf16[64,2560]{1,0:T(8,128)(2,1)S(1)} %get-tuple-element.47), channel_id=1, source_target_pairs={{0,192},{192,0},{384,576},{576,384},{1,193},{193,1},{385,577},{577... | collective-permute-start | bytes 983048 | tf_op jit(solution)/shard_map/ppermute | solution.py:620
  79.3 3.2 %all-to-all-done.2 = bf16[16,8,1024]{2,1,0:T(8,128)(2,1)S(1)} async-done(((bf16[16,8,1024]{2,1,0:T(8,128)(2,1)}), bf16[16,8,1024]{2,1,0:T(8,128)(2,1)S(1)}, u32[]{:S(2)}, u32[]{:S(2)}) %all-to-all-start.2) | async-done | bytes 262176 | tf_op jit(solution)/shard_map/all_to_all | solution.py:532
  82.5 0.9 collective-permute-done.1.refs_1_
  83.4 7.6 %collective-permute-done.2.refs_2_ = bf16[64,2560]{1,0:T(8,128)(2,1)S(1)} collective-permute-done((bf16[64,2560]{1,0:T(8,128)(2,1)S(1)}, bf16[64,2560]{1,0:T(8,128)(2,1)S(1)}, u32[]{:S(2)}, u32[]{:S(2)}) %collective-permute-start.2) | collective-permute-done | bytes 327712 | tf_op jit(solution)/shard_map/ppermute | solution.py:620
  91.0 0.0 collective-permute-done.3.refs_3_
  91.0 0.5 merge.1
  91.4 24.7 %all_to_all.32.in_ref = bf16[8,8,4608]{2,1,0:T(8,128)(2,1)S(1)} all-to-all(bf16[8,8,4608]{2,1,0:T(8,128)(2,1)S(1)} %merge.1), channel_id=1, replica_groups=mesh['x'=4,'z'=12,'y'=8,'c'=2] {'y'}, dimensions={0} | all-to-all | bytes 1179648 | tf_op jit(solution)/shard_map/all_to_all | solution.py:630
  116.1 0.1 fold.1
  116.2 18.5 %all_to_all.33.in_ref = bf16[12,8,256]{2,1,0:T(8,128)(2,1)S(1)} all-to-all(bf16[12,8,256]{2,1,0:T(8,128)(2,1)S(1)} %get-tuple-element.51), channel_id=1, replica_groups=mesh['x'=4,'z'=12,'y'=8,'c'=2] {'z'}, dimensions={0} | all-to-all | bytes 98304 | tf_op jit(solution)/shard_map/all_to_all | solution.py:648
  134.7 0.7 total.1
  135.4 6.2 %all-to-all-start.5 = ((bf16[48,8,256]{2,1,0:T(8,128)(2,1)}), bf16[48,8,256]{2,1,0:T(8,128)(2,1)S(1)}, u32[]{:S(2)}, u32[]{:S(2)}) async-start(bf16[48,8,256]{2,1,0:T(8,128)(2,1)} %total.1), calls=%async_computation.5 | async-start | bytes 393216 | tf_op jit(solution)/shard_map/all_to_all | solution.py:652
  141.6 4.9 %collective-permute-start.4 = (bf16[128,512]{1,0:T(8,128)(2,1)S(1)}, bf16[128,512]{1,0:T(8,128)(2,1)S(1)}, u32[]{:S(2)}, u32[]{:S(2)}) collective-permute-start(bf16[128,512]{1,0:T(8,128)(2,1)S(1)} %get-tuple-element.49), channel_id=1, source_target_pairs={{0,1},{1,0},{2,3},{3,2},{4,5},{5,4},{6,7},{7,6},{8,9},{9,8},{10,11... | collective-permute-start | bytes 393224 | tf_op jit(solution)/shard_map/ppermute | solution.py:644
  146.5 1.0 collective-permute-done.4.arrived_ref
  147.5 1.0 unpack.1
  148.5 6.0 %all-to-all-done.5 = bf16[48,8,256]{2,1,0:T(8,128)(2,1)S(1)} async-done(((bf16[48,8,256]{2,1,0:T(8,128)(2,1)}), bf16[48,8,256]{2,1,0:T(8,128)(2,1)S(1)}, u32[]{:S(2)}, u32[]{:S(2)}) %all-to-all-start.5) | async-done | bytes 196640 | tf_op jit(solution)/shard_map/all_to_all | solution.py:652
  154.5 0.7 result.1
Async XLA Ops:
  3.6 53.5 %copy-start = (bf16[512,2048]{1,0:T(8,128)(2,1)S(1)}, bf16[512,2048]{1,0:T(8,128)(2,1)}, u32[]{:S(2)}) copy-start(bf16[512,2048]{1,0:T(8,128)(2,1)} %weight_ref.3) | copy-start | bytes 6291460
  3.6 53.5 %copy-start.1 = (bf16[512,512]{1,0:T(8,128)(2,1)S(1)}, bf16[512,512]{1,0:T(8,128)(2,1)}, u32[]{:S(2)}) copy-start(bf16[512,512]{1,0:T(8,128)(2,1)} %out_weight_ref.1) | copy-start | bytes 1572868
  3.6 53.5 %copy-start.2 = (s32[1,256]{1,0:T(1,128)S(1)}, s32[1,256]{1,0:T(1,128)}, u32[]{:S(2)}) copy-start(s32[1,256]{1,0:T(1,128)} %seg_ref.1) | copy-start | bytes 3076
  3.6 53.5 %copy-start.3 = (s32[1,256]{1,0:T(1,128)S(1)}, s32[1,256]{1,0:T(1,128)}, u32[]{:S(2)}) copy-start(s32[1,256]{1,0:T(1,128)} %valid_ref.1) | copy-start | bytes 3076
  3.6 53.5 %copy-start.4 = (s32[1,8]{1,0:T(1,128)S(1)}, s32[1,8]{1,0:T(1,128)}, u32[]{:S(2)}) copy-start(s32[1,8]{1,0:T(1,128)} %sources_ref.1) | copy-start | bytes 100
  3.6 53.5 %copy-start.5 = (s32[1,8]{1,0:T(1,128)S(1)}, s32[1,8]{1,0:T(1,128)}, u32[]{:S(2)}) copy-start(s32[1,8]{1,0:T(1,128)} %offsets_ref.1) | copy-start | bytes 100
  63.0 7.6 %collective-permute-start = (bf16[256,2560]{1,0:T(8,128)(2,1)}, bf16[256,2560]{1,0:T(8,128)(2,1)S(1)}, u32[]{:S(2)}, u32[]{:S(2)}) collective-permute-start(bf16[256,2560]{1,0:T(8,128)(2,1)} %get-tuple-element.39), channel_id=1, source_target_pairs={{0,1},{1,0},{2,3},{3,2},{4,5},{5,4},{6,7},{7,6},{8,9},{9,8},{10,11... | collective-permute-start | bytes 3932168 | tf_op jit(solution)/shard_map/ppermute | solution.py:615
  66.8 15.7 %all-to-all-start.2 = ((bf16[16,8,1024]{2,1,0:T(8,128)(2,1)}), bf16[16,8,1024]{2,1,0:T(8,128)(2,1)S(1)}, u32[]{:S(2)}, u32[]{:S(2)}) async-start(bf16[16,8,1024]{2,1,0:T(8,128)(2,1)} %bitcast.6), calls=%async_computation.2 | async-start | bytes 524288 | tf_op jit(solution)/shard_map/all_to_all | solution.py:532
  70.9 12.5 %collective-permute-start.1 = (bf16[64,2560]{1,0:T(8,128)(2,1)S(1)}, bf16[64,2560]{1,0:T(8,128)(2,1)S(1)}, u32[]{:S(2)}, u32[]{:S(2)}) collective-permute-start(bf16[64,2560]{1,0:T(8,128)(2,1)S(1)} %get-tuple-element.45), channel_id=1, source_target_pairs={{0,384},{192,576},{384,0},{576,192},{1,385},{193,577},{385,1},{577... | collective-permute-start | bytes 983048 | tf_op jit(solution)/shard_map/ppermute | solution.py:620
  72.8 18.2 %collective-permute-start.2 = (bf16[64,2560]{1,0:T(8,128)(2,1)S(1)}, bf16[64,2560]{1,0:T(8,128)(2,1)S(1)}, u32[]{:S(2)}, u32[]{:S(2)}) collective-permute-start(bf16[64,2560]{1,0:T(8,128)(2,1)S(1)} %get-tuple-element.46), channel_id=1, source_target_pairs={{0,576},{192,384},{384,192},{576,0},{1,577},{193,385},{385,193},{5... | collective-permute-start | bytes 983048 | tf_op jit(solution)/shard_map/ppermute | solution.py:620
  74.7 16.2 %collective-permute-start.3 = (bf16[64,2560]{1,0:T(8,128)(2,1)S(1)}, bf16[64,2560]{1,0:T(8,128)(2,1)S(1)}, u32[]{:S(2)}, u32[]{:S(2)}) collective-permute-start(bf16[64,2560]{1,0:T(8,128)(2,1)S(1)} %get-tuple-element.47), channel_id=1, source_target_pairs={{0,192},{192,0},{384,576},{576,384},{1,193},{193,1},{385,577},{577... | collective-permute-start | bytes 983048 | tf_op jit(solution)/shard_map/ppermute | solution.py:620
  135.4 19.1 %all-to-all-start.5 = ((bf16[48,8,256]{2,1,0:T(8,128)(2,1)}), bf16[48,8,256]{2,1,0:T(8,128)(2,1)S(1)}, u32[]{:S(2)}, u32[]{:S(2)}) async-start(bf16[48,8,256]{2,1,0:T(8,128)(2,1)} %total.1), calls=%async_computation.5 | async-start | bytes 393216 | tf_op jit(solution)/shard_map/all_to_all | solution.py:652
  141.6 5.9 %collective-permute-start.4 = (bf16[128,512]{1,0:T(8,128)(2,1)S(1)}, bf16[128,512]{1,0:T(8,128)(2,1)S(1)}, u32[]{:S(2)}, u32[]{:S(2)}) collective-permute-start(bf16[128,512]{1,0:T(8,128)(2,1)S(1)} %get-tuple-element.49), channel_id=1, source_target_pairs={{0,1},{1,0},{2,3},{3,2},{4,5},{5,4},{6,7},{7,6},{8,9},{9,8},{10,11... | collective-permute-start | bytes 393224 | tf_op jit(solution)/shard_map/ppermute | solution.py:644

commit v9 on v8

--- a/solution.py
+++ b/solution.py
@@ -475,13 +475,13 @@
 
 def result_kernel(in_ref, after_ref, joined_ref, output_ref):
     del after_ref
-    xs, zs, piece_rows, piece = in_ref.shape
+    _, xs, piece_rows, piece = in_ref.shape
     split = joined_ref.shape[1]
     step = math.gcd(piece, split)
     for x in range(xs):
         span = slice(x * piece_rows, (x + 1) * piece_rows)
         for at in range(0, split + output_ref.shape[1], step):
-            block = in_ref[x, at // piece, :, at % piece : at % piece + step].astype(f32)
+            block = in_ref[at // piece, x, :, at % piece : at % piece + step].astype(f32)
             if at < split:
                 joined_ref[span, at : at + step] = block
             else:
@@ -649,12 +649,12 @@
     (spread,) = call(
         functools.partial(total_kernel, scaling), "total", [shape((xs * zs, own, piece), bf16)], (pieces,)
     )
-    spread = lax.all_to_all(spread, ("x", "z"), 0, 0, tiled=True)
+    spread = lax.all_to_all(spread, ("z", "x"), 0, 0, tiled=True)
     joined_grad, output_grad = call(
         result_kernel,
         "result",
         [shape((width // lanes, 4 * width), f32), shape((width // lanes, width), f32)],
-        (spread.reshape(xs, zs, own, piece), token),
+        (spread.reshape(zs, xs, own, piece), token),
     )
     return (row_grad, joined_grad, output_grad)
 

time: 158 us -> 157 us (level)
  no operation moved by 1% of the time
where the time goes in v9:
time: 157 us; the launch traced here: 155 us
  blocking collectives  95.9 us (61%)
  starting transfers between devices  25.2 us (16%)
  waiting for transfers between devices  18.6 us (12%)
  Pallas kernels  14.6 us (9%)
    all_to_all x2, blocking collectives, exchange(): lax.all_to_all(chunks, ('y', 'c'), 0, 0, tiled=True).reshape(block.shape)  52.8 us
    all_to_all x1, blocking collectives, on_device(): merged = lax.all_to_all(merged, 'y', 0, 0, tiled=True)  24.7 us
    all_to_all x1, blocking collectives, on_device(): pieces = lax.all_to_all(pieces, 'z', 0, 0, tiled=True)  18.5 us
    pallas_call x10, Pallas kernels, call(): pl.pallas_call(kernel, out_shape=tuple(out_shape), in_specs=[smem] * scal...  14.6 us
    ppermute x3, waiting for transfers between devices, on_device(): lax.ppermute(parts[k], 'x', [(i, i ^ k) for i in range(xs)])  8.46 us
    ppermute x3, starting transfers between devices, on_device(): lax.ppermute(parts[k], 'x', [(i, i ^ k) for i in range(xs)])  8.37 us
    all_to_all x1, starting transfers between devices, on_device(): spread = lax.all_to_all(spread, ('z', 'x'), 0, 0, tiled=True)  6.2 us
    all_to_all x1, waiting for transfers between devices, on_device(): spread = lax.all_to_all(spread, ('z', 'x'), 0, 0, tiled=True)  5.92 us
  transfers between devices with their start and end apart: 7, of which 5 were waited for; matrix products, arithmetic and copies ran while one was open for 0% of the time, Pallas kernels for 2%

profile of v9, /device:TPU:1, one launch (start us, length us, event | category | flops | bytes accessed | tf_op | source)
XLA Modules:
  0.0 155.2 jit_solution(7233560718438262742)
XLA Ops:
  0.6 2.9 %pack.1 = bf16[128,2176]{1,0:T(8,128)(2,1)} custom-call(s32[1,8]{1,0:T(1,128)} %dest_ref.1, s32[1]{0:T(128)} %bitcast.me_ref, s32[1]{0:T(128)} %bitcast.1.own_x_ref, bf16[256,512]{1,0:T(8,128)(2,1)} %rows_hbm.1, bf16[256,512]{1,0:T(8,128)(2,1)} %cot_hbm.1), custom_call_target="tpu_custom_call" | custom-call | flops 67108864 | bytes 1081384 | tf_op jit(solution)/shard_map/pack/pallas_call | solution.py:497
  3.6 0.0 copy-start
  3.6 0.0 copy-start.1
  3.6 0.0 copy-start.2
  3.6 0.0 copy-start.3
  3.6 0.0 copy-start.4
  3.6 0.0 copy-start.5
  3.6 32.6 %all_to_all.30 = bf16[16,8,2176]{2,1,0:T(8,128)(2,1)S(1)} all-to-all(bf16[16,8,2176]{2,1,0:T(8,128)(2,1)} %bitcast.14), channel_id=1, replica_groups=mesh['x'=4,'z'=12,'y'=8,'c'=2] {'y','c'}, dimensions={0} | all-to-all | bytes 1114112 | tf_op jit(solution)/shard_map/all_to_all | solution.py:532
  36.2 0.6 route.1
  36.9 20.2 %all_to_all.31 = bf16[16,8,2048]{2,1,0:T(8,128)(2,1)S(1)} all-to-all(bf16[16,8,2048]{2,1,0:T(8,128)(2,1)S(1)} %bitcast.13), channel_id=1, replica_groups=mesh['x'=4,'z'=12,'y'=8,'c'=2] {'y','c'}, dimensions={0} | all-to-all | bytes 1048576 | tf_op jit(solution)/shard_map/all_to_all | solution.py:532
  57.0 0.0 copy-done
  57.0 0.0 copy-done.1
  57.0 0.0 copy-done.2
  57.1 0.0 copy-done.3
  57.1 0.0 copy-done.4
  57.1 0.0 copy-done.5
  57.1 5.9 %layer.1 = (bf16[256,2560]{1,0:T(8,128)(2,1)}, bf16[256,2048]{1,0:T(8,128)(2,1)S(1)}, bf16[256,256]{1,0:T(8,128)(2,1)S(1)}, bf16[256,256]{1,0:T(8,128)(2,1)S(1)}...) custom-call(s32[1]{0:T(128)} %bitcast.me_ref, ...), custom_call_target="tpu_custom_call" | custom-call | flops 1342177280 | bytes 6327368 | tf_op jit(solution)/shard_map/layer/pallas_call | solution.py:497
  63.0 1.9 %collective-permute-start = (bf16[256,2560]{1,0:T(8,128)(2,1)}, bf16[256,2560]{1,0:T(8,128)(2,1)S(1)}, u32[]{:S(2)}, u32[]{:S(2)}) collective-permute-start(bf16[256,2560]{1,0:T(8,128)(2,1)} %get-tuple-element.39), channel_id=1, source_target_pairs={{0,1},{1,0},{2,3},{3,2},{4,5},{5,4},{6,7},{7,6},{8,9},{9,8},{10,11... | collective-permute-start | bytes 3932168 | tf_op jit(solution)/shard_map/ppermute | solution.py:615
  65.0 1.8 %finish.1 = (bf16[128,1024]{1,0:T(8,128)(2,1)}, bf16[64,2560]{1,0:T(8,128)(2,1)S(1)}, bf16[64,2560]{1,0:T(8,128)(2,1)S(1)}, bf16[64,2560]{1,0:T(8,128)(2,1)S(1)}, bf16[64,2560]{1,0:T(8,128)(2,1)S(1)}) custom-call(bf16[512,2048]{1,0:T(8,128)(2,1)S(1)} %copy-done, bf16[256,2048]{1,0:T(8,128)(2,1)S(1)} %get-tuple-element.31.proj_cot_ref, ...), custom_call_target="tpu_custom_call" | custom-call | flops 1073741824 | bytes 5538816 | tf_op jit(solution)/shard_map/finish/pallas_call | solution.py:497
  66.8 3.8 %all-to-all-start.2 = ((bf16[16,8,1024]{2,1,0:T(8,128)(2,1)}), bf16[16,8,1024]{2,1,0:T(8,128)(2,1)S(1)}, u32[]{:S(2)}, u32[]{:S(2)}) async-start(bf16[16,8,1024]{2,1,0:T(8,128)(2,1)} %bitcast.6), calls=%async_computation.2 | async-start | bytes 524288 | tf_op jit(solution)/shard_map/all_to_all | solution.py:532
  70.6 0.0 collective-permute-done.arrived_ref
  70.6 0.2 add.5
  70.9 1.9 %collective-permute-start.1 = (bf16[64,2560]{1,0:T(8,128)(2,1)S(1)}, bf16[64,2560]{1,0:T(8,128)(2,1)S(1)}, u32[]{:S(2)}, u32[]{:S(2)}) collective-permute-start(bf16[64,2560]{1,0:T(8,128)(2,1)S(1)} %get-tuple-element.45), channel_id=1, source_target_pairs={{0,384},{192,576},{384,0},{576,192},{1,385},{193,577},{385,1},{577... | collective-permute-start | bytes 983048 | tf_op jit(solution)/shard_map/ppermute | solution.py:620
  72.8 1.9 %collective-permute-start.2 = (bf16[64,2560]{1,0:T(8,128)(2,1)S(1)}, bf16[64,2560]{1,0:T(8,128)(2,1)S(1)}, u32[]{:S(2)}, u32[]{:S(2)}) collective-permute-start(bf16[64,2560]{1,0:T(8,128)(2,1)S(1)} %get-tuple-element.46), channel_id=1, source_target_pairs={{0,576},{192,384},{384,192},{576,0},{1,577},{193,385},{385,193},{5... | collective-permute-start | bytes 983048 | tf_op jit(solution)/shard_map/ppermute | solution.py:620
  74.7 4.5 %collective-permute-start.3 = (bf16[64,2560]{1,0:T(8,128)(2,1)S(1)}, bf16[64,2560]{1,0:T(8,128)(2,1)S(1)}, u32[]{:S(2)}, u32[]{:S(2)}) collective-permute-start(bf16[64,2560]{1,0:T(8,128)(2,1)S(1)} %get-tuple-element.47), channel_id=1, source_target_pairs={{0,192},{192,0},{384,576},{576,384},{1,193},{193,1},{385,577},{577... | collective-permute-start | bytes 983048 | tf_op jit(solution)/shard_map/ppermute | solution.py:620
  79.3 3.2 %all-to-all-done.2 = bf16[16,8,1024]{2,1,0:T(8,128)(2,1)S(1)} async-done(((bf16[16,8,1024]{2,1,0:T(8,128)(2,1)}), bf16[16,8,1024]{2,1,0:T(8,128)(2,1)S(1)}, u32[]{:S(2)}, u32[]{:S(2)}) %all-to-all-start.2) | async-done | bytes 262176 | tf_op jit(solution)/shard_map/all_to_all | solution.py:532
  82.5 0.9 collective-permute-done.1.refs_1_
  83.4 7.6 %collective-permute-done.2.refs_2_ = bf16[64,2560]{1,0:T(8,128)(2,1)S(1)} collective-permute-done((bf16[64,2560]{1,0:T(8,128)(2,1)S(1)}, bf16[64,2560]{1,0:T(8,128)(2,1)S(1)}, u32[]{:S(2)}, u32[]{:S(2)}) %collective-permute-start.2) | collective-permute-done | bytes 327712 | tf_op jit(solution)/shard_map/ppermute | solution.py:620
  91.0 0.0 collective-permute-done.3.refs_3_
  91.0 0.5 merge.1
  91.4 24.7 %all_to_all.32.in_ref = bf16[8,8,4608]{2,1,0:T(8,128)(2,1)S(1)} all-to-all(bf16[8,8,4608]{2,1,0:T(8,128)(2,1)S(1)} %merge.1), channel_id=1, replica_groups=mesh['x'=4,'z'=12,'y'=8,'c'=2] {'y'}, dimensions={0} | all-to-all | bytes 1179648 | tf_op jit(solution)/shard_map/all_to_all | solution.py:630
  116.1 0.1 fold.1
  116.2 18.5 %all_to_all.33.in_ref = bf16[12,8,256]{2,1,0:T(8,128)(2,1)S(1)} all-to-all(bf16[12,8,256]{2,1,0:T(8,128)(2,1)S(1)} %get-tuple-element.51), channel_id=1, replica_groups=mesh['x'=4,'z'=12,'y'=8,'c'=2] {'z'}, dimensions={0} | all-to-all | bytes 98304 | tf_op jit(solution)/shard_map/all_to_all | solution.py:648
  134.7 0.7 total.1
  135.4 6.2 %all-to-all-start.5 = ((bf16[48,8,256]{2,1,0:T(8,128)(2,1)}), bf16[48,8,256]{2,1,0:T(8,128)(2,1)S(1)}, u32[]{:S(2)}, u32[]{:S(2)}) async-start(bf16[48,8,256]{2,1,0:T(8,128)(2,1)} %total.1), calls=%async_computation.5 | async-start | bytes 393216 | tf_op jit(solution)/shard_map/all_to_all | solution.py:652
  141.6 4.9 %collective-permute-start.4 = (bf16[128,512]{1,0:T(8,128)(2,1)S(1)}, bf16[128,512]{1,0:T(8,128)(2,1)S(1)}, u32[]{:S(2)}, u32[]{:S(2)}) collective-permute-start(bf16[128,512]{1,0:T(8,128)(2,1)S(1)} %get-tuple-element.49), channel_id=1, source_target_pairs={{0,1},{1,0},{2,3},{3,2},{4,5},{5,4},{6,7},{7,6},{8,9},{9,8},{10,11... | collective-permute-start | bytes 393224 | tf_op jit(solution)/shard_map/ppermute | solution.py:644
  146.5 1.0 collective-permute-done.4.arrived_ref
  147.5 1.0 unpack.1
  148.5 5.9 %all-to-all-done.5 = bf16[48,8,256]{2,1,0:T(8,128)(2,1)S(1)} async-done(((bf16[48,8,256]{2,1,0:T(8,128)(2,1)}), bf16[48,8,256]{2,1,0:T(8,128)(2,1)S(1)}, u32[]{:S(2)}, u32[]{:S(2)}) %all-to-all-start.5) | async-done | bytes 196640 | tf_op jit(solution)/shard_map/all_to_all | solution.py:652
  154.4 0.7 result.1
Async XLA Ops:
  3.6 53.5 %copy-start = (bf16[512,2048]{1,0:T(8,128)(2,1)S(1)}, bf16[512,2048]{1,0:T(8,128)(2,1)}, u32[]{:S(2)}) copy-start(bf16[512,2048]{1,0:T(8,128)(2,1)} %weight_ref.3) | copy-start | bytes 6291460
  3.6 53.5 %copy-start.1 = (bf16[512,512]{1,0:T(8,128)(2,1)S(1)}, bf16[512,512]{1,0:T(8,128)(2,1)}, u32[]{:S(2)}) copy-start(bf16[512,512]{1,0:T(8,128)(2,1)} %out_weight_ref.1) | copy-start | bytes 1572868
  3.6 53.5 %copy-start.2 = (s32[1,256]{1,0:T(1,128)S(1)}, s32[1,256]{1,0:T(1,128)}, u32[]{:S(2)}) copy-start(s32[1,256]{1,0:T(1,128)} %seg_ref.1) | copy-start | bytes 3076
  3.6 53.5 %copy-start.3 = (s32[1,256]{1,0:T(1,128)S(1)}, s32[1,256]{1,0:T(1,128)}, u32[]{:S(2)}) copy-start(s32[1,256]{1,0:T(1,128)} %valid_ref.1) | copy-start | bytes 3076
  3.6 53.5 %copy-start.4 = (s32[1,8]{1,0:T(1,128)S(1)}, s32[1,8]{1,0:T(1,128)}, u32[]{:S(2)}) copy-start(s32[1,8]{1,0:T(1,128)} %sources_ref.1) | copy-start | bytes 100
  3.6 53.5 %copy-start.5 = (s32[1,8]{1,0:T(1,128)S(1)}, s32[1,8]{1,0:T(1,128)}, u32[]{:S(2)}) copy-start(s32[1,8]{1,0:T(1,128)} %offsets_ref.1) | copy-start | bytes 100
  63.0 7.6 %collective-permute-start = (bf16[256,2560]{1,0:T(8,128)(2,1)}, bf16[256,2560]{1,0:T(8,128)(2,1)S(1)}, u32[]{:S(2)}, u32[]{:S(2)}) collective-permute-start(bf16[256,2560]{1,0:T(8,128)(2,1)} %get-tuple-element.39), channel_id=1, source_target_pairs={{0,1},{1,0},{2,3},{3,2},{4,5},{5,4},{6,7},{7,6},{8,9},{9,8},{10,11... | collective-permute-start | bytes 3932168 | tf_op jit(solution)/shard_map/ppermute | solution.py:615
  66.8 15.7 %all-to-all-start.2 = ((bf16[16,8,1024]{2,1,0:T(8,128)(2,1)}), bf16[16,8,1024]{2,1,0:T(8,128)(2,1)S(1)}, u32[]{:S(2)}, u32[]{:S(2)}) async-start(bf16[16,8,1024]{2,1,0:T(8,128)(2,1)} %bitcast.6), calls=%async_computation.2 | async-start | bytes 524288 | tf_op jit(solution)/shard_map/all_to_all | solution.py:532
  70.9 12.5 %collective-permute-start.1 = (bf16[64,2560]{1,0:T(8,128)(2,1)S(1)}, bf16[64,2560]{1,0:T(8,128)(2,1)S(1)}, u32[]{:S(2)}, u32[]{:S(2)}) collective-permute-start(bf16[64,2560]{1,0:T(8,128)(2,1)S(1)} %get-tuple-element.45), channel_id=1, source_target_pairs={{0,384},{192,576},{384,0},{576,192},{1,385},{193,577},{385,1},{577... | collective-permute-start | bytes 983048 | tf_op jit(solution)/shard_map/ppermute | solution.py:620
  72.8 18.2 %collective-permute-start.2 = (bf16[64,2560]{1,0:T(8,128)(2,1)S(1)}, bf16[64,2560]{1,0:T(8,128)(2,1)S(1)}, u32[]{:S(2)}, u32[]{:S(2)}) collective-permute-start(bf16[64,2560]{1,0:T(8,128)(2,1)S(1)} %get-tuple-element.46), channel_id=1, source_target_pairs={{0,576},{192,384},{384,192},{576,0},{1,577},{193,385},{385,193},{5... | collective-permute-start | bytes 983048 | tf_op jit(solution)/shard_map/ppermute | solution.py:620
  74.7 16.2 %collective-permute-start.3 = (bf16[64,2560]{1,0:T(8,128)(2,1)S(1)}, bf16[64,2560]{1,0:T(8,128)(2,1)S(1)}, u32[]{:S(2)}, u32[]{:S(2)}) collective-permute-start(bf16[64,2560]{1,0:T(8,128)(2,1)S(1)} %get-tuple-element.47), channel_id=1, source_target_pairs={{0,192},{192,0},{384,576},{576,384},{1,193},{193,1},{385,577},{577... | collective-permute-start | bytes 983048 | tf_op jit(solution)/shard_map/ppermute | solution.py:620
  135.4 19.0 %all-to-all-start.5 = ((bf16[48,8,256]{2,1,0:T(8,128)(2,1)}), bf16[48,8,256]{2,1,0:T(8,128)(2,1)S(1)}, u32[]{:S(2)}, u32[]{:S(2)}) async-start(bf16[48,8,256]{2,1,0:T(8,128)(2,1)} %total.1), calls=%async_computation.5 | async-start | bytes 393216 | tf_op jit(solution)/shard_map/all_to_all | solution.py:652
  141.6 5.9 %collective-permute-start.4 = (bf16[128,512]{1,0:T(8,128)(2,1)S(1)}, bf16[128,512]{1,0:T(8,128)(2,1)S(1)}, u32[]{:S(2)}, u32[]{:S(2)}) collective-permute-start(bf16[128,512]{1,0:T(8,128)(2,1)S(1)} %get-tuple-element.49), channel_id=1, source_target_pairs={{0,1},{1,0},{2,3},{3,2},{4,5},{5,4},{6,7},{7,6},{8,9},{9,8},{10,11... | collective-permute-start | bytes 393224 | tf_op jit(solution)/shard_map/ppermute | solution.py:644
